TPU v7x, 32 devices: a whole 2x2x4 slice. The times are simulated.
32 devices in a mesh: fsdp: 4 (over x, core), tensor: 8 (over z, y).
Axes of the slice: x: 2, y: 2, z: 4, core: 2. Of those that a mesh axis runs over, the one named last changes fastest.
Arguments:
- weight: bfloat16 [896, 2048], P('tensor', 'fsdp'), may hold values from -0.0017929077 to 0.0017929077
- momentum: float32 [896, 2048], P('tensor', 'fsdp'), may hold values from -18 to 18
- grad: bfloat16 [896, 2048], P('tensor', 'fsdp'), may hold values from -6 to 6
- q_prev: float32 [896, 256], P('tensor'), may hold values from -0.1875 to 0.1875
Outputs:
- new_weight: bfloat16 [896, 2048], P('tensor', 'fsdp')
- new_momentum: float32 [896, 2048], P('tensor', 'fsdp')
- q_new: float32 [896, 256], P('tensor')
All inputs are finite; a program needn't handle non-finite values.
Results may differ from a plain program's by a relative error of at most 0.001.
Values sent between devices are 32-bit elements; how exact they have to be, the bound alone decides.
No kernel may reach another device: no remote copies, remote signals or barrier semaphores. Data moves between devices by JAX's collectives and lax.ppermute only.
A program may use at most 64 MiB of HBM per device.

v0:
```python
import math

import jax
import jax.numpy as jnp
from jax import lax
from jax.sharding import PartitionSpec as P

momentum_decay = 0.95
step_rate = 0.02
norm_eps = 1e-06


def contract_first(left, right):
    return lax.dot_general(
        left,
        right,
        (((0,), (0,)), ((), ())),
        precision=lax.Precision.HIGHEST,
        preferred_element_type=jnp.float32,
    )


def right_solve(lower, values):
    return jax.scipy.linalg.solve_triangular(lower, values.T, lower=True).T


def per_device(weight, momentum, grad, q_prev):
    highest = lax.Precision.HIGHEST
    buffer = momentum + grad.astype(jnp.float32)
    cols_here = buffer.shape[0]
    rows_here = buffer.shape[1]
    factor = step_rate * math.sqrt(
        cols_here * lax.axis_size("tensor") / (rows_here * lax.axis_size("fsdp"))
    )
    pieces = lax.psum_scatter(
        contract_first(buffer, q_prev), "tensor", scatter_dimension=0, tiled=True
    )
    raw = lax.all_gather(pieces, "tensor", axis=0, tiled=True)
    local_gram = contract_first(raw, raw)
    local_cross = jnp.dot(buffer, raw, precision=highest, preferred_element_type=jnp.float32)
    gram, cross = lax.psum((local_gram, local_cross), "fsdp")
    lower = jnp.linalg.cholesky(gram)
    ortho = right_solve(lower, raw)
    right = right_solve(lower, cross)
    column_sq = lax.psum(jnp.sum(right * right, axis=0), "tensor")
    q_new = right / (jnp.sqrt(column_sq) + norm_eps)
    new_momentum = buffer - (1.0 - momentum_decay) * lax.dot_general(
        right,
        ortho,
        (((1,), (1,)), ((), ())),
        precision=highest,
        preferred_element_type=jnp.float32,
    )
    update = lax.dot_general(
        q_new,
        ortho,
        (((1,), (1,)), ((), ())),
        precision=highest,
        preferred_element_type=jnp.float32,
    )
    new_weight = (weight.astype(jnp.float32) - factor * update).astype(jnp.bfloat16)
    return (new_weight, new_momentum, q_new)


def solution(mesh):
    placed = (P("tensor", "fsdp"), P("tensor", "fsdp"), P("tensor", "fsdp"), P("tensor", None))
    return jax.shard_map(
        per_device,
        mesh=mesh,
        in_specs=placed,
        out_specs=(P("tensor", "fsdp"), P("tensor", "fsdp"), P("tensor", None)),
        check_vma=False,
    )
```

profile of v0, /device:TPU:0, one launch (start us, length us, event | category | flops | bytes accessed | tf_op | source)
XLA Modules:
  0.0 237.3 jit_solution(13918556376953336574)
XLA Ops:
  7.2 0.8 copy-done
  8.1 2.4 %fusion.7 = f32[512,256]{1,0:T(8,128)} fusion(f32[112,256]{1,0:T(8,128)S(1)} %copy-done, f32[112,512]{1,0:T(8,128)} %param.5, bf16[112,512]{1,0:T(8,128)(2,1)} %param.6), kind=kOutput, calls=%fused_computation.21 | convolution fusion | flops 176275456 | bytes 983040 | tf_op jit(solution)/shard_map/dot_general | solution.py:14
  10.6 65.9 %reduce-scatter.2.cloned.1.call-done = f32[64,256]{1,0:T(8,128)} async-done(((f32[512,256]{1,0:T(8,128)}), f32[64,256]{1,0:T(8,128)}) %reduce-scatter.2.cloned.1.call-update) | async-done | bytes 65552 | tf_op jit(solution)/shard_map/reduce_scatter | solution.py:35
  76.4 31.6 %all_gather.3 = f32[512,256]{1,0:T(8,128)S(1)} all-gather(f32[64,256]{1,0:T(8,128)} %reduce-scatter.2.cloned.1.call-done), channel_id=1, replica_groups=mesh['fsdp'=4,'tensor'=8] {'tensor'}, dimensions={0}, use_global_device_ids=true | all-gather | bytes 589824 | tf_op jit(solution)/shard_map/all_gather | solution.py:38
  108.1 1.7 fusion.23
  109.8 1.1 fusion.6
  110.9 31.5 %all-reduce.4.cloned.1.call-done = (f32[256,256]{0,1:T(8,128)}, f32[256,112]{0,1:T(8,128)}) async-done(((f32[256,256]{0,1:T(8,128)}, f32[256,112]{0,1:T(8,128)}), (f32[256,256]{0,1:T(8,128)}, f32[256,112]{0,1:T(8,128)})) %all-reduce.4.cloned.1.call-update) | async-done | bytes 376848 | tf_op jit(solution)/shard_map/psum | solution.py:41
  142.4 1.1 copy.8
  143.7 11.7 %cholesky.50 = f32[128,128]{1,0:T(8,128)S(1)} custom-call(f32[128,128]{1,0:T(8,128)S(1)} %cholesky.118), custom_call_target="Cholesky" | custom-call | tf_op jit(solution)/shard_map/jit(cholesky)/cholesky | solution.py:42
  155.4 9.8 %custom-call.18 = f32[1,128,128]{1,2,0:T(8,128)S(1)} custom-call(f32[1,128,128]{2,1,0:T(8,128)S(1)} %get-tuple-element.26), custom_call_target="InvertDiagBlocksLowerTriangular" | custom-call | tf_op jit(solution)/shard_map/jit(cholesky)/cholesky | solution.py:42
  165.7 11.7 %cholesky.105 = f32[128,128]{1,0:T(8,128)S(1)} custom-call(f32[128,128]{1,0:T(8,128)S(1)} %convolution_subtract_fusion.1), custom_call_target="Cholesky" | custom-call | tf_op jit(solution)/shard_map/jit(cholesky)/cholesky | solution.py:42
  177.5 0.6 compare_reduce_fusion
  179.5 4.1 %while.1 = (s32[]{:T(128)}, f32[256,256]{1,0:T(8,128)S(1)}, s32[2,2]{1,0:T(2,128)S(1)}, f32[2,128,128]{2,1,0:T(8,128)S(1)}, s32[]{:T(128)}) while((s32[]{:T(128)}, f32[256,256]{1,0:T(8,128)S(1)}, s32[2,2]{1,0:T(2,128)S(1)}, f32[2,128,128]{2,1,0:T(8,128)S(1)}, s32[]{:T(128)}) %tuple.27), condition=%wide.while_cond, body=%wide.while_body.sunk | while | flops 2 | bytes 131189 | solution.py:24
  179.7 0.6 fusion.35
  180.3 1.4 bitcast_dynamic-update-slice_fusion.2
  181.7 0.6 fusion.35
  182.3 1.4 bitcast_dynamic-update-slice_fusion.2
  183.7 19.7 %custom-call.19 = f32[2,128,128]{1,2,0:T(8,128)S(1)} custom-call(f32[2,128,128]{2,1,0:T(8,128)S(1)} %get-tuple-element.10), custom_call_target="InvertDiagBlocksLowerTriangular" | custom-call | tf_op jit(solution)/shard_map/jit(_solve_triangular)/triangular_solve | solution.py:24
  203.8 0.6 convolution_subtract_fusion
  204.8 0.5 copy-done.4
  206.0 21.4 %psum.23 = f32[256]{0:T(256)S(1)} all-reduce(f32[256]{0:T(256)S(1)} %multiply_reduce_fusion), channel_id=1, replica_groups=mesh['fsdp'=4,'tensor'=8] {'tensor'}, use_global_device_ids=true, to_apply=%region_8.9 | all-reduce | flops 256 | bytes 2048 | tf_op jit(solution)/shard_map/psum | solution.py:45
  227.4 1.1 fusion
  228.5 0.7 fusion.18
  229.4 1.1 fusion.2
  (34 shorter events, 2.7 us)
Async XLA Ops:
  7.2 0.9 copy-start
  7.2 69.2 %reduce-scatter.2.cloned.1.call-start = ((), (), s32[]{:S(2)}) async-start(), calls=%async_computation.1 | async-start | bytes 589824 | tf_op jit(solution)/shard_map/reduce_scatter | solution.py:35
  10.5 131.9 %all-reduce.4.cloned.1.call-start = ((), (), s32[]{:S(2)}) async-start(), calls=%async_computation.2 | async-start | bytes 753664 | tf_op jit(solution)/shard_map/psum | solution.py:41
  108.1 1.7 copy-start.1
  108.1 1.7 copy-start.3
  142.4 1.2 copy-start.2
  204.4 0.9 copy-start.4
  228.5 0.9 copy-start.5
Sparse Core Ops, SparseCore 0:
  11.4 65.0 reduce-scatter.1
  111.0 31.4 all-reduce.3
where the time goes:
time: 238 us; the launch traced here: 237 us
  waiting for transfers between devices  97.4 us (41%)
  other arithmetic  54.4 us (23%)
  blocking collectives  53 us (22%)
  between operations  15.5 us (7%)
  matrix products  9.93 us (4%)
  local copies, waits for them, and re-layouts  6.81 us (3%)
    reduce_scatter x1, waiting for transfers between devices, per_device(): lax.psum_scatter(contract_first(buffer, q_prev), 'tensor', scatter_dimens...  65.9 us
    another operation x6, other arithmetic, per_device(): lower = jnp.linalg.cholesky(gram)  33.9 us
    all_gather x1, blocking collectives, per_device(): raw = lax.all_gather(pieces, 'tensor', axis=0, tiled=True)  31.6 us
    psum x1, waiting for transfers between devices, per_device(): gram, cross = lax.psum((local_gram, local_cross), 'fsdp')  31.5 us
    psum x1, blocking collectives, per_device(): column_sq = lax.psum(jnp.sum(right * right, axis=0), 'tensor')  21.4 us
    another operation x3, other arithmetic, right_solve(): return jax.scipy.linalg.solve_triangular(lower, values.T, lower=True).T  19.7 us
  transfers between devices with their start and end apart: 2, of which 2 were waited for; matrix products, arithmetic and copies ran while one was open for 0% of the time, Pallas kernels for 0%

commit v1 on v0

v1 whole, which is shorter than its diff:
```python
import functools
import math

import jax
import jax.numpy as jnp
from jax import lax
from jax.experimental import pallas as pl
from jax.experimental.pallas import tpu as pltpu
from jax.sharding import PartitionSpec as P

momentum_decay = 0.95
step_rate = 0.02
norm_eps = 1e-06
f32 = jnp.float32
bf16 = jnp.bfloat16
block_rows = 16
vmem_bytes = 32 * 1024 * 1024
TT = (((0,), (0,)), ((), ()))
NN = (((1,), (0,)), ((), ()))
NT = (((1,), (1,)), ((), ()))


def split3(x):
    high = x.astype(bf16)
    rest = x - high.astype(f32)
    mid = rest.astype(bf16)
    return high, mid, (rest - mid.astype(f32)).astype(bf16)


def dot6(a, b, dims):
    ah, am, al = split3(a)
    bh, bm, bl = split3(b)

    def one(x, y):
        return lax.dot_general(x, y, dims, preferred_element_type=f32)

    small = one(am, bm) + one(ah, bl) + one(al, bh)
    return one(ah, bh) + (one(ah, bm) + one(am, bh) + small)


def bits_of(size):
    return size.bit_length() - 1


def orders(tensor):
    straight = list(range(bits_of(tensor)))
    other = straight[:]
    if len(straight) > 2:
        other[0], other[1] = other[1], other[0]
    return straight, other


def block_id(tensor):
    mine, core = lax.axis_index("tensor"), lax.axis_index("fsdp") % 2
    kept = bits_of(tensor) - 1
    ids = []
    for order in orders(tensor):
        value = 0
        for step in range(kept):
            bit = (mine // 2 ** order[step]) % 2
            value = value + bit * 2 ** (kept - 1 - step)
        ids.append(value)
    return jnp.where(core == 0, ids[0], ids[1])


def flip_tensor(x, step, fsdp, tensor):
    pairs = []
    for f in range(fsdp):
        bit = orders(tensor)[f % 2][step]
        for t in range(tensor):
            pairs.append((f * tensor + t, f * tensor + (t ^ (1 << bit))))
    return lax.ppermute(x, ("fsdp", "tensor"), pairs)


def flip_fsdp(x, bit, fsdp):
    return lax.ppermute(x, "fsdp", [(f, f ^ (1 << bit)) for f in range(fsdp)])


def call(body, outs, ins, scratch=()):
    shapes = [jax.ShapeDtypeStruct(shape, dtype) for shape, dtype in outs]
    return pl.pallas_call(
        body,
        out_shape=shapes,
        in_specs=[pl.BlockSpec(memory_space=pltpu.VMEM)] * len(ins),
        out_specs=[pl.BlockSpec(memory_space=pltpu.VMEM)] * len(outs),
        scratch_shapes=[pltpu.VMEM(shape, f32) for shape in scratch],
        compiler_params=pltpu.CompilerParams(vmem_limit_bytes=vmem_bytes),
    )(*ins)


def block_at(index, size):
    return pl.ds(pl.multiple_of(index * size, size), size)


def power_kernel(tensor, blocks, mom, grad, q, buf, keep, send, total):
    buffer = mom[...] + grad[...].astype(f32)
    buf[...] = buffer
    total[...] = dot6(buffer, q[...], TT)
    rows = total.shape[0] // blocks
    me = block_id(tensor)
    for j in range(blocks):
        part = total[block_at(me ^ j, rows), :]
        if j < blocks // 2:
            keep[j * rows : (j + 1) * rows, :] = part
        else:
            send[(j - blocks // 2) * rows : (j + 1 - blocks // 2) * rows, :] = part


def cross_kernel(tensor, blocks, count, *refs):
    pieces, buf = refs[:count], refs[count]
    power, keep, send, both = refs[count + 1 :]
    rows = power.shape[0] // blocks
    me = block_id(tensor)
    j = 0
    for piece in pieces:
        for i in range(piece.shape[0] // rows):
            power[block_at(me ^ j, rows), :] = piece[i * rows : (i + 1) * rows, :]
            j += 1
    rank = power.shape[1]
    whole = power[...]
    both[:rank, :] = dot6(whole, whole, TT)
    both[rank:, :] = dot6(buf[...], whole, NN)
    half = both.shape[0] // 2
    core = lax.axis_index("fsdp") % 2
    keep[...] = both[block_at(core, half), :]
    send[...] = both[block_at(1 - core, half), :]


def invert_factor(a):
    size = a.shape[0]
    nb = block_rows
    groups = nb // 8
    lane = lax.broadcasted_iota(jnp.int32, (8, size), 1)
    row = lax.broadcasted_iota(jnp.int32, (8, size), 0)
    row_short = lax.broadcasted_iota(jnp.int32, (8, 128), 0)
    wide = size // 128

    def widen(x):
        return jnp.concatenate([x] * wide, axis=1)

    def spread(x, s):
        return jnp.broadcast_to(x[s : s + 1, :], x.shape)

    for start in range(0, size, nb):
        cols = [
            [
                jnp.broadcast_to(a[start + 8 * g : start + 8 * g + 8, start + j : start + j + 1], (8, 128))
                for g in range(groups)
            ]
            for j in range(nb)
        ]
        panel = []
        for g in range(groups):
            here = (lane >= start) & (lane < start + nb)
            unit = jnp.where(lane - start == row + 8 * g, 1.0, 0.0)
            panel.append(jnp.where(here, unit, a[start + 8 * g : start + 8 * g + 8, :]))
        pivots = [jnp.ones((8, 128), f32) for _ in range(groups)]
        for k in range(nb):
            top, s = divmod(k, 8)
            pivot = spread(cols[k][top], s)
            inverse = 1.0 / pivot
            pivots[top] = jnp.where(row_short == s, pivot, pivots[top])
            lead = spread(panel[top], s)
            leads = [spread(cols[j][top], s) for j in range(nb)]
            for g in range(top, groups):
                factor = cols[k][g] * inverse
                if g == top:
                    if s == 7:
                        continue
                    factor = jnp.where(row_short > s, factor, 0.0)
                for j in range(k + 1, nb):
                    cols[j][g] = cols[j][g] - factor * leads[j]
                panel[g] = panel[g] - widen(factor) * lead
        done = jnp.concatenate([panel[g] * widen(lax.rsqrt(pivots[g])) for g in range(groups)], axis=0)
        a[start : start + nb, :] = done
        below = start + nb
        if below < size:
            h, m, l = split3(done)
            skip = below // 128 * 128
            left = jnp.concatenate([h, h, m, m, h, l], axis=0)[:, skip:]
            right = jnp.concatenate([h, m, h, m, l, h], axis=0)
            change = lax.dot_general(left, right, TT, preferred_element_type=f32)
            lanes = lax.broadcasted_iota(jnp.int32, (size - below, size), 1)
            here = (lanes >= start) & (lanes < below)
            a[below:, :] = jnp.where(here, 0.0, a[below:, :]) - change[below - skip :, :]
    i = lax.broadcasted_iota(jnp.int32, (size, size), 0)
    j = lax.broadcasted_iota(jnp.int32, (size, size), 1)
    a[...] = jnp.where(i >= j, a[...], 0.0)


def factor_kernel(mine, theirs, inverse, right, mixed, squares, both):
    half = mine.shape[0]
    core = lax.axis_index("fsdp") % 2
    both[block_at(core, half), :] = mine[...]
    both[block_at(1 - core, half), :] = theirs[...]
    rank = both.shape[1]
    inverse[...] = both[:rank, :]
    invert_factor(inverse)
    low = inverse[...]
    r = dot6(both[rank:, :], low, NT)
    right[...] = r
    squares[...] = jnp.sum(r * r, axis=0, keepdims=True)
    mixed[...] = dot6(r, low, NN)


def momentum_kernel(buf, mixed, power, out):
    out[...] = buf[...] - (1.0 - momentum_decay) * dot6(mixed[...], power[...], NT)


def weight_kernel(scale, weight, right, squares, inverse, power, out, q_new):
    q = right[...] / (jnp.sqrt(squares[...]) + norm_eps)
    q_new[...] = q
    update = dot6(dot6(q, inverse[...], NN), power[...], NT)
    out[...] = (weight[...].astype(f32) - scale * update).astype(bf16)


def per_device(fsdp, tensor, weight, momentum, grad, q_prev):
    cols, rows = momentum.shape
    rank = q_prev.shape[1]
    scale = step_rate * math.sqrt(cols * tensor / (rows * fsdp))
    steps = bits_of(tensor)
    blocks = 2 ** (steps - 1)
    full = (rows, rank)
    buf, keep, send = call(
        functools.partial(power_kernel, tensor, blocks),
        [((cols, rows), f32), ((rows // 2, rank), f32), ((rows // 2, rank), f32)],
        [momentum, grad, q_prev],
        [full],
    )
    for step in range(steps - 1):
        total = keep + flip_tensor(send, step, fsdp, tensor)
        half = total.shape[0] // 2
        if step < steps - 2:
            send, keep = total[half:], total[:half]
    total = total + flip_tensor(total, steps - 1, fsdp, tensor)
    pieces = [total]
    for step in reversed(range(steps - 1)):
        came = flip_tensor(total, step, fsdp, tensor)
        pieces.append(came)
        if step > 0:
            total = jnp.concatenate([total, came], axis=0)
    half = (rank + cols) // 2
    power, keep, send = call(
        functools.partial(cross_kernel, tensor, blocks, len(pieces)),
        [(full, f32), ((half, rank), f32), ((half, rank), f32)],
        [*pieces, buf],
        [(rank + cols, rank)],
    )
    mine = keep + flip_fsdp(send, 0, fsdp)
    for bit in range(1, bits_of(fsdp)):
        mine = mine + flip_fsdp(mine, bit, fsdp)
    theirs = flip_fsdp(mine, 0, fsdp)
    inverse, right, mixed, squares = call(
        factor_kernel,
        [((rank, rank), f32), ((cols, rank), f32), ((cols, rank), f32), ((1, rank), f32)],
        [mine, theirs],
        [(rank + cols, rank)],
    )
    (new_momentum,) = call(momentum_kernel, [((cols, rows), f32)], [buf, mixed, power])
    for step in range(steps):
        squares = squares + flip_tensor(squares, step, fsdp, tensor)
    new_weight, q_new = call(
        functools.partial(weight_kernel, scale),
        [((cols, rows), bf16), ((cols, rank), f32)],
        [weight, right, squares, inverse, power],
    )
    return (new_weight, new_momentum, q_new)


def solution(mesh):
    placed = (P("tensor", "fsdp"), P("tensor", "fsdp"), P("tensor", "fsdp"), P("tensor", None))
    return jax.shard_map(
        functools.partial(per_device, mesh.shape["fsdp"], mesh.shape["tensor"]),
        mesh=mesh,
        in_specs=placed,
        out_specs=(P("tensor", "fsdp"), P("tensor", "fsdp"), P("tensor", None)),
        check_vma=False,
    )
```

time: 238 us -> 69.4 us (0.29)
  waiting for transfers between devices: 97.4 us -> 31.5 us
  other arithmetic: 54.4 us -> 0.15 us
  blocking collectives: 53 us -> 0 us
  starting transfers between devices: 0.08 us -> 21.4 us
  between operations: 15.5 us -> 0.71 us
  Pallas kernels: 0 us -> 12.7 us
  matrix products: 9.93 us -> 0 us
  local copies, waits for them, and re-layouts: 6.81 us -> 2.74 us
    reduce_scatter x1 -> x0, waiting for transfers between devices: 65.9 us -> none  [per_device(): lax.psum_scatter(contract_first(buffer, q_prev), 'tensor', scatter_dimens...]
    another operation x9 -> x0, other arithmetic: 53.7 us -> none  [the longest x6 33.9 us: per_device(): lower = jnp.linalg.cholesky(gram)]
    all_gather x1 -> x0, blocking collectives: 31.6 us -> none  [per_device(): raw = lax.all_gather(pieces, 'tensor', axis=0, tiled=True)]
    psum x1 -> x0, waiting for transfers between devices: 31.5 us -> none  [per_device(): gram, cross = lax.psum((local_gram, local_cross), 'fsdp')]
    ppermute x0 -> x11, waiting for transfers between devices: none -> 31.5 us  [the longest x8 23.6 us: flip_tensor(): return lax.ppermute(x, ('fsdp', 'tensor'), pairs)]
    ppermute x0 -> x11, starting transfers between devices: none -> 21.4 us  [the longest x8 19.2 us: flip_tensor(): return lax.ppermute(x, ('fsdp', 'tensor'), pairs)]
    psum x1 -> x0, blocking collectives: 21.4 us -> none  [per_device(): column_sq = lax.psum(jnp.sum(right * right, axis=0), 'tensor')]
    pallas_call x0 -> x5, Pallas kernels: none -> 12.7 us  [call(): pl.pallas_call(body, out_shape=shapes, in_specs=[pl.BlockSpec(memory_spac...]
  transfers between devices with their start and end apart: 2 -> 11, of which waited for: 2 -> 11; matrix products, arithmetic and copies ran while one was open for 0% -> 0% of each run, Pallas kernels for 0% -> 2%
where the time goes in v1:
time: 69.4 us; the launch traced here: 69.2 us
  waiting for transfers between devices  31.5 us (45%)
  starting transfers between devices  21.4 us (31%)
  Pallas kernels  12.7 us (18%)
  local copies, waits for them, and re-layouts  2.74 us (4%)
  between operations  0.71 us (1%)
    ppermute x8, waiting for transfers between devices, flip_tensor(): return lax.ppermute(x, ('fsdp', 'tensor'), pairs)  23.6 us
    ppermute x8, starting transfers between devices, flip_tensor(): return lax.ppermute(x, ('fsdp', 'tensor'), pairs)  19.2 us
    pallas_call x5, Pallas kernels, call(): pl.pallas_call(body, out_shape=shapes, in_specs=[pl.BlockSpec(memory_spac...  12.7 us
    ppermute x3, waiting for transfers between devices, flip_fsdp(): return lax.ppermute(x, 'fsdp', [(f, f ^ 1 << bit) for f in range(fsdp)])  7.86 us
    unnamed x8, local copies, waits for them, and re-layouts  2.73 us
    ppermute x3, starting transfers between devices, flip_fsdp(): return lax.ppermute(x, 'fsdp', [(f, f ^ 1 << bit) for f in range(fsdp)])  2.19 us
  transfers between devices with their start and end apart: 11, of which 11 were waited for; matrix products, arithmetic and copies ran while one was open for 0% of the time, Pallas kernels for 2%

profile of v1, /device:TPU:0, one launch (start us, length us, event | category | flops | bytes accessed | tf_op | source)
XLA Modules:
  0.0 69.2 jit_solution(17217811639689949864)
XLA Ops:
  0.6 0.9 %copy-done = f32[112,512]{1,0:T(8,128)S(1)} copy-done((f32[112,512]{1,0:T(8,128)S(1)}, f32[112,512]{1,0:T(8,128)}, u32[]{:S(2)}) %copy-start) | copy-done | bytes 229400
  4.0 3.0 %collective-permute-start = (f32[256,256]{1,0:T(8,128)S(1)}, f32[256,256]{1,0:T(8,128)S(1)}, u32[]{:S(2)}, u32[]{:S(2)}) collective-permute-start(f32[256,256]{1,0:T(8,128)S(1)} %get-tuple-element.16), channel_id=1, source_target_pairs={{0,1},{1,0},{2,3},{3,2},{4,5},{5,4},{6,7},{7,6},{8,10},{9,11},{10,... | collective-permute-start | bytes 786440 | tf_op jit(solution)/shard_map/ppermute | solution.py:72
  7.1 4.4 %collective-permute-done = f32[256,256]{1,0:T(8,128)S(1)} collective-permute-done((f32[256,256]{1,0:T(8,128)S(1)}, f32[256,256]{1,0:T(8,128)S(1)}, u32[]{:S(2)}, u32[]{:S(2)}) %collective-permute-start) | collective-permute-done | bytes 262176 | tf_op jit(solution)/shard_map/ppermute | solution.py:72
  11.5 2.1 %collective-permute-start.1 = (f32[128,256]{1,0:T(8,128)S(1)}, f32[128,256]{1,0:T(8,128)S(1)}, u32[]{:S(2)}, u32[]{:S(2)}) collective-permute-start(f32[128,256]{1,0:T(8,128)S(1)} %slice.9), channel_id=1, source_target_pairs={{0,2},{1,3},{2,0},{3,1},{4,6},{5,7},{6,4},{7,5},{8,9},{9,8},{10,11... | collective-permute-start | bytes 393224 | tf_op jit(solution)/shard_map/ppermute | solution.py:72
  13.6 2.9 %collective-permute-done.1 = f32[128,256]{1,0:T(8,128)S(1)} collective-permute-done((f32[128,256]{1,0:T(8,128)S(1)}, f32[128,256]{1,0:T(8,128)S(1)}, u32[]{:S(2)}, u32[]{:S(2)}) %collective-permute-start.1) | collective-permute-done | bytes 131104 | tf_op jit(solution)/shard_map/ppermute | solution.py:72
  16.6 3.1 %collective-permute-start.2 = (f32[128,256]{1,0:T(8,128)S(1)}, f32[128,256]{1,0:T(8,128)S(1)}, u32[]{:S(2)}, u32[]{:S(2)}) collective-permute-start(f32[128,256]{1,0:T(8,128)S(1)} %slice_add_fusion), channel_id=1, source_target_pairs={{0,4},{1,5},{2,6},{3,7},{4,0},{5,1},{6,2},{7,3},{8,12},{9,13},{10,... | collective-permute-start | bytes 393224 | tf_op jit(solution)/shard_map/ppermute | solution.py:72
  19.7 3.0 %collective-permute-done.2 = f32[128,256]{1,0:T(8,128)S(1)} collective-permute-done((f32[128,256]{1,0:T(8,128)S(1)}, f32[128,256]{1,0:T(8,128)S(1)}, u32[]{:S(2)}, u32[]{:S(2)}) %collective-permute-start.2) | collective-permute-done | bytes 131104 | tf_op jit(solution)/shard_map/ppermute | solution.py:72
  22.6 2.5 %collective-permute-start.3 = (f32[128,256]{1,0:T(8,128)S(1)}, f32[128,256]{1,0:T(8,128)S(1)}, u32[]{:S(2)}, u32[]{:S(2)}) collective-permute-start(f32[128,256]{1,0:T(8,128)S(1)} %add.26.refs_0_), channel_id=1, source_target_pairs={{0,2},{1,3},{2,0},{3,1},{4,6},{5,7},{6,4},{7,5},{8,9},{9,8},{10,11... | collective-permute-start | bytes 393224 | tf_op jit(solution)/shard_map/ppermute | solution.py:72
  25.1 3.9 %collective-permute-done.3.refs_1_ = f32[128,256]{1,0:T(8,128)S(1)} collective-permute-done((f32[128,256]{1,0:T(8,128)S(1)}, f32[128,256]{1,0:T(8,128)S(1)}, u32[]{:S(2)}, u32[]{:S(2)}) %collective-permute-start.3) | collective-permute-done | bytes 131104 | tf_op jit(solution)/shard_map/ppermute | solution.py:72
  29.0 3.3 %collective-permute-start.4 = (f32[256,256]{1,0:T(8,128)S(1)}, f32[256,256]{1,0:T(8,128)S(1)}, u32[]{:S(2)}, u32[]{:S(2)}) collective-permute-start(f32[256,256]{1,0:T(8,128)S(1)} %pad_maximum_fusion), channel_id=1, source_target_pairs={{0,1},{1,0},{2,3},{3,2},{4,5},{5,4},{6,7},{7,6},{8,10},{9,11},{10,... | collective-permute-start | bytes 786440 | tf_op jit(solution)/shard_map/ppermute | solution.py:72
  32.3 4.4 %collective-permute-done.4.refs_2_ = f32[256,256]{1,0:T(8,128)S(1)} collective-permute-done((f32[256,256]{1,0:T(8,128)S(1)}, f32[256,256]{1,0:T(8,128)S(1)}, u32[]{:S(2)}, u32[]{:S(2)}) %collective-permute-start.4) | collective-permute-done | bytes 262176 | tf_op jit(solution)/shard_map/ppermute | solution.py:72
  36.7 0.9 %shard_map.68 = (f32[512,256]{1,0:T(8,128)S(1)}, f32[184,256]{1,0:T(8,128)S(1)}, f32[184,256]{1,0:T(8,128)S(1)}) custom-call(f32[128,256]{1,0:T(8,128)S(1)} %add.26.refs_0_, f32[128,256]{1,0:T(8,128)S(1)} %collective-permute-done.3.refs_1_, f32[256,256]{1,0:T(8,128)S(1)} %collective-permute-done.4.refs_2_, f32[112,512]{1,0:T(8,128)S(1)} %get-tuple-element.17.refs_3_.buf), custom_call_target="tpu_custom_call" | custom-call | tf_op jit(solution)/shard_map/pallas_call | solution.py:81
  37.7 1.4 %collective-permute-done.5 = f32[184,256]{1,0:T(8,128)S(1)} collective-permute-done((f32[184,256]{1,0:T(8,128)S(1)}, f32[184,256]{1,0:T(8,128)S(1)}, u32[]{:S(2)}, u32[]{:S(2)}) %collective-permute-start.5) | collective-permute-done | bytes 188448 | tf_op jit(solution)/shard_map/ppermute | solution.py:76
  39.1 2.1 %collective-permute-start.6 = (f32[184,256]{1,0:T(8,128)S(1)}, f32[184,256]{1,0:T(8,128)S(1)}, u32[]{:S(2)}, u32[]{:S(2)}) collective-permute-start(f32[184,256]{1,0:T(8,128)S(1)} %add.27), channel_id=1, source_target_pairs={{0,16},{8,24},{16,0},{24,8},{1,17},{9,25},{17,1},{25,9},{2,18},{10... | collective-permute-start | bytes 565256 | tf_op jit(solution)/shard_map/ppermute | solution.py:76
  41.2 5.0 %collective-permute-done.6 = f32[184,256]{1,0:T(8,128)S(1)} collective-permute-done((f32[184,256]{1,0:T(8,128)S(1)}, f32[184,256]{1,0:T(8,128)S(1)}, u32[]{:S(2)}, u32[]{:S(2)}) %collective-permute-start.6) | collective-permute-done | bytes 188448 | tf_op jit(solution)/shard_map/ppermute | solution.py:76
  46.3 1.4 %collective-permute-done.7.theirs = f32[184,256]{1,0:T(8,128)S(1)} collective-permute-done((f32[184,256]{1,0:T(8,128)S(1)}, f32[184,256]{1,0:T(8,128)S(1)}, u32[]{:S(2)}, u32[]{:S(2)}) %collective-permute-start.7) | collective-permute-done | bytes 188448 | tf_op jit(solution)/shard_map/ppermute | solution.py:76
  47.7 8.1 %shard_map.69 = (f32[256,256]{1,0:T(8,128)S(1)}, f32[112,256]{1,0:T(8,128)S(1)}, f32[112,256]{1,0:T(8,128)S(1)}, f32[1,256]{1,0:T(1,128)S(1)}) custom-call(f32[184,256]{1,0:T(8,128)S(1)} %add.28.mine, f32[184,256]{1,0:T(8,128)S(1)} %collective-permute-done.7.theirs), custom_call_target="tpu_custom_call" | custom-call | tf_op jit(solution)/shard_map/pallas_call | solution.py:81
  55.9 1.8 %collective-permute-start.8 = (f32[1,256]{1,0:T(1,128)S(1)}, f32[1,256]{1,0:T(1,128)S(1)}, u32[]{:S(2)}, u32[]{:S(2)}) collective-permute-start(f32[1,256]{1,0:T(1,128)S(1)} %get-tuple-element.21), channel_id=1, source_target_pairs={{0,1},{1,0},{2,3},{3,2},{4,5},{5,4},{6,7},{7,6},{8,10},{9,11},{10,... | collective-permute-start | bytes 3080 | tf_op jit(solution)/shard_map/ppermute | solution.py:72
  57.7 1.8 %collective-permute-done.8 = f32[1,256]{1,0:T(1,128)S(1)} collective-permute-done((f32[1,256]{1,0:T(1,128)S(1)}, f32[1,256]{1,0:T(1,128)S(1)}, u32[]{:S(2)}, u32[]{:S(2)}) %collective-permute-start.8) | collective-permute-done | bytes 1056 | tf_op jit(solution)/shard_map/ppermute | solution.py:72
  59.5 1.0 %collective-permute-start.9 = (f32[1,256]{1,0:T(1,128)S(1)}, f32[1,256]{1,0:T(1,128)S(1)}, u32[]{:S(2)}, u32[]{:S(2)}) collective-permute-start(f32[1,256]{1,0:T(1,128)S(1)} %add.29), channel_id=1, source_target_pairs={{0,2},{1,3},{2,0},{3,1},{4,6},{5,7},{6,4},{7,5},{8,9},{9,8},{10,11... | collective-permute-start | bytes 3080 | tf_op jit(solution)/shard_map/ppermute | solution.py:72
  60.5 2.6 %collective-permute-done.9 = f32[1,256]{1,0:T(1,128)S(1)} collective-permute-done((f32[1,256]{1,0:T(1,128)S(1)}, f32[1,256]{1,0:T(1,128)S(1)}, u32[]{:S(2)}, u32[]{:S(2)}) %collective-permute-start.9) | collective-permute-done | bytes 1056 | tf_op jit(solution)/shard_map/ppermute | solution.py:72
  63.1 2.4 %collective-permute-start.10 = (f32[1,256]{1,0:T(1,128)S(1)}, f32[1,256]{1,0:T(1,128)S(1)}, u32[]{:S(2)}, u32[]{:S(2)}) collective-permute-start(f32[1,256]{1,0:T(1,128)S(1)} %add.30), channel_id=1, source_target_pairs={{0,4},{1,5},{2,6},{3,7},{4,0},{5,1},{6,2},{7,3},{8,12},{9,13},{10,... | collective-permute-start | bytes 3080 | tf_op jit(solution)/shard_map/ppermute | solution.py:72
  65.4 1.4 %shard_map.71 = f32[112,512]{1,0:T(8,128)} custom-call(f32[112,512]{1,0:T(8,128)S(1)} %get-tuple-element.17.refs_3_.buf, f32[112,256]{1,0:T(8,128)S(1)} %get-tuple-element.25.mixed, f32[512,256]{1,0:T(8,128)S(1)} %get-tuple-element.23.power), custom_call_target="tpu_custom_call" | custom-call | tf_op jit(solution)/shard_map/pallas_call | solution.py:81
  67.5 1.7 %shard_map.70 = (bf16[112,512]{1,0:T(8,128)(2,1)}, f32[112,256]{1,0:T(8,128)}) custom-call(bf16[112,512]{1,0:T(8,128)(2,1)S(1)} %copy-done.1, f32[112,256]{1,0:T(8,128)S(1)} %get-tuple-element.20.right, f32[1,256]{1,0:T(1,128)S(1)} %add.31.squares, f32[256,256]{1,0:T(8,128)S(1)} %get-tuple-element.22.inverse, f32[512,256]{1,0:T(8,128)S(1)} %get-tuple-element.23.power), custom_call_target="tpu_custom_call" | custom-call | tf_op jit(solution)/shard_map/pallas_call | solution.py:81
  (21 shorter events, 3.5 us)
Async XLA Ops:
  0.6 0.9 %copy-start = (f32[112,512]{1,0:T(8,128)S(1)}, f32[112,512]{1,0:T(8,128)}, u32[]{:S(2)}) copy-start(f32[112,512]{1,0:T(8,128)} %mom.1) | copy-start | bytes 688132
  1.6 0.9 %copy-start.2 = (bf16[112,512]{1,0:T(8,128)(2,1)S(1)}, bf16[112,512]{1,0:T(8,128)(2,1)}, u32[]{:S(2)}) copy-start(bf16[112,512]{1,0:T(8,128)(2,1)} %grad.1) | copy-start | bytes 344068
  2.5 0.9 %copy-start.3 = (f32[112,256]{1,0:T(8,128)S(1)}, f32[112,256]{1,0:T(8,128)}, u32[]{:S(2)}) copy-start(f32[112,256]{1,0:T(8,128)} %q.1) | copy-start | bytes 344068
  4.0 7.4 %collective-permute-start = (f32[256,256]{1,0:T(8,128)S(1)}, f32[256,256]{1,0:T(8,128)S(1)}, u32[]{:S(2)}, u32[]{:S(2)}) collective-permute-start(f32[256,256]{1,0:T(8,128)S(1)} %get-tuple-element.16), channel_id=1, source_target_pairs={{0,1},{1,0},{2,3},{3,2},{4,5},{5,4},{6,7},{7,6},{8,10},{9,11},{10,... | collective-permute-start | bytes 786440 | tf_op jit(solution)/shard_map/ppermute | solution.py:72
  11.5 5.1 %collective-permute-start.1 = (f32[128,256]{1,0:T(8,128)S(1)}, f32[128,256]{1,0:T(8,128)S(1)}, u32[]{:S(2)}, u32[]{:S(2)}) collective-permute-start(f32[128,256]{1,0:T(8,128)S(1)} %slice.9), channel_id=1, source_target_pairs={{0,2},{1,3},{2,0},{3,1},{4,6},{5,7},{6,4},{7,5},{8,9},{9,8},{10,11... | collective-permute-start | bytes 393224 | tf_op jit(solution)/shard_map/ppermute | solution.py:72
  16.6 6.1 %collective-permute-start.2 = (f32[128,256]{1,0:T(8,128)S(1)}, f32[128,256]{1,0:T(8,128)S(1)}, u32[]{:S(2)}, u32[]{:S(2)}) collective-permute-start(f32[128,256]{1,0:T(8,128)S(1)} %slice_add_fusion), channel_id=1, source_target_pairs={{0,4},{1,5},{2,6},{3,7},{4,0},{5,1},{6,2},{7,3},{8,12},{9,13},{10,... | collective-permute-start | bytes 393224 | tf_op jit(solution)/shard_map/ppermute | solution.py:72
  22.6 6.4 %collective-permute-start.3 = (f32[128,256]{1,0:T(8,128)S(1)}, f32[128,256]{1,0:T(8,128)S(1)}, u32[]{:S(2)}, u32[]{:S(2)}) collective-permute-start(f32[128,256]{1,0:T(8,128)S(1)} %add.26.refs_0_), channel_id=1, source_target_pairs={{0,2},{1,3},{2,0},{3,1},{4,6},{5,7},{6,4},{7,5},{8,9},{9,8},{10,11... | collective-permute-start | bytes 393224 | tf_op jit(solution)/shard_map/ppermute | solution.py:72
  29.0 7.7 %collective-permute-start.4 = (f32[256,256]{1,0:T(8,128)S(1)}, f32[256,256]{1,0:T(8,128)S(1)}, u32[]{:S(2)}, u32[]{:S(2)}) collective-permute-start(f32[256,256]{1,0:T(8,128)S(1)} %pad_maximum_fusion), channel_id=1, source_target_pairs={{0,1},{1,0},{2,3},{3,2},{4,5},{5,4},{6,7},{7,6},{8,10},{9,11},{10,... | collective-permute-start | bytes 786440 | tf_op jit(solution)/shard_map/ppermute | solution.py:72
  37.6 1.5 %collective-permute-start.5 = (f32[184,256]{1,0:T(8,128)S(1)}, f32[184,256]{1,0:T(8,128)S(1)}, u32[]{:S(2)}, u32[]{:S(2)}) collective-permute-start(f32[184,256]{1,0:T(8,128)S(1)} %get-tuple-element.19), channel_id=1, source_target_pairs={{0,8},{8,0},{16,24},{24,16},{1,9},{9,1},{17,25},{25,17},{2,10},{10... | collective-permute-start | bytes 565256 | tf_op jit(solution)/shard_map/ppermute | solution.py:76
  39.1 7.1 %collective-permute-start.6 = (f32[184,256]{1,0:T(8,128)S(1)}, f32[184,256]{1,0:T(8,128)S(1)}, u32[]{:S(2)}, u32[]{:S(2)}) collective-permute-start(f32[184,256]{1,0:T(8,128)S(1)} %add.27), channel_id=1, source_target_pairs={{0,16},{8,24},{16,0},{24,8},{1,17},{9,25},{17,1},{25,9},{2,18},{10... | collective-permute-start | bytes 565256 | tf_op jit(solution)/shard_map/ppermute | solution.py:76
  46.2 1.5 %collective-permute-start.7 = (f32[184,256]{1,0:T(8,128)S(1)}, f32[184,256]{1,0:T(8,128)S(1)}, u32[]{:S(2)}, u32[]{:S(2)}) collective-permute-start(f32[184,256]{1,0:T(8,128)S(1)} %add.28.mine), channel_id=1, source_target_pairs={{0,8},{8,0},{16,24},{24,16},{1,9},{9,1},{17,25},{25,17},{2,10},{10... | collective-permute-start | bytes 565256 | tf_op jit(solution)/shard_map/ppermute | solution.py:76
  55.9 3.6 %collective-permute-start.8 = (f32[1,256]{1,0:T(1,128)S(1)}, f32[1,256]{1,0:T(1,128)S(1)}, u32[]{:S(2)}, u32[]{:S(2)}) collective-permute-start(f32[1,256]{1,0:T(1,128)S(1)} %get-tuple-element.21), channel_id=1, source_target_pairs={{0,1},{1,0},{2,3},{3,2},{4,5},{5,4},{6,7},{7,6},{8,10},{9,11},{10,... | collective-permute-start | bytes 3080 | tf_op jit(solution)/shard_map/ppermute | solution.py:72
  59.5 3.6 %collective-permute-start.9 = (f32[1,256]{1,0:T(1,128)S(1)}, f32[1,256]{1,0:T(1,128)S(1)}, u32[]{:S(2)}, u32[]{:S(2)}) collective-permute-start(f32[1,256]{1,0:T(1,128)S(1)} %add.29), channel_id=1, source_target_pairs={{0,2},{1,3},{2,0},{3,1},{4,6},{5,7},{6,4},{7,5},{8,9},{9,8},{10,11... | collective-permute-start | bytes 3080 | tf_op jit(solution)/shard_map/ppermute | solution.py:72
  63.1 4.5 %collective-permute-start.10 = (f32[1,256]{1,0:T(1,128)S(1)}, f32[1,256]{1,0:T(1,128)S(1)}, u32[]{:S(2)}, u32[]{:S(2)}) collective-permute-start(f32[1,256]{1,0:T(1,128)S(1)} %add.30), channel_id=1, source_target_pairs={{0,4},{1,5},{2,6},{3,7},{4,0},{5,1},{6,2},{7,3},{8,12},{9,13},{10,... | collective-permute-start | bytes 3080 | tf_op jit(solution)/shard_map/ppermute | solution.py:72
  65.4 2.1 %copy-start.1 = (bf16[112,512]{1,0:T(8,128)(2,1)S(1)}, bf16[112,512]{1,0:T(8,128)(2,1)}, u32[]{:S(2)}) copy-start(bf16[112,512]{1,0:T(8,128)(2,1)} %weight.1) | copy-start | bytes 344068

commit v2 on v1

v2 whole, which is shorter than its diff:
```python
import functools
import math

import jax
import jax.numpy as jnp
from jax import lax
from jax.experimental import pallas as pl
from jax.experimental.pallas import tpu as pltpu
from jax.sharding import PartitionSpec as P

momentum_decay = 0.95
step_rate = 0.02
norm_eps = 1e-06
f32 = jnp.float32
bf16 = jnp.bfloat16
block_rows = 16
vmem_bytes = 32 * 1024 * 1024
TT = (((0,), (0,)), ((), ()))
NN = (((1,), (0,)), ((), ()))
NT = (((1,), (1,)), ((), ()))


def split3(x):
    high = x.astype(bf16)
    rest = x - high.astype(f32)
    mid = rest.astype(bf16)
    return high, mid, (rest - mid.astype(f32)).astype(bf16)


def dot6(a, b, dims):
    ah, am, al = split3(a)
    bh, bm, bl = split3(b)

    def one(x, y):
        return lax.dot_general(x, y, dims, preferred_element_type=f32)

    small = one(am, bm) + one(ah, bl) + one(al, bh)
    return one(ah, bh) + (one(ah, bm) + one(am, bh) + small)


def bits_of(size):
    return size.bit_length() - 1


def partner(core, j):
    return ((0, 1, 2, 3), (0, 2, 1, 3))[core][j]


def block_of(j):
    mine, core = lax.axis_index("tensor") % 4, lax.axis_index("fsdp") % 2
    return jnp.where(core == 0, mine ^ partner(0, j), mine ^ partner(1, j))


def to_partner(x, j, fsdp, tensor):
    pairs = []
    for f in range(fsdp):
        for t in range(tensor):
            pairs.append((f * tensor + t, f * tensor + (t ^ partner(f % 2, j))))
    return lax.ppermute(x, ("fsdp", "tensor"), pairs)


def flip_tensor(x, bit, tensor):
    return lax.ppermute(x, "tensor", [(t, t ^ (1 << bit)) for t in range(tensor)])


def flip_fsdp(x, bit, fsdp):
    return lax.ppermute(x, "fsdp", [(f, f ^ (1 << bit)) for f in range(fsdp)])


def flip_across(x, f_flip, t_flip, fsdp, tensor):
    pairs = []
    for f in range(fsdp):
        for t in range(tensor):
            pairs.append((f * tensor + t, (f ^ 1 ^ f_flip) * tensor + (t ^ t_flip)))
    return lax.ppermute(x, ("fsdp", "tensor"), pairs)


def call(body, outs, ins, scratch=(), micros=1):
    shapes = [jax.ShapeDtypeStruct(shape, dtype) for shape, dtype in outs]
    return pl.pallas_call(
        body,
        out_shape=shapes,
        in_specs=[pl.BlockSpec(memory_space=pltpu.VMEM)] * len(ins),
        out_specs=[pl.BlockSpec(memory_space=pltpu.VMEM)] * len(outs),
        scratch_shapes=[pltpu.VMEM(shape, f32) for shape in scratch],
        compiler_params=pltpu.CompilerParams(vmem_limit_bytes=vmem_bytes),
        cost_estimate=pl.CostEstimate(flops=int(micros * 1e9), bytes_accessed=0, transcendentals=0),
    )(*ins)


def block_at(index, size):
    return pl.ds(pl.multiple_of(index * size, size), size)


def power_kernel(mom_in, grad_in, q_in, buf, *refs):
    parts, (total, mom, grad, q, sems) = refs[:4], refs[4:]
    copies = [
        pltpu.make_async_copy(src, dst, sems.at[i])
        for i, (src, dst) in enumerate(((mom_in, mom), (grad_in, grad), (q_in, q)))
    ]
    for copy in copies:
        copy.start()
    for copy in copies:
        copy.wait()
    buffer = mom[...] + grad[...].astype(f32)
    buf[...] = buffer
    total[...] = dot6(buffer, q[...], TT)
    rows = total.shape[0] // 4
    for j in range(4):
        parts[j][...] = total[block_at(block_of(j), rows), :]


def first_gram_kernel(p0, p1, p2, p3, power, first):
    rows = power.shape[0] // 4
    half = first.shape[0]
    for j, piece in enumerate((p0, p1, p2, p3)):
        power[block_at(block_of(j), rows), :] = piece[...]
    left = power[:, :half]
    first[...] = dot6(left, left, TT)


def cross_kernel(power, buf, second, third):
    whole = power[...]
    half = second.shape[1]
    second[...] = dot6(whole, whole[:, half:], TT)
    third[...] = dot6(buf[...], whole, NN)


def invert_factor(a):
    size = a.shape[0]
    nb = block_rows
    groups = nb // 8
    lane = lax.broadcasted_iota(jnp.int32, (8, size), 1)
    row = lax.broadcasted_iota(jnp.int32, (8, size), 0)
    row_short = lax.broadcasted_iota(jnp.int32, (8, 128), 0)
    wide = size // 128

    def widen(x):
        return jnp.concatenate([x] * wide, axis=1)

    def spread(x, s):
        return jnp.broadcast_to(x[s : s + 1, :], x.shape)

    for start in range(0, size, nb):
        cols = [
            [
                jnp.broadcast_to(a[start + 8 * g : start + 8 * g + 8, start + j : start + j + 1], (8, 128))
                for g in range(groups)
            ]
            for j in range(nb)
        ]
        panel = []
        for g in range(groups):
            here = (lane >= start) & (lane < start + nb)
            unit = jnp.where(lane - start == row + 8 * g, 1.0, 0.0)
            panel.append(jnp.where(here, unit, a[start + 8 * g : start + 8 * g + 8, :]))
        pivots = [jnp.ones((8, 128), f32) for _ in range(groups)]
        for k in range(nb):
            top, s = divmod(k, 8)
            pivot = spread(cols[k][top], s)
            inverse = 1.0 / pivot
            pivots[top] = jnp.where(row_short == s, pivot, pivots[top])
            lead = spread(panel[top], s)
            leads = [spread(cols[j][top], s) for j in range(nb)]
            for g in range(top, groups):
                factor = cols[k][g] * inverse
                if g == top:
                    if s == 7:
                        continue
                    factor = jnp.where(row_short > s, factor, 0.0)
                for j in range(k + 1, nb):
                    cols[j][g] = cols[j][g] - factor * leads[j]
                panel[g] = panel[g] - widen(factor) * lead
        done = jnp.concatenate([panel[g] * widen(lax.rsqrt(pivots[g])) for g in range(groups)], axis=0)
        a[start : start + nb, :] = done
        below = start + nb
        if below < size:
            h, m, l = split3(done)
            skip = below // 128 * 128
            left = jnp.concatenate([h, h, m, m, h, l], axis=0)[:, skip:]
            right = jnp.concatenate([h, m, h, m, l, h], axis=0)
            change = lax.dot_general(left, right, TT, preferred_element_type=f32)
            lanes = lax.broadcasted_iota(jnp.int32, (size - below, size), 1)
            here = (lanes >= start) & (lanes < below)
            a[below:, :] = jnp.where(here, 0.0, a[below:, :]) - change[below - skip :, :]
    i = lax.broadcasted_iota(jnp.int32, (size, size), 0)
    j = lax.broadcasted_iota(jnp.int32, (size, size), 1)
    a[...] = jnp.where(i >= j, a[...], 0.0)


def first_kernel(gram, came, inverse):
    inverse[...] = gram[...] + came[...]
    invert_factor(inverse)


def second_kernel(rest, came, inverse1, inverse, corner):
    half = inverse1.shape[0]
    inv1 = inverse1[...]
    upper = dot6(inv1, rest[:half, :] + came[:half, :], NN)
    corner[...] = rest[half:, :] + came[half:, :] - dot6(upper, upper, TT)
    invert_factor(corner)
    inv2 = corner[...]
    inverse[:half, :half] = inv1
    inverse[:half, half:] = jnp.zeros_like(inv1)
    inverse[half:, :half] = -dot6(inv2, dot6(upper, inv1, TT), NN)
    inverse[half:, half:] = inv2


def right_kernel(cross, came, inverse, right, squares):
    r = dot6(cross[...] + came[...], inverse[...], NT)
    right[...] = r
    squares[...] = jnp.sum(r * r, axis=0, keepdims=True)


def ortho_kernel(power, inverse, ortho):
    ortho[...] = dot6(power[...], inverse[...], NT)


def momentum_kernel(buf, right, ortho, out):
    out[...] = buf[...] - (1.0 - momentum_decay) * dot6(right[...], ortho[...], NT)


def weight_kernel(scale, weight, right, squares, ortho, out, q_new):
    q = right[...] / (jnp.sqrt(squares[...]) + norm_eps)
    q_new[...] = q
    update = dot6(q, ortho[...], NT)
    out[...] = (weight[...].astype(f32) - scale * update).astype(bf16)


def per_device(fsdp, tensor, weight, momentum, grad, q_prev):
    cols, rows = momentum.shape
    rank = q_prev.shape[1]
    half = rank // 2
    scale = step_rate * math.sqrt(cols * tensor / (rows * fsdp))
    block = ((rows // 4, rank), f32)
    buf, *parts = pl.pallas_call(
        power_kernel,
        out_shape=[jax.ShapeDtypeStruct(*x) for x in [((cols, rows), f32), block, block, block, block]],
        in_specs=[pl.BlockSpec(memory_space=pltpu.HBM)] * 3,
        out_specs=[pl.BlockSpec(memory_space=pltpu.VMEM)] * 5,
        scratch_shapes=[
            pltpu.VMEM((rows, rank), f32),
            pltpu.VMEM((cols, rows), f32),
            pltpu.VMEM((cols, rows), bf16),
            pltpu.VMEM((cols, rank), f32),
            pltpu.SemaphoreType.DMA((3,)),
        ],
        compiler_params=pltpu.CompilerParams(vmem_limit_bytes=vmem_bytes),
    )(*[pltpu.with_memory_space_constraint(x, pltpu.HBM) for x in (momentum, grad, q_prev)])
    came = [to_partner(parts[j], j, fsdp, tensor) for j in (1, 2, 3)]
    total = parts[0] + came[0] + came[1] + came[2]
    for bit in range(2, bits_of(tensor)):
        total = total + flip_tensor(total, bit, tensor)
    pieces = [total] + [to_partner(total, j, fsdp, tensor) for j in (1, 2, 3)]
    power, first = call(first_gram_kernel, [((rows, rank), f32), ((half, half), f32)], pieces)
    second, third = call(cross_kernel, [((rank, half), f32), ((cols, rank), f32)], [power, buf])
    came = [flip_fsdp(x, 0, fsdp) for x in (first, second, third)]
    first, second, third = first + came[0], second + came[1], third + came[2]
    first, second, third = lax.optimization_barrier((first, second, third))
    for bit in range(1, bits_of(fsdp) - 1):
        first, second, third = [x + flip_across(x, 1 << bit, 0, fsdp, tensor) for x in (first, second, third)]
    came = [flip_across(x, fsdp // 2, 0, fsdp, tensor) for x in (first, second, third)]
    (inverse1,) = call(first_kernel, [((half, half), f32)], [first, came[0]], micros=4)
    (inverse,) = call(second_kernel, [((rank, rank), f32)], [second, came[1], inverse1], [(half, half)], micros=4)
    right, squares = call(right_kernel, [((cols, rank), f32), ((1, rank), f32)], [third, came[2], inverse])
    (ortho,) = call(ortho_kernel, [((rows, rank), f32)], [power, inverse], micros=2)
    (new_momentum,) = call(momentum_kernel, [((cols, rows), f32)], [buf, right, ortho], micros=2)
    for bit in range(bits_of(tensor)):
        if bit == bits_of(tensor) - 1:
            squares, ortho = lax.optimization_barrier((squares, ortho))
        squares = squares + flip_across(squares, 0, 1 << bit, fsdp, tensor)
    new_weight, q_new = call(
        functools.partial(weight_kernel, scale),
        [((cols, rows), bf16), ((cols, rank), f32)],
        [weight, right, squares, ortho],
    )
    return (new_weight, new_momentum, q_new)


def solution(mesh):
    placed = (P("tensor", "fsdp"), P("tensor", "fsdp"), P("tensor", "fsdp"), P("tensor", None))
    return jax.shard_map(
        functools.partial(per_device, mesh.shape["fsdp"], mesh.shape["tensor"]),
        mesh=mesh,
        in_specs=placed,
        out_specs=(P("tensor", "fsdp"), P("tensor", "fsdp"), P("tensor", None)),
        check_vma=False,
    )
```

time: 69.4 us -> 56.9 us (0.82)
  waiting for transfers between devices: 31.5 us -> 20.5 us
  local copies, waits for them, and re-layouts: 2.74 us -> 0.01 us
  Pallas kernels: 12.7 us -> 14.3 us
    ppermute x3, waiting for transfers between devices: 7.86 us -> 1.18 us  [flip_fsdp(): return lax.ppermute(x, 'fsdp', [(f, f ^ 1 << bit) for f in range(fsdp)])]
    ppermute x8 -> x13, waiting for transfers between devices: 23.6 us -> 19.4 us  [the longest x6 10.5 us: to_partner(): return lax.ppermute(x, ('fsdp', 'tensor'), pairs)]
    unnamed x8 -> x2, local copies, waits for them, and re-layouts: 2.73 us -> 0.01 us
    pallas_call x0 -> x1, Pallas kernels: none -> 1.75 us  [per_device(): pl.pallas_call(power_kernel, out_shape=[jax.ShapeDtypeStruct(*x) for x in...]
    ppermute x3, starting transfers between devices: 2.19 us -> 0.65 us  [flip_fsdp(): return lax.ppermute(x, 'fsdp', [(f, f ^ 1 << bit) for f in range(fsdp)])]
    ppermute x8 -> x13, starting transfers between devices: 19.2 us -> 20.4 us  [the longest x6 9.38 us: flip_across(): return lax.ppermute(x, ('fsdp', 'tensor'), pairs)]
    pallas_call x5 -> x8, Pallas kernels: 12.7 us -> 12.5 us  [call(): pl.pallas_call(body, out_shape=shapes, in_specs=[pl.BlockSpec(memory_spac...]
  transfers between devices with their start and end apart: 11 -> 16, of which waited for: 11 -> 10; matrix products, arithmetic and copies ran while one was open for 0% -> 0% of each run, Pallas kernels for 2% -> 17%
where the time goes in v2:
time: 56.9 us; the launch traced here: 56.8 us
  starting transfers between devices  21.1 us (37%)
  waiting for transfers between devices  20.5 us (36%)
  Pallas kernels  14.3 us (25%)
  between operations  0.76 us (1%)
    pallas_call x8, Pallas kernels, call(): pl.pallas_call(body, out_shape=shapes, in_specs=[pl.BlockSpec(memory_spac...  12.5 us
    ppermute x6, waiting for transfers between devices, to_partner(): return lax.ppermute(x, ('fsdp', 'tensor'), pairs)  10.5 us
    ppermute x6, starting transfers between devices, flip_across(): return lax.ppermute(x, ('fsdp', 'tensor'), pairs)  9.38 us
    ppermute x6, starting transfers between devices, to_partner(): return lax.ppermute(x, ('fsdp', 'tensor'), pairs)  8.16 us
    ppermute x1, waiting for transfers between devices, flip_tensor(): return lax.ppermute(x, 'tensor', [(t, t ^ 1 << bit) for t in range(tensor)])  5.39 us
    ppermute x6, waiting for transfers between devices, flip_across(): return lax.ppermute(x, ('fsdp', 'tensor'), pairs)  3.45 us
    ppermute x1, starting transfers between devices, flip_tensor(): return lax.ppermute(x, 'tensor', [(t, t ^ 1 << bit) for t in range(tensor)])  2.89 us
    pallas_call x1, Pallas kernels, per_device(): pl.pallas_call(power_kernel, out_shape=[jax.ShapeDtypeStruct(*x) for x in...  1.75 us
  transfers between devices with their start and end apart: 16, of which 10 were waited for; matrix products, arithmetic and copies ran while one was open for 0% of the time, Pallas kernels for 17%

profile of v2, /device:TPU:0, one launch (start us, length us, event | category | flops | bytes accessed | tf_op | source)
XLA Modules:
  0.0 56.8 jit_solution(4324255347879466522)
XLA Ops:
  0.6 1.7 %shard_map.67 = (f32[112,512]{1,0:T(8,128)S(1)}, f32[128,256]{1,0:T(8,128)S(1)}, f32[128,256]{1,0:T(8,128)S(1)}, f32[128,256]{1,0:T(8,128)S(1)}, f32[128,256]{1,0:T(8,128)S(1)}) custom-call(f32[112,512]{1,0:T(8,128)} %mom_in.1, bf16[112,512]{1,0:T(8,128)(2,1)} %grad_in.1, f32[112,256]{1,0:T(8,128)} %q_in.1), custom_call_target="tpu_custom_call" | custom-call | tf_op jit(solution)/shard_map/pallas_call | solution.py:236
  2.4 3.0 %collective-permute-start = (f32[128,256]{1,0:T(8,128)S(1)}, f32[128,256]{1,0:T(8,128)S(1)}, u32[]{:S(2)}, u32[]{:S(2)}) collective-permute-start(f32[128,256]{1,0:T(8,128)S(1)} %get-tuple-element.22), channel_id=1, source_target_pairs={{0,1},{1,0},{2,3},{3,2},{4,5},{5,4},{6,7},{7,6},{8,10},{9,11},{10,... | collective-permute-start | bytes 393224 | tf_op jit(solution)/shard_map/ppermute | solution.py:59
  5.4 1.6 %collective-permute-start.1 = (f32[128,256]{1,0:T(8,128)S(1)}, f32[128,256]{1,0:T(8,128)S(1)}, u32[]{:S(2)}, u32[]{:S(2)}) collective-permute-start(f32[128,256]{1,0:T(8,128)S(1)} %get-tuple-element.23), channel_id=1, source_target_pairs={{0,2},{1,3},{2,0},{3,1},{4,6},{5,7},{6,4},{7,5},{8,9},{9,8},{10,11... | collective-permute-start | bytes 393224 | tf_op jit(solution)/shard_map/ppermute | solution.py:59
  7.0 3.2 %collective-permute-done = f32[128,256]{1,0:T(8,128)S(1)} collective-permute-done((f32[128,256]{1,0:T(8,128)S(1)}, f32[128,256]{1,0:T(8,128)S(1)}, u32[]{:S(2)}, u32[]{:S(2)}) %collective-permute-start) | collective-permute-done | bytes 131104 | tf_op jit(solution)/shard_map/ppermute | solution.py:59
  10.2 1.4 %collective-permute-done.1 = f32[128,256]{1,0:T(8,128)S(1)} collective-permute-done((f32[128,256]{1,0:T(8,128)S(1)}, f32[128,256]{1,0:T(8,128)S(1)}, u32[]{:S(2)}, u32[]{:S(2)}) %collective-permute-start.1) | collective-permute-done | bytes 131104 | tf_op jit(solution)/shard_map/ppermute | solution.py:59
  11.6 1.3 %collective-permute-done.2 = f32[128,256]{1,0:T(8,128)S(1)} collective-permute-done((f32[128,256]{1,0:T(8,128)S(1)}, f32[128,256]{1,0:T(8,128)S(1)}, u32[]{:S(2)}, u32[]{:S(2)}) %collective-permute-start.2) | collective-permute-done | bytes 131104 | tf_op jit(solution)/shard_map/ppermute | solution.py:59
  12.9 2.9 %collective-permute-start.3 = (f32[128,256]{1,0:T(8,128)S(1)}, f32[128,256]{1,0:T(8,128)S(1)}, u32[]{:S(2)}, u32[]{:S(2)}) collective-permute-start(f32[128,256]{1,0:T(8,128)S(1)} %add_add_fusion), channel_id=1, source_target_pairs={{0,4},{1,5},{2,6},{3,7},{4,0},{5,1},{6,2},{7,3},{8,12},{9,13},{10,... | collective-permute-start | bytes 393224 | tf_op jit(solution)/shard_map/ppermute | solution.py:63
  15.8 5.4 %collective-permute-done.3 = f32[128,256]{1,0:T(8,128)S(1)} collective-permute-done((f32[128,256]{1,0:T(8,128)S(1)}, f32[128,256]{1,0:T(8,128)S(1)}, u32[]{:S(2)}, u32[]{:S(2)}) %collective-permute-start.3) | collective-permute-done | bytes 131104 | tf_op jit(solution)/shard_map/ppermute | solution.py:63
  21.2 1.3 %collective-permute-start.4 = (f32[128,256]{1,0:T(8,128)S(1)}, f32[128,256]{1,0:T(8,128)S(1)}, u32[]{:S(2)}, u32[]{:S(2)}) collective-permute-start(f32[128,256]{1,0:T(8,128)S(1)} %add.33.p0), channel_id=1, source_target_pairs={{0,1},{1,0},{2,3},{3,2},{4,5},{5,4},{6,7},{7,6},{8,10},{9,11},{10,... | collective-permute-start | bytes 393224 | tf_op jit(solution)/shard_map/ppermute | solution.py:59
  23.2 1.6 %collective-permute-start.6 = (f32[128,256]{1,0:T(8,128)S(1)}, f32[128,256]{1,0:T(8,128)S(1)}, u32[]{:S(2)}, u32[]{:S(2)}) collective-permute-start(f32[128,256]{1,0:T(8,128)S(1)} %add.33.p0), channel_id=1, source_target_pairs={{0,3},{1,2},{2,1},{3,0},{4,7},{5,6},{6,5},{7,4},{8,11},{9,10},{10,... | collective-permute-start | bytes 393224 | tf_op jit(solution)/shard_map/ppermute | solution.py:59
  24.8 3.0 %collective-permute-done.4.p1 = f32[128,256]{1,0:T(8,128)S(1)} collective-permute-done((f32[128,256]{1,0:T(8,128)S(1)}, f32[128,256]{1,0:T(8,128)S(1)}, u32[]{:S(2)}, u32[]{:S(2)}) %collective-permute-start.4) | collective-permute-done | bytes 131104 | tf_op jit(solution)/shard_map/ppermute | solution.py:59
  27.8 1.6 %collective-permute-done.6.p3 = f32[128,256]{1,0:T(8,128)S(1)} collective-permute-done((f32[128,256]{1,0:T(8,128)S(1)}, f32[128,256]{1,0:T(8,128)S(1)}, u32[]{:S(2)}, u32[]{:S(2)}) %collective-permute-start.6) | collective-permute-done | bytes 131104 | tf_op jit(solution)/shard_map/ppermute | solution.py:59
  31.3 1.2 %collective-permute-done.7 = f32[128,128]{1,0:T(8,128)S(1)} collective-permute-done((f32[128,128]{1,0:T(8,128)S(1)}, f32[128,128]{1,0:T(8,128)S(1)}, u32[]{:S(2)}, u32[]{:S(2)}) %collective-permute-start.7) | collective-permute-done | bytes 65568 | tf_op jit(solution)/shard_map/ppermute | solution.py:67
  32.6 1.3 %collective-permute-start.12 = (f32[128,128]{1,0:T(8,128)S(1)}, f32[128,128]{1,0:T(8,128)S(1)}, u32[]{:S(2)}, u32[]{:S(2)}) collective-permute-start(f32[128,128]{1,0:T(8,128)S(1)} %add.34.gram), channel_id=1, source_target_pairs={{0,24},{1,25},{2,26},{3,27},{4,28},{5,29},{6,30},{7,31},{8,16},{9,... | collective-permute-start | bytes 196616 | tf_op jit(solution)/shard_map/ppermute | solution.py:75
  34.4 1.3 %collective-permute-start.10 = (f32[112,256]{1,0:T(8,128)S(1)}, f32[112,256]{1,0:T(8,128)S(1)}, u32[]{:S(2)}, u32[]{:S(2)}) collective-permute-start(f32[112,256]{1,0:T(8,128)S(1)} %add.36.cross), channel_id=1, source_target_pairs={{0,24},{1,25},{2,26},{3,27},{4,28},{5,29},{6,30},{7,31},{8,16},{9,... | collective-permute-start | bytes 344072 | tf_op jit(solution)/shard_map/ppermute | solution.py:75
  35.7 1.0 %collective-permute-done.12.came = f32[128,128]{1,0:T(8,128)S(1)} collective-permute-done((f32[128,128]{1,0:T(8,128)S(1)}, f32[128,128]{1,0:T(8,128)S(1)}, u32[]{:S(2)}, u32[]{:S(2)}) %collective-permute-start.12) | collective-permute-done | bytes 65568 | tf_op jit(solution)/shard_map/ppermute | solution.py:75
  36.7 3.4 %shard_map.70.inverse1 = f32[128,128]{1,0:T(8,128)S(1)} custom-call(f32[128,128]{1,0:T(8,128)S(1)} %add.34.gram, f32[128,128]{1,0:T(8,128)S(1)} %collective-permute-done.12.came), custom_call_target="tpu_custom_call" | custom-call | flops 4000000000 | tf_op jit(solution)/shard_map/pallas_call | solution.py:80
  40.1 4.1 %shard_map.71.inverse = f32[256,256]{1,0:T(8,128)S(1)} custom-call(f32[256,128]{1,0:T(8,128)S(1)} %add.35.rest, f32[256,128]{1,0:T(8,128)S(1)} %collective-permute-done.11.came, f32[128,128]{1,0:T(8,128)S(1)} %shard_map.70.inverse1), custom_call_target="tpu_custom_call" | custom-call | flops 4000000000 | tf_op jit(solution)/shard_map/pallas_call | solution.py:80
  44.7 1.7 %collective-permute-start.13 = (f32[1,256]{1,0:T(1,128)S(1)}, f32[1,256]{1,0:T(1,128)S(1)}, u32[]{:S(2)}, u32[]{:S(2)}) collective-permute-start(f32[1,256]{1,0:T(1,128)S(1)} %get-tuple-element.34), channel_id=1, source_target_pairs={{0,9},{1,8},{2,11},{3,10},{4,13},{5,12},{6,15},{7,14},{8,1},{9,0},... | collective-permute-start | bytes 3080 | tf_op jit(solution)/shard_map/ppermute | solution.py:75
  46.4 1.4 %collective-permute-done.13 = f32[1,256]{1,0:T(1,128)S(1)} collective-permute-done((f32[1,256]{1,0:T(1,128)S(1)}, f32[1,256]{1,0:T(1,128)S(1)}, u32[]{:S(2)}, u32[]{:S(2)}) %collective-permute-start.13) | collective-permute-done | bytes 1056 | tf_op jit(solution)/shard_map/ppermute | solution.py:75
  47.8 1.3 %collective-permute-start.14 = (f32[1,256]{1,0:T(1,128)S(1)}, f32[1,256]{1,0:T(1,128)S(1)}, u32[]{:S(2)}, u32[]{:S(2)}) collective-permute-start(f32[1,256]{1,0:T(1,128)S(1)} %add.37), channel_id=1, source_target_pairs={{0,10},{1,11},{2,8},{3,9},{4,14},{5,15},{6,12},{7,13},{8,2},{9,3},... | collective-permute-start | bytes 3080 | tf_op jit(solution)/shard_map/ppermute | solution.py:75
  50.8 3.3 %collective-permute-start.15 = (f32[1,256]{1,0:T(1,128)S(1)}, f32[1,256]{1,0:T(1,128)S(1)}, u32[]{:S(2)}, u32[]{:S(2)}) collective-permute-start(f32[1,256]{1,0:T(1,128)S(1)} %add.38), channel_id=1, source_target_pairs={{0,12},{1,13},{2,14},{3,15},{4,8},{5,9},{6,10},{7,11},{8,4},{9,5},... | collective-permute-start | bytes 3080 | tf_op jit(solution)/shard_map/ppermute | solution.py:75
  54.1 1.4 %shard_map.75 = f32[112,512]{1,0:T(8,128)} custom-call(f32[112,512]{1,0:T(8,128)S(1)} %get-tuple-element.27.buf, f32[112,256]{1,0:T(8,128)S(1)} %get-tuple-element.33.right, f32[512,256]{1,0:T(8,128)S(1)} %shard_map.73.ortho), custom_call_target="tpu_custom_call" | custom-call | flops 2000000000 | tf_op jit(solution)/shard_map/pallas_call | solution.py:80
  55.4 1.3 %shard_map.74 = (bf16[112,512]{1,0:T(8,128)(2,1)}, f32[112,256]{1,0:T(8,128)}) custom-call(bf16[112,512]{1,0:T(8,128)(2,1)S(1)} %copy-done, f32[112,256]{1,0:T(8,128)S(1)} %get-tuple-element.33.right, f32[1,256]{1,0:T(1,128)S(1)} %add.39.squares, f32[512,256]{1,0:T(8,128)S(1)} %shard_map.73.ortho), custom_call_target="tpu_custom_call" | custom-call | flops 1000000000 | tf_op jit(solution)/shard_map/pallas_call | solution.py:80
  (27 shorter events, 5.2 us)
Async XLA Ops:
  2.4 7.8 %collective-permute-start = (f32[128,256]{1,0:T(8,128)S(1)}, f32[128,256]{1,0:T(8,128)S(1)}, u32[]{:S(2)}, u32[]{:S(2)}) collective-permute-start(f32[128,256]{1,0:T(8,128)S(1)} %get-tuple-element.22), channel_id=1, source_target_pairs={{0,1},{1,0},{2,3},{3,2},{4,5},{5,4},{6,7},{7,6},{8,10},{9,11},{10,... | collective-permute-start | bytes 393224 | tf_op jit(solution)/shard_map/ppermute | solution.py:59
  5.4 6.2 %collective-permute-start.1 = (f32[128,256]{1,0:T(8,128)S(1)}, f32[128,256]{1,0:T(8,128)S(1)}, u32[]{:S(2)}, u32[]{:S(2)}) collective-permute-start(f32[128,256]{1,0:T(8,128)S(1)} %get-tuple-element.23), channel_id=1, source_target_pairs={{0,2},{1,3},{2,0},{3,1},{4,6},{5,7},{6,4},{7,5},{8,9},{9,8},{10,11... | collective-permute-start | bytes 393224 | tf_op jit(solution)/shard_map/ppermute | solution.py:59
  7.0 5.9 %collective-permute-start.2 = (f32[128,256]{1,0:T(8,128)S(1)}, f32[128,256]{1,0:T(8,128)S(1)}, u32[]{:S(2)}, u32[]{:S(2)}) collective-permute-start(f32[128,256]{1,0:T(8,128)S(1)} %get-tuple-element.24), channel_id=1, source_target_pairs={{0,3},{1,2},{2,1},{3,0},{4,7},{5,6},{6,5},{7,4},{8,11},{9,10},{10,... | collective-permute-start | bytes 393224 | tf_op jit(solution)/shard_map/ppermute | solution.py:59
  12.9 8.3 %collective-permute-start.3 = (f32[128,256]{1,0:T(8,128)S(1)}, f32[128,256]{1,0:T(8,128)S(1)}, u32[]{:S(2)}, u32[]{:S(2)}) collective-permute-start(f32[128,256]{1,0:T(8,128)S(1)} %add_add_fusion), channel_id=1, source_target_pairs={{0,4},{1,5},{2,6},{3,7},{4,0},{5,1},{6,2},{7,3},{8,12},{9,13},{10,... | collective-permute-start | bytes 393224 | tf_op jit(solution)/shard_map/ppermute | solution.py:63
  21.2 6.5 %collective-permute-start.4 = (f32[128,256]{1,0:T(8,128)S(1)}, f32[128,256]{1,0:T(8,128)S(1)}, u32[]{:S(2)}, u32[]{:S(2)}) collective-permute-start(f32[128,256]{1,0:T(8,128)S(1)} %add.33.p0), channel_id=1, source_target_pairs={{0,1},{1,0},{2,3},{3,2},{4,5},{5,4},{6,7},{7,6},{8,10},{9,11},{10,... | collective-permute-start | bytes 393224 | tf_op jit(solution)/shard_map/ppermute | solution.py:59
  22.5 5.3 %collective-permute-start.5 = (f32[128,256]{1,0:T(8,128)S(1)}, f32[128,256]{1,0:T(8,128)S(1)}, u32[]{:S(2)}, u32[]{:S(2)}) collective-permute-start(f32[128,256]{1,0:T(8,128)S(1)} %add.33.p0), channel_id=1, source_target_pairs={{0,2},{1,3},{2,0},{3,1},{4,6},{5,7},{6,4},{7,5},{8,9},{9,8},{10,11... | collective-permute-start | bytes 393224 | tf_op jit(solution)/shard_map/ppermute | solution.py:59
  23.2 6.2 %collective-permute-start.6 = (f32[128,256]{1,0:T(8,128)S(1)}, f32[128,256]{1,0:T(8,128)S(1)}, u32[]{:S(2)}, u32[]{:S(2)}) collective-permute-start(f32[128,256]{1,0:T(8,128)S(1)} %add.33.p0), channel_id=1, source_target_pairs={{0,3},{1,2},{2,1},{3,0},{4,7},{5,6},{6,5},{7,4},{8,11},{9,10},{10,... | collective-permute-start | bytes 393224 | tf_op jit(solution)/shard_map/ppermute | solution.py:59
  30.7 1.9 %collective-permute-start.8 = (f32[256,128]{1,0:T(8,128)S(1)}, f32[256,128]{1,0:T(8,128)S(1)}, u32[]{:S(2)}, u32[]{:S(2)}) collective-permute-start(f32[256,128]{1,0:T(8,128)S(1)} %get-tuple-element.28), channel_id=1, source_target_pairs={{0,8},{8,0},{16,24},{24,16},{1,9},{9,1},{17,25},{25,17},{2,10},{10... | collective-permute-start | bytes 393224 | tf_op jit(solution)/shard_map/ppermute | solution.py:67
  30.8 1.8 %collective-permute-start.9 = (f32[112,256]{1,0:T(8,128)S(1)}, f32[112,256]{1,0:T(8,128)S(1)}, u32[]{:S(2)}, u32[]{:S(2)}) collective-permute-start(f32[112,256]{1,0:T(8,128)S(1)} %get-tuple-element.29), channel_id=1, source_target_pairs={{0,8},{8,0},{16,24},{24,16},{1,9},{9,1},{17,25},{25,17},{2,10},{10... | collective-permute-start | bytes 344072 | tf_op jit(solution)/shard_map/ppermute | solution.py:67
  31.2 1.3 %collective-permute-start.7 = (f32[128,128]{1,0:T(8,128)S(1)}, f32[128,128]{1,0:T(8,128)S(1)}, u32[]{:S(2)}, u32[]{:S(2)}) collective-permute-start(f32[128,128]{1,0:T(8,128)S(1)} %get-tuple-element.25), channel_id=1, source_target_pairs={{0,8},{8,0},{16,24},{24,16},{1,9},{9,1},{17,25},{25,17},{2,10},{10... | collective-permute-start | bytes 196616 | tf_op jit(solution)/shard_map/ppermute | solution.py:67
  32.6 4.1 %collective-permute-start.12 = (f32[128,128]{1,0:T(8,128)S(1)}, f32[128,128]{1,0:T(8,128)S(1)}, u32[]{:S(2)}, u32[]{:S(2)}) collective-permute-start(f32[128,128]{1,0:T(8,128)S(1)} %add.34.gram), channel_id=1, source_target_pairs={{0,24},{1,25},{2,26},{3,27},{4,28},{5,29},{6,30},{7,31},{8,16},{9,... | collective-permute-start | bytes 196616 | tf_op jit(solution)/shard_map/ppermute | solution.py:75
  33.9 6.2 %collective-permute-start.11 = (f32[256,128]{1,0:T(8,128)S(1)}, f32[256,128]{1,0:T(8,128)S(1)}, u32[]{:S(2)}, u32[]{:S(2)}) collective-permute-start(f32[256,128]{1,0:T(8,128)S(1)} %add.35.rest), channel_id=1, source_target_pairs={{0,24},{1,25},{2,26},{3,27},{4,28},{5,29},{6,30},{7,31},{8,16},{9,... | collective-permute-start | bytes 393224 | tf_op jit(solution)/shard_map/ppermute | solution.py:75
  34.4 9.9 %collective-permute-start.10 = (f32[112,256]{1,0:T(8,128)S(1)}, f32[112,256]{1,0:T(8,128)S(1)}, u32[]{:S(2)}, u32[]{:S(2)}) collective-permute-start(f32[112,256]{1,0:T(8,128)S(1)} %add.36.cross), channel_id=1, source_target_pairs={{0,24},{1,25},{2,26},{3,27},{4,28},{5,29},{6,30},{7,31},{8,16},{9,... | collective-permute-start | bytes 344072 | tf_op jit(solution)/shard_map/ppermute | solution.py:75
  44.7 3.1 %collective-permute-start.13 = (f32[1,256]{1,0:T(1,128)S(1)}, f32[1,256]{1,0:T(1,128)S(1)}, u32[]{:S(2)}, u32[]{:S(2)}) collective-permute-start(f32[1,256]{1,0:T(1,128)S(1)} %get-tuple-element.34), channel_id=1, source_target_pairs={{0,9},{1,8},{2,11},{3,10},{4,13},{5,12},{6,15},{7,14},{8,1},{9,0},... | collective-permute-start | bytes 3080 | tf_op jit(solution)/shard_map/ppermute | solution.py:75
  47.8 3.0 %collective-permute-start.14 = (f32[1,256]{1,0:T(1,128)S(1)}, f32[1,256]{1,0:T(1,128)S(1)}, u32[]{:S(2)}, u32[]{:S(2)}) collective-permute-start(f32[1,256]{1,0:T(1,128)S(1)} %add.37), channel_id=1, source_target_pairs={{0,10},{1,11},{2,8},{3,9},{4,14},{5,15},{6,12},{7,13},{8,2},{9,3},... | collective-permute-start | bytes 3080 | tf_op jit(solution)/shard_map/ppermute | solution.py:75
  50.8 4.7 %collective-permute-start.15 = (f32[1,256]{1,0:T(1,128)S(1)}, f32[1,256]{1,0:T(1,128)S(1)}, u32[]{:S(2)}, u32[]{:S(2)}) collective-permute-start(f32[1,256]{1,0:T(1,128)S(1)} %add.38), channel_id=1, source_target_pairs={{0,12},{1,13},{2,14},{3,15},{4,8},{5,9},{6,10},{7,11},{8,4},{9,5},... | collective-permute-start | bytes 3080 | tf_op jit(solution)/shard_map/ppermute | solution.py:75
  54.1 1.4 %copy-start = (bf16[112,512]{1,0:T(8,128)(2,1)S(1)}, bf16[112,512]{1,0:T(8,128)(2,1)}, u32[]{:S(2)}) copy-start(bf16[112,512]{1,0:T(8,128)(2,1)} %weight.1) | copy-start | bytes 344068

commit v3 on v2

v3 whole, which is shorter than its diff:
```python
import functools
import math

import jax
import jax.numpy as jnp
from jax import lax
from jax.experimental import pallas as pl
from jax.experimental.pallas import tpu as pltpu
from jax.sharding import PartitionSpec as P

momentum_decay = 0.95
step_rate = 0.02
norm_eps = 1e-06
f32 = jnp.float32
bf16 = jnp.bfloat16
block_rows = 32
step_rows = 16
vmem_bytes = 32 * 1024 * 1024
TT = (((0,), (0,)), ((), ()))
NN = (((1,), (0,)), ((), ()))
NT = (((1,), (1,)), ((), ()))


def split3(x):
    high = x.astype(bf16)
    rest = x - high.astype(f32)
    mid = rest.astype(bf16)
    return high, mid, (rest - mid.astype(f32)).astype(bf16)


def dot6(a, b, dims):
    ah, am, al = split3(a)
    bh, bm, bl = split3(b)

    def one(x, y):
        return lax.dot_general(x, y, dims, preferred_element_type=f32)

    small = one(am, bm) + one(ah, bl) + one(al, bh)
    return one(ah, bh) + (one(ah, bm) + one(am, bh) + small)


def bits_of(size):
    return size.bit_length() - 1


def partner(core, j):
    return ((0, 1, 2, 3), (0, 2, 1, 3))[core][j]


def block_of(j):
    mine, core = lax.axis_index("tensor") % 4, lax.axis_index("fsdp") % 2
    return jnp.where(core == 0, mine ^ partner(0, j), mine ^ partner(1, j))


def to_partner(x, j, fsdp, tensor):
    pairs = []
    for f in range(fsdp):
        for t in range(tensor):
            pairs.append((f * tensor + t, f * tensor + (t ^ partner(f % 2, j))))
    return lax.ppermute(x, ("fsdp", "tensor"), pairs)


def flip_tensor(x, bit, tensor):
    return lax.ppermute(x, "tensor", [(t, t ^ (1 << bit)) for t in range(tensor)])


def flip_fsdp(x, bit, fsdp):
    return lax.ppermute(x, "fsdp", [(f, f ^ (1 << bit)) for f in range(fsdp)])


def flip_across(x, f_flip, t_flip, fsdp, tensor):
    pairs = []
    for f in range(fsdp):
        for t in range(tensor):
            pairs.append((f * tensor + t, (f ^ 1 ^ f_flip) * tensor + (t ^ t_flip)))
    return lax.ppermute(x, ("fsdp", "tensor"), pairs)


def call(body, outs, ins, scratch=(), micros=1):
    shapes = [jax.ShapeDtypeStruct(shape, dtype) for shape, dtype in outs]
    return pl.pallas_call(
        body,
        out_shape=shapes,
        in_specs=[pl.BlockSpec(memory_space=pltpu.VMEM)] * len(ins),
        out_specs=[pl.BlockSpec(memory_space=pltpu.VMEM)] * len(outs),
        scratch_shapes=[pltpu.VMEM(shape, f32) for shape in scratch],
        compiler_params=pltpu.CompilerParams(vmem_limit_bytes=vmem_bytes),
        cost_estimate=pl.CostEstimate(flops=int(micros * 1e9), bytes_accessed=0, transcendentals=0),
    )(*ins)


def block_at(index, size):
    return pl.ds(pl.multiple_of(index * size, size), size)


def power_kernel(mom_in, grad_in, q_in, buf, *refs):
    parts, (total, mom, grad, q, sems) = refs[:8], refs[8:]
    copies = [
        pltpu.make_async_copy(src, dst, sems.at[i])
        for i, (src, dst) in enumerate(((mom_in, mom), (grad_in, grad), (q_in, q)))
    ]
    for copy in copies:
        copy.start()
    for copy in copies:
        copy.wait()
    buffer = mom[...] + grad[...].astype(f32)
    buf[...] = buffer
    total[...] = dot6(buffer, q[...], TT)
    rows = total.shape[0] // 4
    half = total.shape[1] // 2
    for j in range(4):
        here = block_at(block_of(j), rows)
        parts[j][...] = total[here, :half]
        parts[4 + j][...] = total[here, half:]


def gather_blocks(pieces, out):
    rows = out.shape[0] // 4
    for j, piece in enumerate(pieces):
        out[block_at(block_of(j), rows), :] = piece[...]


def first_gram_kernel(p0, p1, p2, p3, left, first):
    gather_blocks((p0, p1, p2, p3), left)
    first[...] = dot6(left[...], left[...], TT)


def cross_kernel(p0, p1, p2, p3, left, buf, power, second, third, right):
    gather_blocks((p0, p1, p2, p3), right)
    whole = jnp.concatenate([left[...], right[...]], axis=1)
    power[...] = whole
    second[...] = dot6(whole, right[...], TT)
    third[...] = dot6(buf[...], whole, NN)


def invert_factor(a):
    size = a.shape[0]
    groups = block_rows // 8
    lane = lax.broadcasted_iota(jnp.int32, (8, size), 1)
    row = lax.broadcasted_iota(jnp.int32, (8, size), 0)
    row_short = lax.broadcasted_iota(jnp.int32, (8, 128), 0)
    wide = size // 128

    def widen(x):
        return jnp.concatenate([x] * wide, axis=1) if wide > 1 else x

    def spread(x, s):
        return jnp.broadcast_to(x[s : s + 1, :], x.shape)

    for start in range(0, size, block_rows):
        panel = [a[start + 8 * g : start + 8 * g + 8, :] for g in range(groups)]
        pivots = [jnp.ones((8, 128), f32) for _ in range(groups)]
        for done in range(0, block_rows, step_rows):
            first = start + done
            cols = [
                {g: jnp.broadcast_to(panel[g][:, first + j : first + j + 1], (8, 128)) for g in range(done // 8, groups)}
                for j in range(step_rows)
            ]
            for g in range(groups):
                here = (lane >= first) & (lane < first + step_rows)
                panel[g] = jnp.where(here, jnp.where(lane - start == row + 8 * g, 1.0, 0.0), panel[g])
            for k in range(step_rows):
                top, s = divmod(done + k, 8)
                leads = {j: spread(cols[j][top], s) for j in range(k, step_rows)}
                inverse = 1.0 / leads[k]
                pivots[top] = jnp.where(row_short == s, leads[k], pivots[top])
                lead = spread(panel[top], s)
                for g in range(top, groups):
                    if g == top and s == 7:
                        continue
                    factor = cols[k][g] * inverse
                    for j in range(k + 1, step_rows):
                        cols[j][g] = cols[j][g] - factor * leads[j]
                    if g == top:
                        factor = jnp.where(row_short > s, factor, 0.0)
                    panel[g] = panel[g] - widen(factor) * lead
        rows = jnp.concatenate([panel[g] * widen(lax.rsqrt(pivots[g])) for g in range(groups)], axis=0)
        below = start + block_rows
        a[start:below, :] = rows
        if below < size:
            h, m, l = split3(rows)
            skip = below // 128 * 128
            left = jnp.concatenate([h, h, m, m, h, l], axis=0)[:, skip:]
            right = jnp.concatenate([h, m, h, m, l, h], axis=0)
            change = lax.dot_general(left, right, TT, preferred_element_type=f32)
            lanes = lax.broadcasted_iota(jnp.int32, (size - below, size), 1)
            here = (lanes >= start) & (lanes < below)
            a[below:, :] = jnp.where(here, 0.0, a[below:, :]) - change[below - skip :, :]
    i = lax.broadcasted_iota(jnp.int32, (size, size), 0)
    j = lax.broadcasted_iota(jnp.int32, (size, size), 1)
    a[...] = jnp.where(i >= j, a[...], 0.0)


def first_kernel(gram, came, inverse):
    inverse[...] = gram[...] + came[...]
    invert_factor(inverse)


def second_kernel(rest, came, inverse1, inverse, corner):
    half = inverse1.shape[0]
    inv1 = inverse1[...]
    upper = dot6(inv1, rest[:half, :] + came[:half, :], NN)
    corner[...] = rest[half:, :] + came[half:, :] - dot6(upper, upper, TT)
    below = dot6(upper, inv1, TT)
    invert_factor(corner)
    inv2 = corner[...]
    inverse[:half, :half] = inv1
    inverse[:half, half:] = jnp.zeros_like(inv1)
    inverse[half:, :half] = -dot6(inv2, below, NN)
    inverse[half:, half:] = inv2


def right_kernel(cross, came, inverse, right, squares):
    r = dot6(cross[...] + came[...], inverse[...], NT)
    right[...] = r
    squares[...] = jnp.sum(r * r, axis=0, keepdims=True)


def ortho_kernel(power, inverse, ortho, high, mid):
    o = dot6(power[...], inverse[...], NT)
    ortho[...] = o
    high[...], mid[...], _ = split3(o)


def momentum_kernel(buf, right, ortho, out):
    out[...] = buf[...] - (1.0 - momentum_decay) * dot6(right[...], ortho[...], NT)


def weight_kernel(scale, weight, right, squares, high, mid, out, q_new):
    q = right[...] / (jnp.sqrt(squares[...]) + norm_eps)
    q_new[...] = q
    qh, qm, _ = split3(q)

    def one(x, y):
        return lax.dot_general(x, y[...], NT, preferred_element_type=f32)

    update = one(qh, high) + (one(qh, mid) + one(qm, high) + one(qm, mid))
    out[...] = (weight[...].astype(f32) - scale * update).astype(bf16)


def per_device(fsdp, tensor, weight, momentum, grad, q_prev):
    cols, rows = momentum.shape
    rank = q_prev.shape[1]
    half = rank // 2
    scale = step_rate * math.sqrt(cols * tensor / (rows * fsdp))
    block = ((rows // 4, half), f32)
    buf, *parts = pl.pallas_call(
        power_kernel,
        out_shape=[jax.ShapeDtypeStruct(*x) for x in [((cols, rows), f32)] + [block] * 8],
        in_specs=[pl.BlockSpec(memory_space=pltpu.HBM)] * 3,
        out_specs=[pl.BlockSpec(memory_space=pltpu.VMEM)] * 9,
        scratch_shapes=[
            pltpu.VMEM((rows, rank), f32),
            pltpu.VMEM((cols, rows), f32),
            pltpu.VMEM((cols, rows), bf16),
            pltpu.VMEM((cols, rank), f32),
            pltpu.SemaphoreType.DMA((3,)),
        ],
        compiler_params=pltpu.CompilerParams(vmem_limit_bytes=vmem_bytes),
    )(*[pltpu.with_memory_space_constraint(x, pltpu.HBM) for x in (momentum, grad, q_prev)])
    totals = []
    for mine in (parts[:4], parts[4:]):
        came = [to_partner(mine[j], j, fsdp, tensor) for j in (1, 2, 3)]
        totals.append(mine[0] + came[0] + came[1] + came[2])
    for bit in range(2, bits_of(tensor)):
        totals = [x + flip_tensor(x, bit, tensor) for x in totals]
    pieces = [[x] + [to_partner(x, j, fsdp, tensor) for j in (1, 2, 3)] for x in totals]
    left, first = call(first_gram_kernel, [((rows, half), f32), ((half, half), f32)], pieces[0])
    power, second, third = call(
        cross_kernel,
        [((rows, rank), f32), ((rank, half), f32), ((cols, rank), f32)],
        [*pieces[1], left, buf],
        [(rows, half)],
    )
    first = first + flip_fsdp(first, 0, fsdp)
    came = [flip_fsdp(x, 0, fsdp) for x in (second, third)]
    second, third = lax.optimization_barrier((second + came[0], third + came[1]))
    for bit in range(1, bits_of(fsdp) - 1):
        first, second, third = [x + flip_across(x, 1 << bit, 0, fsdp, tensor) for x in (first, second, third)]
    came = [flip_across(x, fsdp // 2, 0, fsdp, tensor) for x in (first, second, third)]
    (inverse1,) = call(first_kernel, [((half, half), f32)], [first, came[0]], micros=4)
    (inverse,) = call(second_kernel, [((rank, rank), f32)], [second, came[1], inverse1], [(half, half)], micros=4)
    right, squares = call(right_kernel, [((cols, rank), f32), ((1, rank), f32)], [third, came[2], inverse])
    ortho, high, mid = call(
        ortho_kernel,
        [((rows, rank), f32), ((rows, rank), bf16), ((rows, rank), bf16)],
        [power, inverse],
    )
    (new_momentum,) = call(momentum_kernel, [((cols, rows), f32)], [buf, right, ortho], micros=2)
    came = [flip_across(squares, 0, j, fsdp, tensor) for j in (1, 2, 3)]
    squares = squares + came[0] + came[1] + came[2]
    squares, ortho = lax.optimization_barrier((squares, ortho))
    for bit in range(2, bits_of(tensor)):
        squares = squares + flip_across(squares, 0, 1 << bit, fsdp, tensor)
    new_weight, q_new = call(
        functools.partial(weight_kernel, scale),
        [((cols, rows), bf16), ((cols, rank), f32)],
        [weight, right, squares, high, mid],
    )
    return (new_weight, new_momentum, q_new)


def solution(mesh):
    placed = (P("tensor", "fsdp"), P("tensor", "fsdp"), P("tensor", "fsdp"), P("tensor", None))
    return jax.shard_map(
        functools.partial(per_device, mesh.shape["fsdp"], mesh.shape["tensor"]),
        mesh=mesh,
        in_specs=placed,
        out_specs=(P("tensor", "fsdp"), P("tensor", "fsdp"), P("tensor", None)),
        check_vma=False,
    )
```

time: 56.9 us -> 55 us (0.967)
  waiting for transfers between devices: 20.5 us -> 9.29 us
  starting transfers between devices: 21.1 us -> 31.4 us
  Pallas kernels: 14.3 us -> 13.1 us
    ppermute x6 -> x12, starting transfers between devices: 8.16 us -> 16.1 us  [to_partner(): return lax.ppermute(x, ('fsdp', 'tensor'), pairs)]
    ppermute x6 -> x12, waiting for transfers between devices: 10.5 us -> 4.2 us  [to_partner(): return lax.ppermute(x, ('fsdp', 'tensor'), pairs)]
    ppermute x1 -> x2, waiting for transfers between devices: 5.39 us -> 0.8 us  [flip_tensor(): return lax.ppermute(x, 'tensor', [(t, t ^ 1 << bit) for t in range(tensor)])]
    ppermute x1 -> x2, starting transfers between devices: 2.89 us -> 5.59 us  [flip_tensor(): return lax.ppermute(x, 'tensor', [(t, t ^ 1 << bit) for t in range(tensor)])]
    pallas_call x8, Pallas kernels: 12.5 us -> 11.3 us  [call(): pl.pallas_call(body, out_shape=shapes, in_specs=[pl.BlockSpec(memory_spac...]
    ppermute x6 -> x7, starting transfers between devices: 9.38 us -> 9.03 us  [flip_across(): return lax.ppermute(x, ('fsdp', 'tensor'), pairs)]
    ppermute x6 -> x7, waiting for transfers between devices: 3.45 us -> 3.44 us  [flip_across(): return lax.ppermute(x, ('fsdp', 'tensor'), pairs)]
  transfers between devices with their start and end apart: 16 -> 24, of which waited for: 10 -> 12; matrix products, arithmetic and copies ran while one was open for 0% -> 0% of each run, Pallas kernels for 17% -> 16%
where the time goes in v3:
time: 55 us; the launch traced here: 54.6 us
  starting transfers between devices  31.4 us (57%)
  Pallas kernels  13.1 us (24%)
  waiting for transfers between devices  9.29 us (17%)
  between operations  0.76 us (1%)
    ppermute x12, starting transfers between devices, to_partner(): return lax.ppermute(x, ('fsdp', 'tensor'), pairs)  16.1 us
    pallas_call x8, Pallas kernels, call(): pl.pallas_call(body, out_shape=shapes, in_specs=[pl.BlockSpec(memory_spac...  11.3 us
    ppermute x7, starting transfers between devices, flip_across(): return lax.ppermute(x, ('fsdp', 'tensor'), pairs)  9.03 us
    ppermute x2, starting transfers between devices, flip_tensor(): return lax.ppermute(x, 'tensor', [(t, t ^ 1 << bit) for t in range(tensor)])  5.59 us
    ppermute x12, waiting for transfers between devices, to_partner(): return lax.ppermute(x, ('fsdp', 'tensor'), pairs)  4.2 us
    ppermute x7, waiting for transfers between devices, flip_across(): return lax.ppermute(x, ('fsdp', 'tensor'), pairs)  3.44 us
    pallas_call x1, Pallas kernels, per_device(): pl.pallas_call(power_kernel, out_shape=[jax.ShapeDtypeStruct(*x) for x in...  1.75 us
  transfers between devices with their start and end apart: 24, of which 12 were waited for; matrix products, arithmetic and copies ran while one was open for 0% of the time, Pallas kernels for 16%

profile of v3, /device:TPU:0, one launch (start us, length us, event | category | flops | bytes accessed | tf_op | source)
XLA Modules:
  0.0 54.6 jit_solution(4979119593697024146)
XLA Ops:
  0.6 1.7 %shard_map.67 = (f32[112,512]{1,0:T(8,128)S(1)}, f32[128,128]{1,0:T(8,128)S(1)}, f32[128,128]{1,0:T(8,128)S(1)}, f32[128,128]{1,0:T(8,128)S(1)}, f32[128,128]{1,...) custom-call(f32[112,512]{1,0:T(8,128)} %mom_in.1, ...), custom_call_target="tpu_custom_call" | custom-call | tf_op jit(solution)/shard_map/pallas_call | solution.py:247
  2.4 3.0 %collective-permute-start.7 = (f32[128,128]{1,0:T(8,128)S(1)}, f32[128,128]{1,0:T(8,128)S(1)}, u32[]{:S(2)}, u32[]{:S(2)}) collective-permute-start(f32[128,128]{1,0:T(8,128)S(1)} %get-tuple-element.32), channel_id=1, source_target_pairs={{0,1},{1,0},{2,3},{3,2},{4,5},{5,4},{6,7},{7,6},{8,10},{9,11},{10,... | collective-permute-start | bytes 196616 | tf_op jit(solution)/shard_map/ppermute | solution.py:60
  5.4 1.6 %collective-permute-start.8 = (f32[128,128]{1,0:T(8,128)S(1)}, f32[128,128]{1,0:T(8,128)S(1)}, u32[]{:S(2)}, u32[]{:S(2)}) collective-permute-start(f32[128,128]{1,0:T(8,128)S(1)} %get-tuple-element.33), channel_id=1, source_target_pairs={{0,2},{1,3},{2,0},{3,1},{4,6},{5,7},{6,4},{7,5},{8,9},{9,8},{10,11... | collective-permute-start | bytes 196616 | tf_op jit(solution)/shard_map/ppermute | solution.py:60
  7.0 1.9 %collective-permute-start = (f32[128,128]{1,0:T(8,128)S(1)}, f32[128,128]{1,0:T(8,128)S(1)}, u32[]{:S(2)}, u32[]{:S(2)}) collective-permute-start(f32[128,128]{1,0:T(8,128)S(1)} %get-tuple-element.28), channel_id=1, source_target_pairs={{0,1},{1,0},{2,3},{3,2},{4,5},{5,4},{6,7},{7,6},{8,10},{9,11},{10,... | collective-permute-start | bytes 196616 | tf_op jit(solution)/shard_map/ppermute | solution.py:60
  8.9 1.6 %collective-permute-start.1 = (f32[128,128]{1,0:T(8,128)S(1)}, f32[128,128]{1,0:T(8,128)S(1)}, u32[]{:S(2)}, u32[]{:S(2)}) collective-permute-start(f32[128,128]{1,0:T(8,128)S(1)} %get-tuple-element.29), channel_id=1, source_target_pairs={{0,2},{1,3},{2,0},{3,1},{4,6},{5,7},{6,4},{7,5},{8,9},{9,8},{10,11... | collective-permute-start | bytes 196616 | tf_op jit(solution)/shard_map/ppermute | solution.py:60
  10.5 0.9 %collective-permute-start.2 = (f32[128,128]{1,0:T(8,128)S(1)}, f32[128,128]{1,0:T(8,128)S(1)}, u32[]{:S(2)}, u32[]{:S(2)}) collective-permute-start(f32[128,128]{1,0:T(8,128)S(1)} %get-tuple-element.30), channel_id=1, source_target_pairs={{0,3},{1,2},{2,1},{3,0},{4,7},{5,6},{6,5},{7,4},{8,11},{9,10},{10,... | collective-permute-start | bytes 196616 | tf_op jit(solution)/shard_map/ppermute | solution.py:60
  12.3 2.7 %collective-permute-start.10 = (f32[128,128]{1,0:T(8,128)S(1)}, f32[128,128]{1,0:T(8,128)S(1)}, u32[]{:S(2)}, u32[]{:S(2)}) collective-permute-start(f32[128,128]{1,0:T(8,128)S(1)} %add_add_fusion), channel_id=1, source_target_pairs={{0,4},{1,5},{2,6},{3,7},{4,0},{5,1},{6,2},{7,3},{8,12},{9,13},{10,... | collective-permute-start | bytes 196616 | tf_op jit(solution)/shard_map/ppermute | solution.py:64
  15.8 2.9 %collective-permute-start.3 = (f32[128,128]{1,0:T(8,128)S(1)}, f32[128,128]{1,0:T(8,128)S(1)}, u32[]{:S(2)}, u32[]{:S(2)}) collective-permute-start(f32[128,128]{1,0:T(8,128)S(1)} %add_add_fusion.1), channel_id=1, source_target_pairs={{0,4},{1,5},{2,6},{3,7},{4,0},{5,1},{6,2},{7,3},{8,12},{9,13},{10,... | collective-permute-start | bytes 196616 | tf_op jit(solution)/shard_map/ppermute | solution.py:64
  19.5 1.4 %collective-permute-start.11 = (f32[128,128]{1,0:T(8,128)S(1)}, f32[128,128]{1,0:T(8,128)S(1)}, u32[]{:S(2)}, u32[]{:S(2)}) collective-permute-start(f32[128,128]{1,0:T(8,128)S(1)} %add.52.p0), channel_id=1, source_target_pairs={{0,1},{1,0},{2,3},{3,2},{4,5},{5,4},{6,7},{7,6},{8,10},{9,11},{10,... | collective-permute-start | bytes 196616 | tf_op jit(solution)/shard_map/ppermute | solution.py:60
  20.9 2.2 %collective-permute-start.13 = (f32[128,128]{1,0:T(8,128)S(1)}, f32[128,128]{1,0:T(8,128)S(1)}, u32[]{:S(2)}, u32[]{:S(2)}) collective-permute-start(f32[128,128]{1,0:T(8,128)S(1)} %add.52.p0), channel_id=1, source_target_pairs={{0,3},{1,2},{2,1},{3,0},{4,7},{5,6},{6,5},{7,4},{8,11},{9,10},{10,... | collective-permute-start | bytes 196616 | tf_op jit(solution)/shard_map/ppermute | solution.py:60
  23.1 1.4 %collective-permute-start.4 = (f32[128,128]{1,0:T(8,128)S(1)}, f32[128,128]{1,0:T(8,128)S(1)}, u32[]{:S(2)}, u32[]{:S(2)}) collective-permute-start(f32[128,128]{1,0:T(8,128)S(1)} %add.48.p0), channel_id=1, source_target_pairs={{0,1},{1,0},{2,3},{3,2},{4,5},{5,4},{6,7},{7,6},{8,10},{9,11},{10,... | collective-permute-start | bytes 196616 | tf_op jit(solution)/shard_map/ppermute | solution.py:60
  24.4 2.2 %collective-permute-start.6 = (f32[128,128]{1,0:T(8,128)S(1)}, f32[128,128]{1,0:T(8,128)S(1)}, u32[]{:S(2)}, u32[]{:S(2)}) collective-permute-start(f32[128,128]{1,0:T(8,128)S(1)} %add.48.p0), channel_id=1, source_target_pairs={{0,3},{1,2},{2,1},{3,0},{4,7},{5,6},{6,5},{7,4},{8,11},{9,10},{10,... | collective-permute-start | bytes 196616 | tf_op jit(solution)/shard_map/ppermute | solution.py:60
  27.4 1.3 %collective-permute-done.5.p2 = f32[128,128]{1,0:T(8,128)S(1)} collective-permute-done((f32[128,128]{1,0:T(8,128)S(1)}, f32[128,128]{1,0:T(8,128)S(1)}, u32[]{:S(2)}, u32[]{:S(2)}) %collective-permute-start.5) | collective-permute-done | bytes 65568 | tf_op jit(solution)/shard_map/ppermute | solution.py:60
  28.7 0.9 %collective-permute-done.6.p3 = f32[128,128]{1,0:T(8,128)S(1)} collective-permute-done((f32[128,128]{1,0:T(8,128)S(1)}, f32[128,128]{1,0:T(8,128)S(1)}, u32[]{:S(2)}, u32[]{:S(2)}) %collective-permute-start.6) | collective-permute-done | bytes 65568 | tf_op jit(solution)/shard_map/ppermute | solution.py:60
  32.0 1.5 %collective-permute-start.19 = (f32[128,128]{1,0:T(8,128)S(1)}, f32[128,128]{1,0:T(8,128)S(1)}, u32[]{:S(2)}, u32[]{:S(2)}) collective-permute-start(f32[128,128]{1,0:T(8,128)S(1)} %add.55.gram), channel_id=1, source_target_pairs={{0,24},{1,25},{2,26},{3,27},{4,28},{5,29},{6,30},{7,31},{8,16},{9,... | collective-permute-start | bytes 196616 | tf_op jit(solution)/shard_map/ppermute | solution.py:76
  33.9 1.4 %collective-permute-start.16 = (f32[112,256]{1,0:T(8,128)S(1)}, f32[112,256]{1,0:T(8,128)S(1)}, u32[]{:S(2)}, u32[]{:S(2)}) collective-permute-start(f32[112,256]{1,0:T(8,128)S(1)} %add.54.cross), channel_id=1, source_target_pairs={{0,24},{1,25},{2,26},{3,27},{4,28},{5,29},{6,30},{7,31},{8,16},{9,... | collective-permute-start | bytes 344072 | tf_op jit(solution)/shard_map/ppermute | solution.py:76
  36.0 2.9 %shard_map.70.inverse1 = f32[128,128]{1,0:T(8,128)S(1)} custom-call(f32[128,128]{1,0:T(8,128)S(1)} %add.55.gram, f32[128,128]{1,0:T(8,128)S(1)} %collective-permute-done.19.came), custom_call_target="tpu_custom_call" | custom-call | flops 4000000000 | tf_op jit(solution)/shard_map/pallas_call | solution.py:81
  39.1 3.6 %shard_map.71.inverse = f32[256,256]{1,0:T(8,128)S(1)} custom-call(f32[256,128]{1,0:T(8,128)S(1)} %add.53.rest, f32[256,128]{1,0:T(8,128)S(1)} %collective-permute-done.17.came, f32[128,128]{1,0:T(8,128)S(1)} %shard_map.70.inverse1), custom_call_target="tpu_custom_call" | custom-call | flops 4000000000 | tf_op jit(solution)/shard_map/pallas_call | solution.py:81
  43.2 1.7 %collective-permute-start.20 = (f32[1,256]{1,0:T(1,128)S(1)}, f32[1,256]{1,0:T(1,128)S(1)}, u32[]{:S(2)}, u32[]{:S(2)}) collective-permute-start(f32[1,256]{1,0:T(1,128)S(1)} %get-tuple-element.43), channel_id=1, source_target_pairs={{0,9},{1,8},{2,11},{3,10},{4,13},{5,12},{6,15},{7,14},{8,1},{9,0},... | collective-permute-start | bytes 3080 | tf_op jit(solution)/shard_map/ppermute | solution.py:76
  45.7 1.0 %collective-permute-start.22 = (f32[1,256]{1,0:T(1,128)S(1)}, f32[1,256]{1,0:T(1,128)S(1)}, u32[]{:S(2)}, u32[]{:S(2)}) collective-permute-start(f32[1,256]{1,0:T(1,128)S(1)} %get-tuple-element.43), channel_id=1, source_target_pairs={{0,11},{1,10},{2,9},{3,8},{4,15},{5,14},{6,13},{7,12},{8,3},{9,2},... | collective-permute-start | bytes 3080 | tf_op jit(solution)/shard_map/ppermute | solution.py:76
  47.9 1.7 %collective-permute-done.22 = f32[1,256]{1,0:T(1,128)S(1)} collective-permute-done((f32[1,256]{1,0:T(1,128)S(1)}, f32[1,256]{1,0:T(1,128)S(1)}, u32[]{:S(2)}, u32[]{:S(2)}) %collective-permute-start.22) | collective-permute-done | bytes 1056 | tf_op jit(solution)/shard_map/ppermute | solution.py:76
  49.6 2.2 %collective-permute-start.23 = (f32[1,256]{1,0:T(1,128)S(1)}, f32[1,256]{1,0:T(1,128)S(1)}, u32[]{:S(2)}, u32[]{:S(2)}) collective-permute-start(f32[1,256]{1,0:T(1,128)S(1)} %add_add_fusion.2), channel_id=1, source_target_pairs={{0,12},{1,13},{2,14},{3,15},{4,8},{5,9},{6,10},{7,11},{8,4},{9,5},... | collective-permute-start | bytes 3080 | tf_op jit(solution)/shard_map/ppermute | solution.py:76
  51.8 1.4 %shard_map.75 = f32[112,512]{1,0:T(8,128)} custom-call(f32[112,512]{1,0:T(8,128)S(1)} %get-tuple-element.36.buf, f32[112,256]{1,0:T(8,128)S(1)} %get-tuple-element.42.right, f32[512,256]{1,0:T(8,128)S(1)} %get-tuple-element.45.ortho), custom_call_target="tpu_custom_call" | custom-call | flops 2000000000 | tf_op jit(solution)/shard_map/pallas_call | solution.py:81
  53.5 1.1 %shard_map.74 = (bf16[112,512]{1,0:T(8,128)(2,1)}, f32[112,256]{1,0:T(8,128)}) custom-call(bf16[112,512]{1,0:T(8,128)(2,1)S(1)} %copy-done, f32[112,256]{1,0:T(8,128)S(1)} %get-tuple-element.42.right, f32[1,256]{1,0:T(1,128)S(1)} %add.59.squares, bf16[512,256]{1,0:T(8,128)(2,1)S(1)} %get-tuple-element.47.high, bf16[512,256]{1,0:T(8,128)(2,1)S(1)} %get-tuple-element.48.mid), custom_call_target="tpu_custom_call" | custom-call | flops 1000000000 | tf_op jit(solution)/shard_map/pallas_call | solution.py:81
  (44 shorter events, 9.6 us)
Async XLA Ops:
  2.4 8.1 %collective-permute-start.7 = (f32[128,128]{1,0:T(8,128)S(1)}, f32[128,128]{1,0:T(8,128)S(1)}, u32[]{:S(2)}, u32[]{:S(2)}) collective-permute-start(f32[128,128]{1,0:T(8,128)S(1)} %get-tuple-element.32), channel_id=1, source_target_pairs={{0,1},{1,0},{2,3},{3,2},{4,5},{5,4},{6,7},{7,6},{8,10},{9,11},{10,... | collective-permute-start | bytes 196616 | tf_op jit(solution)/shard_map/ppermute | solution.py:60
  5.4 6.0 %collective-permute-start.8 = (f32[128,128]{1,0:T(8,128)S(1)}, f32[128,128]{1,0:T(8,128)S(1)}, u32[]{:S(2)}, u32[]{:S(2)}) collective-permute-start(f32[128,128]{1,0:T(8,128)S(1)} %get-tuple-element.33), channel_id=1, source_target_pairs={{0,2},{1,3},{2,0},{3,1},{4,6},{5,7},{6,4},{7,5},{8,9},{9,8},{10,11... | collective-permute-start | bytes 196616 | tf_op jit(solution)/shard_map/ppermute | solution.py:60
  7.0 5.3 %collective-permute-start.9 = (f32[128,128]{1,0:T(8,128)S(1)}, f32[128,128]{1,0:T(8,128)S(1)}, u32[]{:S(2)}, u32[]{:S(2)}) collective-permute-start(f32[128,128]{1,0:T(8,128)S(1)} %get-tuple-element.34), channel_id=1, source_target_pairs={{0,3},{1,2},{2,1},{3,0},{4,7},{5,6},{6,5},{7,4},{8,11},{9,10},{10,... | collective-permute-start | bytes 196616 | tf_op jit(solution)/shard_map/ppermute | solution.py:60
  7.0 7.9 %collective-permute-start = (f32[128,128]{1,0:T(8,128)S(1)}, f32[128,128]{1,0:T(8,128)S(1)}, u32[]{:S(2)}, u32[]{:S(2)}) collective-permute-start(f32[128,128]{1,0:T(8,128)S(1)} %get-tuple-element.28), channel_id=1, source_target_pairs={{0,1},{1,0},{2,3},{3,2},{4,5},{5,4},{6,7},{7,6},{8,10},{9,11},{10,... | collective-permute-start | bytes 196616 | tf_op jit(solution)/shard_map/ppermute | solution.py:60
  8.9 6.0 %collective-permute-start.1 = (f32[128,128]{1,0:T(8,128)S(1)}, f32[128,128]{1,0:T(8,128)S(1)}, u32[]{:S(2)}, u32[]{:S(2)}) collective-permute-start(f32[128,128]{1,0:T(8,128)S(1)} %get-tuple-element.29), channel_id=1, source_target_pairs={{0,2},{1,3},{2,0},{3,1},{4,6},{5,7},{6,4},{7,5},{8,9},{9,8},{10,11... | collective-permute-start | bytes 196616 | tf_op jit(solution)/shard_map/ppermute | solution.py:60
  10.5 5.2 %collective-permute-start.2 = (f32[128,128]{1,0:T(8,128)S(1)}, f32[128,128]{1,0:T(8,128)S(1)}, u32[]{:S(2)}, u32[]{:S(2)}) collective-permute-start(f32[128,128]{1,0:T(8,128)S(1)} %get-tuple-element.30), channel_id=1, source_target_pairs={{0,3},{1,2},{2,1},{3,0},{4,7},{5,6},{6,5},{7,4},{8,11},{9,10},{10,... | collective-permute-start | bytes 196616 | tf_op jit(solution)/shard_map/ppermute | solution.py:60
  12.3 7.2 %collective-permute-start.10 = (f32[128,128]{1,0:T(8,128)S(1)}, f32[128,128]{1,0:T(8,128)S(1)}, u32[]{:S(2)}, u32[]{:S(2)}) collective-permute-start(f32[128,128]{1,0:T(8,128)S(1)} %add_add_fusion), channel_id=1, source_target_pairs={{0,4},{1,5},{2,6},{3,7},{4,0},{5,1},{6,2},{7,3},{8,12},{9,13},{10,... | collective-permute-start | bytes 196616 | tf_op jit(solution)/shard_map/ppermute | solution.py:64
  15.8 7.3 %collective-permute-start.3 = (f32[128,128]{1,0:T(8,128)S(1)}, f32[128,128]{1,0:T(8,128)S(1)}, u32[]{:S(2)}, u32[]{:S(2)}) collective-permute-start(f32[128,128]{1,0:T(8,128)S(1)} %add_add_fusion.1), channel_id=1, source_target_pairs={{0,4},{1,5},{2,6},{3,7},{4,0},{5,1},{6,2},{7,3},{8,12},{9,13},{10,... | collective-permute-start | bytes 196616 | tf_op jit(solution)/shard_map/ppermute | solution.py:64
  19.5 4.9 %collective-permute-start.11 = (f32[128,128]{1,0:T(8,128)S(1)}, f32[128,128]{1,0:T(8,128)S(1)}, u32[]{:S(2)}, u32[]{:S(2)}) collective-permute-start(f32[128,128]{1,0:T(8,128)S(1)} %add.52.p0), channel_id=1, source_target_pairs={{0,1},{1,0},{2,3},{3,2},{4,5},{5,4},{6,7},{7,6},{8,10},{9,11},{10,... | collective-permute-start | bytes 196616 | tf_op jit(solution)/shard_map/ppermute | solution.py:60
  20.9 5.8 %collective-permute-start.12 = (f32[128,128]{1,0:T(8,128)S(1)}, f32[128,128]{1,0:T(8,128)S(1)}, u32[]{:S(2)}, u32[]{:S(2)}) collective-permute-start(f32[128,128]{1,0:T(8,128)S(1)} %add.52.p0), channel_id=1, source_target_pairs={{0,2},{1,3},{2,0},{3,1},{4,6},{5,7},{6,4},{7,5},{8,9},{9,8},{10,11... | collective-permute-start | bytes 196616 | tf_op jit(solution)/shard_map/ppermute | solution.py:60
  20.9 5.8 %collective-permute-start.13 = (f32[128,128]{1,0:T(8,128)S(1)}, f32[128,128]{1,0:T(8,128)S(1)}, u32[]{:S(2)}, u32[]{:S(2)}) collective-permute-start(f32[128,128]{1,0:T(8,128)S(1)} %add.52.p0), channel_id=1, source_target_pairs={{0,3},{1,2},{2,1},{3,0},{4,7},{5,6},{6,5},{7,4},{8,11},{9,10},{10,... | collective-permute-start | bytes 196616 | tf_op jit(solution)/shard_map/ppermute | solution.py:60
  23.1 4.3 %collective-permute-start.4 = (f32[128,128]{1,0:T(8,128)S(1)}, f32[128,128]{1,0:T(8,128)S(1)}, u32[]{:S(2)}, u32[]{:S(2)}) collective-permute-start(f32[128,128]{1,0:T(8,128)S(1)} %add.48.p0), channel_id=1, source_target_pairs={{0,1},{1,0},{2,3},{3,2},{4,5},{5,4},{6,7},{7,6},{8,10},{9,11},{10,... | collective-permute-start | bytes 196616 | tf_op jit(solution)/shard_map/ppermute | solution.py:60
  24.4 4.3 %collective-permute-start.5 = (f32[128,128]{1,0:T(8,128)S(1)}, f32[128,128]{1,0:T(8,128)S(1)}, u32[]{:S(2)}, u32[]{:S(2)}) collective-permute-start(f32[128,128]{1,0:T(8,128)S(1)} %add.48.p0), channel_id=1, source_target_pairs={{0,2},{1,3},{2,0},{3,1},{4,6},{5,7},{6,4},{7,5},{8,9},{9,8},{10,11... | collective-permute-start | bytes 196616 | tf_op jit(solution)/shard_map/ppermute | solution.py:60
  24.4 5.2 %collective-permute-start.6 = (f32[128,128]{1,0:T(8,128)S(1)}, f32[128,128]{1,0:T(8,128)S(1)}, u32[]{:S(2)}, u32[]{:S(2)}) collective-permute-start(f32[128,128]{1,0:T(8,128)S(1)} %add.48.p0), channel_id=1, source_target_pairs={{0,3},{1,2},{2,1},{3,0},{4,7},{5,6},{6,5},{7,4},{8,11},{9,10},{10,... | collective-permute-start | bytes 196616 | tf_op jit(solution)/shard_map/ppermute | solution.py:60
  30.5 3.0 %collective-permute-start.14 = (f32[256,128]{1,0:T(8,128)S(1)}, f32[256,128]{1,0:T(8,128)S(1)}, u32[]{:S(2)}, u32[]{:S(2)}) collective-permute-start(f32[256,128]{1,0:T(8,128)S(1)} %get-tuple-element.37), channel_id=1, source_target_pairs={{0,8},{8,0},{16,24},{24,16},{1,9},{9,1},{17,25},{25,17},{2,10},{10... | collective-permute-start | bytes 393224 | tf_op jit(solution)/shard_map/ppermute | solution.py:68
  30.6 1.4 %collective-permute-start.18 = (f32[128,128]{1,0:T(8,128)S(1)}, f32[128,128]{1,0:T(8,128)S(1)}, u32[]{:S(2)}, u32[]{:S(2)}) collective-permute-start(f32[128,128]{1,0:T(8,128)S(1)} %get-tuple-element.41), channel_id=1, source_target_pairs={{0,8},{8,0},{16,24},{24,16},{1,9},{9,1},{17,25},{25,17},{2,10},{10... | collective-permute-start | bytes 196616 | tf_op jit(solution)/shard_map/ppermute | solution.py:68
  31.1 2.4 %collective-permute-start.15 = (f32[112,256]{1,0:T(8,128)S(1)}, f32[112,256]{1,0:T(8,128)S(1)}, u32[]{:S(2)}, u32[]{:S(2)}) collective-permute-start(f32[112,256]{1,0:T(8,128)S(1)} %get-tuple-element.38), channel_id=1, source_target_pairs={{0,8},{8,0},{16,24},{24,16},{1,9},{9,1},{17,25},{25,17},{2,10},{10... | collective-permute-start | bytes 344072 | tf_op jit(solution)/shard_map/ppermute | solution.py:68
  32.0 4.0 %collective-permute-start.19 = (f32[128,128]{1,0:T(8,128)S(1)}, f32[128,128]{1,0:T(8,128)S(1)}, u32[]{:S(2)}, u32[]{:S(2)}) collective-permute-start(f32[128,128]{1,0:T(8,128)S(1)} %add.55.gram), channel_id=1, source_target_pairs={{0,24},{1,25},{2,26},{3,27},{4,28},{5,29},{6,30},{7,31},{8,16},{9,... | collective-permute-start | bytes 196616 | tf_op jit(solution)/shard_map/ppermute | solution.py:76
  33.5 5.6 %collective-permute-start.17 = (f32[256,128]{1,0:T(8,128)S(1)}, f32[256,128]{1,0:T(8,128)S(1)}, u32[]{:S(2)}, u32[]{:S(2)}) collective-permute-start(f32[256,128]{1,0:T(8,128)S(1)} %add.53.rest), channel_id=1, source_target_pairs={{0,24},{1,25},{2,26},{3,27},{4,28},{5,29},{6,30},{7,31},{8,16},{9,... | collective-permute-start | bytes 393224 | tf_op jit(solution)/shard_map/ppermute | solution.py:76
  33.9 8.8 %collective-permute-start.16 = (f32[112,256]{1,0:T(8,128)S(1)}, f32[112,256]{1,0:T(8,128)S(1)}, u32[]{:S(2)}, u32[]{:S(2)}) collective-permute-start(f32[112,256]{1,0:T(8,128)S(1)} %add.54.cross), channel_id=1, source_target_pairs={{0,24},{1,25},{2,26},{3,27},{4,28},{5,29},{6,30},{7,31},{8,16},{9,... | collective-permute-start | bytes 344072 | tf_op jit(solution)/shard_map/ppermute | solution.py:76
  43.2 4.2 %collective-permute-start.20 = (f32[1,256]{1,0:T(1,128)S(1)}, f32[1,256]{1,0:T(1,128)S(1)}, u32[]{:S(2)}, u32[]{:S(2)}) collective-permute-start(f32[1,256]{1,0:T(1,128)S(1)} %get-tuple-element.43), channel_id=1, source_target_pairs={{0,9},{1,8},{2,11},{3,10},{4,13},{5,12},{6,15},{7,14},{8,1},{9,0},... | collective-permute-start | bytes 3080 | tf_op jit(solution)/shard_map/ppermute | solution.py:76
  44.9 3.0 %collective-permute-start.21 = (f32[1,256]{1,0:T(1,128)S(1)}, f32[1,256]{1,0:T(1,128)S(1)}, u32[]{:S(2)}, u32[]{:S(2)}) collective-permute-start(f32[1,256]{1,0:T(1,128)S(1)} %get-tuple-element.43), channel_id=1, source_target_pairs={{0,10},{1,11},{2,8},{3,9},{4,14},{5,15},{6,12},{7,13},{8,2},{9,3},... | collective-permute-start | bytes 3080 | tf_op jit(solution)/shard_map/ppermute | solution.py:76
  45.7 3.9 %collective-permute-start.22 = (f32[1,256]{1,0:T(1,128)S(1)}, f32[1,256]{1,0:T(1,128)S(1)}, u32[]{:S(2)}, u32[]{:S(2)}) collective-permute-start(f32[1,256]{1,0:T(1,128)S(1)} %get-tuple-element.43), channel_id=1, source_target_pairs={{0,11},{1,10},{2,9},{3,8},{4,15},{5,14},{6,13},{7,12},{8,3},{9,2},... | collective-permute-start | bytes 3080 | tf_op jit(solution)/shard_map/ppermute | solution.py:76
  49.6 3.9 %collective-permute-start.23 = (f32[1,256]{1,0:T(1,128)S(1)}, f32[1,256]{1,0:T(1,128)S(1)}, u32[]{:S(2)}, u32[]{:S(2)}) collective-permute-start(f32[1,256]{1,0:T(1,128)S(1)} %add_add_fusion.2), channel_id=1, source_target_pairs={{0,12},{1,13},{2,14},{3,15},{4,8},{5,9},{6,10},{7,11},{8,4},{9,5},... | collective-permute-start | bytes 3080 | tf_op jit(solution)/shard_map/ppermute | solution.py:76
  (1 other events, 1.7 us)

commit v4 on v3

--- a/solution.py
+++ b/solution.py
@@ -31,12 +31,10 @@
 def dot6(a, b, dims):
     ah, am, al = split3(a)
     bh, bm, bl = split3(b)
-
-    def one(x, y):
-        return lax.dot_general(x, y, dims, preferred_element_type=f32)
-
-    small = one(am, bm) + one(ah, bl) + one(al, bh)
-    return one(ah, bh) + (one(ah, bm) + one(am, bh) + small)
+    (a_dim,), (b_dim,) = dims[0]
+    left = jnp.concatenate([ah, ah, am, am, ah, al], axis=a_dim)
+    right = jnp.concatenate([bh, bm, bh, bm, bl, bh], axis=b_dim)
+    return lax.dot_general(left, right, dims, preferred_element_type=f32)
 
 
 def bits_of(size):
@@ -44,7 +42,7 @@
 
 
 def partner(core, j):
-    return ((0, 1, 2, 3), (0, 2, 1, 3))[core][j]
+    return ((0, 3, 1, 2), (0, 3, 2, 1))[core][j]
 
 
 def block_of(j):
@@ -105,32 +103,35 @@
         copy.wait()
     buffer = mom[...] + grad[...].astype(f32)
     buf[...] = buffer
-    total[...] = dot6(buffer, q[...], TT)
-    rows = total.shape[0] // 4
-    half = total.shape[1] // 2
+    total[...] = dot6(q[...], buffer, TT)
+    half = total.shape[0] // 2
     for j in range(4):
-        here = block_at(block_of(j), rows)
-        parts[j][...] = total[here, :half]
-        parts[4 + j][...] = total[here, half:]
+        here = block_at(block_of(j), total.shape[1] // 4)
+        parts[j][...] = total[:half, here]
+        parts[4 + j][...] = total[half:, here]
 
 
 def gather_blocks(pieces, out):
-    rows = out.shape[0] // 4
     for j, piece in enumerate(pieces):
-        out[block_at(block_of(j), rows), :] = piece[...]
-
-
-def first_gram_kernel(p0, p1, p2, p3, left, first):
-    gather_blocks((p0, p1, p2, p3), left)
-    first[...] = dot6(left[...], left[...], TT)
-
-
-def cross_kernel(p0, p1, p2, p3, left, buf, power, second, third, right):
-    gather_blocks((p0, p1, p2, p3), right)
-    whole = jnp.concatenate([left[...], right[...]], axis=1)
-    power[...] = whole
-    second[...] = dot6(whole, right[...], TT)
-    third[...] = dot6(buf[...], whole, NN)
+        out[:, block_at(block_of(j), out.shape[1] // 4)] = piece[...]
+
+
+def first_gram_kernel(p0, p1, p2, p3, upper, first):
+    gather_blocks((p0, p1, p2, p3), upper)
+    first[...] = dot6(upper[...], upper[...], NT)
+
+
+def second_gram_kernel(p0, p1, p2, p3, upper, lower, second):
+    gather_blocks((p0, p1, p2, p3), lower)
+    half = lower.shape[0]
+    second[:, :half] = dot6(lower[...], upper[...], NT)
+    second[:, half:] = dot6(lower[...], lower[...], NT)
+
+
+def cross_kernel(upper, lower, buf, third):
+    half = lower.shape[0]
+    third[:, :half] = dot6(buf[...], upper[...], NT)
+    third[:, half:] = dot6(buf[...], lower[...], NT)
 
 
 def invert_factor(a):
@@ -199,9 +200,10 @@
 def second_kernel(rest, came, inverse1, inverse, corner):
     half = inverse1.shape[0]
     inv1 = inverse1[...]
-    upper = dot6(inv1, rest[:half, :] + came[:half, :], NN)
-    corner[...] = rest[half:, :] + came[half:, :] - dot6(upper, upper, TT)
-    below = dot6(upper, inv1, TT)
+    gram = rest[...] + came[...]
+    low = dot6(gram[:, :half], inv1, NT)
+    corner[...] = gram[:, half:] - dot6(low, low, NT)
+    below = dot6(low, inv1, NN)
     invert_factor(corner)
     inv2 = corner[...]
     inverse[:half, :half] = inv1
@@ -216,14 +218,14 @@
     squares[...] = jnp.sum(r * r, axis=0, keepdims=True)
 
 
-def ortho_kernel(power, inverse, ortho, high, mid):
-    o = dot6(power[...], inverse[...], NT)
+def ortho_kernel(upper, lower, inverse, ortho, high, mid):
+    o = dot6(inverse[...], jnp.concatenate([upper[...], lower[...]], axis=0), NN)
     ortho[...] = o
     high[...], mid[...], _ = split3(o)
 
 
 def momentum_kernel(buf, right, ortho, out):
-    out[...] = buf[...] - (1.0 - momentum_decay) * dot6(right[...], ortho[...], NT)
+    out[...] = buf[...] - (1.0 - momentum_decay) * dot6(right[...], ortho[...], NN)
 
 
 def weight_kernel(scale, weight, right, squares, high, mid, out, q_new):
@@ -232,7 +234,7 @@
     qh, qm, _ = split3(q)
 
     def one(x, y):
-        return lax.dot_general(x, y[...], NT, preferred_element_type=f32)
+        return lax.dot_general(x, y[...], NN, preferred_element_type=f32)
 
     update = one(qh, high) + (one(qh, mid) + one(qm, high) + one(qm, mid))
     out[...] = (weight[...].astype(f32) - scale * update).astype(bf16)
@@ -243,14 +245,14 @@
     rank = q_prev.shape[1]
     half = rank // 2
     scale = step_rate * math.sqrt(cols * tensor / (rows * fsdp))
-    block = ((rows // 4, half), f32)
+    block = ((half, rows // 4), f32)
     buf, *parts = pl.pallas_call(
         power_kernel,
         out_shape=[jax.ShapeDtypeStruct(*x) for x in [((cols, rows), f32)] + [block] * 8],
         in_specs=[pl.BlockSpec(memory_space=pltpu.HBM)] * 3,
         out_specs=[pl.BlockSpec(memory_space=pltpu.VMEM)] * 9,
         scratch_shapes=[
-            pltpu.VMEM((rows, rank), f32),
+            pltpu.VMEM((rank, rows), f32),
             pltpu.VMEM((cols, rows), f32),
             pltpu.VMEM((cols, rows), bf16),
             pltpu.VMEM((cols, rank), f32),
@@ -265,13 +267,9 @@
     for bit in range(2, bits_of(tensor)):
         totals = [x + flip_tensor(x, bit, tensor) for x in totals]
     pieces = [[x] + [to_partner(x, j, fsdp, tensor) for j in (1, 2, 3)] for x in totals]
-    left, first = call(first_gram_kernel, [((rows, half), f32), ((half, half), f32)], pieces[0])
-    power, second, third = call(
-        cross_kernel,
-        [((rows, rank), f32), ((rank, half), f32), ((cols, rank), f32)],
-        [*pieces[1], left, buf],
-        [(rows, half)],
-    )
+    upper, first = call(first_gram_kernel, [((half, rows), f32), ((half, half), f32)], pieces[0])
+    lower, second = call(second_gram_kernel, [((half, rows), f32), ((half, rank), f32)], [*pieces[1], upper])
+    (third,) = call(cross_kernel, [((cols, rank), f32)], [upper, lower, buf])
     first = first + flip_fsdp(first, 0, fsdp)
     came = [flip_fsdp(x, 0, fsdp) for x in (second, third)]
     second, third = lax.optimization_barrier((second + came[0], third + came[1]))
@@ -283,11 +281,11 @@
     right, squares = call(right_kernel, [((cols, rank), f32), ((1, rank), f32)], [third, came[2], inverse])
     ortho, high, mid = call(
         ortho_kernel,
-        [((rows, rank), f32), ((rows, rank), bf16), ((rows, rank), bf16)],
-        [power, inverse],
+        [((rank, rows), f32), ((rank, rows), bf16), ((rank, rows), bf16)],
+        [upper, lower, inverse],
     )
     (new_momentum,) = call(momentum_kernel, [((cols, rows), f32)], [buf, right, ortho], micros=2)
-    came = [flip_across(squares, 0, j, fsdp, tensor) for j in (1, 2, 3)]
+    came = [flip_across(squares, 0, j, fsdp, tensor) for j in (3, 1, 2)]
     squares = squares + came[0] + came[1] + came[2]
     squares, ortho = lax.optimization_barrier((squares, ortho))
     for bit in range(2, bits_of(tensor)):

time: 55 us -> 53 us (0.964)
  starting transfers between devices: 31.4 us -> 29.9 us
    ppermute x12, starting transfers between devices: 16.1 us -> 14.9 us  [to_partner(): return lax.ppermute(x, ('fsdp', 'tensor'), pairs)]
    ppermute x3, waiting for transfers between devices: 0.86 us -> 0.01 us  [flip_fsdp(): return lax.ppermute(x, 'fsdp', [(f, f ^ 1 << bit) for f in range(fsdp)])]
    ppermute x7, starting transfers between devices: 9.03 us -> 8.3 us  [flip_across(): return lax.ppermute(x, ('fsdp', 'tensor'), pairs)]
    pallas_call x8 -> x9, Pallas kernels: 11.3 us -> 11.1 us  [call(): pl.pallas_call(body, out_shape=shapes, in_specs=[pl.BlockSpec(memory_spac...]
  transfers between devices with their start and end apart: 24 -> 24, of which waited for: 12 -> 11; matrix products, arithmetic and copies ran while one was open for 0% -> 0% of each run, Pallas kernels for 16% -> 19%
where the time goes in v4:
time: 53 us; the launch traced here: 52.6 us
  starting transfers between devices  29.9 us (56%)
  Pallas kernels  12.7 us (24%)
  waiting for transfers between devices  9.16 us (17%)
  between operations  0.79 us (1%)
    ppermute x12, starting transfers between devices, to_partner(): return lax.ppermute(x, ('fsdp', 'tensor'), pairs)  14.9 us
    pallas_call x9, Pallas kernels, call(): pl.pallas_call(body, out_shape=shapes, in_specs=[pl.BlockSpec(memory_spac...  11.1 us
    ppermute x7, starting transfers between devices, flip_across(): return lax.ppermute(x, ('fsdp', 'tensor'), pairs)  8.3 us
    ppermute x2, starting transfers between devices, flip_tensor(): return lax.ppermute(x, 'tensor', [(t, t ^ 1 << bit) for t in range(tensor)])  5.99 us
    ppermute x12, waiting for transfers between devices, to_partner(): return lax.ppermute(x, ('fsdp', 'tensor'), pairs)  4.37 us
    ppermute x7, waiting for transfers between devices, flip_across(): return lax.ppermute(x, ('fsdp', 'tensor'), pairs)  3.52 us
    pallas_call x1, Pallas kernels, per_device(): pl.pallas_call(power_kernel, out_shape=[jax.ShapeDtypeStruct(*x) for x in...  1.58 us
    ppermute x2, waiting for transfers between devices, flip_tensor(): return lax.ppermute(x, 'tensor', [(t, t ^ 1 << bit) for t in range(tensor)])  1.25 us
  transfers between devices with their start and end apart: 24, of which 11 were waited for; matrix products, arithmetic and copies ran while one was open for 0% of the time, Pallas kernels for 19%

profile of v4, /device:TPU:0, one launch (start us, length us, event | category | flops | bytes accessed | tf_op | source)
XLA Modules:
  0.0 52.6 jit_solution(4443464259996679649)
XLA Ops:
  0.6 1.6 %shard_map.67 = (f32[112,512]{1,0:T(8,128)S(1)}, f32[128,128]{1,0:T(8,128)S(1)}, f32[128,128]{1,0:T(8,128)S(1)}, f32[128,128]{1,0:T(8,128)S(1)}, f32[128,128]{1,...) custom-call(f32[112,512]{1,0:T(8,128)} %mom_in.1, ...), custom_call_target="tpu_custom_call" | custom-call | tf_op jit(solution)/shard_map/pallas_call | solution.py:249
  2.2 4.0 %collective-permute-start.7 = (f32[128,128]{1,0:T(8,128)S(1)}, f32[128,128]{1,0:T(8,128)S(1)}, u32[]{:S(2)}, u32[]{:S(2)}) collective-permute-start(f32[128,128]{1,0:T(8,128)S(1)} %get-tuple-element.31), channel_id=1, source_target_pairs={{0,3},{1,2},{2,1},{3,0},{4,7},{5,6},{6,5},{7,4},{8,11},{9,10},{10,... | collective-permute-start | bytes 196616 | tf_op jit(solution)/shard_map/ppermute | solution.py:58
  6.9 2.8 %collective-permute-start = (f32[128,128]{1,0:T(8,128)S(1)}, f32[128,128]{1,0:T(8,128)S(1)}, u32[]{:S(2)}, u32[]{:S(2)}) collective-permute-start(f32[128,128]{1,0:T(8,128)S(1)} %get-tuple-element.27), channel_id=1, source_target_pairs={{0,3},{1,2},{2,1},{3,0},{4,7},{5,6},{6,5},{7,4},{8,11},{9,10},{10,... | collective-permute-start | bytes 196616 | tf_op jit(solution)/shard_map/ppermute | solution.py:58
  11.3 2.6 %collective-permute-start.10 = (f32[128,128]{1,0:T(8,128)S(1)}, f32[128,128]{1,0:T(8,128)S(1)}, u32[]{:S(2)}, u32[]{:S(2)}) collective-permute-start(f32[128,128]{1,0:T(8,128)S(1)} %add_add_fusion), channel_id=1, source_target_pairs={{0,4},{1,5},{2,6},{3,7},{4,0},{5,1},{6,2},{7,3},{8,12},{9,13},{10,... | collective-permute-start | bytes 196616 | tf_op jit(solution)/shard_map/ppermute | solution.py:62
  14.6 3.3 %collective-permute-start.3 = (f32[128,128]{1,0:T(8,128)S(1)}, f32[128,128]{1,0:T(8,128)S(1)}, u32[]{:S(2)}, u32[]{:S(2)}) collective-permute-start(f32[128,128]{1,0:T(8,128)S(1)} %add_add_fusion.1), channel_id=1, source_target_pairs={{0,4},{1,5},{2,6},{3,7},{4,0},{5,1},{6,2},{7,3},{8,12},{9,13},{10,... | collective-permute-start | bytes 196616 | tf_op jit(solution)/shard_map/ppermute | solution.py:62
  17.9 1.2 %collective-permute-done.10 = f32[128,128]{1,0:T(8,128)S(1)} collective-permute-done((f32[128,128]{1,0:T(8,128)S(1)}, f32[128,128]{1,0:T(8,128)S(1)}, u32[]{:S(2)}, u32[]{:S(2)}) %collective-permute-start.10) | collective-permute-done | bytes 65568 | tf_op jit(solution)/shard_map/ppermute | solution.py:62
  19.5 1.1 %collective-permute-start.12 = (f32[128,128]{1,0:T(8,128)S(1)}, f32[128,128]{1,0:T(8,128)S(1)}, u32[]{:S(2)}, u32[]{:S(2)}) collective-permute-start(f32[128,128]{1,0:T(8,128)S(1)} %add.52.p0), channel_id=1, source_target_pairs={{0,1},{1,0},{2,3},{3,2},{4,5},{5,4},{6,7},{7,6},{8,10},{9,11},{10,... | collective-permute-start | bytes 196616 | tf_op jit(solution)/shard_map/ppermute | solution.py:58
  20.5 2.2 %collective-permute-start.13 = (f32[128,128]{1,0:T(8,128)S(1)}, f32[128,128]{1,0:T(8,128)S(1)}, u32[]{:S(2)}, u32[]{:S(2)}) collective-permute-start(f32[128,128]{1,0:T(8,128)S(1)} %add.52.p0), channel_id=1, source_target_pairs={{0,2},{1,3},{2,0},{3,1},{4,6},{5,7},{6,4},{7,5},{8,9},{9,8},{10,11... | collective-permute-start | bytes 196616 | tf_op jit(solution)/shard_map/ppermute | solution.py:58
  23.1 1.2 %collective-permute-start.5 = (f32[128,128]{1,0:T(8,128)S(1)}, f32[128,128]{1,0:T(8,128)S(1)}, u32[]{:S(2)}, u32[]{:S(2)}) collective-permute-start(f32[128,128]{1,0:T(8,128)S(1)} %add.48.p0), channel_id=1, source_target_pairs={{0,1},{1,0},{2,3},{3,2},{4,5},{5,4},{6,7},{7,6},{8,10},{9,11},{10,... | collective-permute-start | bytes 196616 | tf_op jit(solution)/shard_map/ppermute | solution.py:58
  25.1 1.2 %collective-permute-start.6 = (f32[128,128]{1,0:T(8,128)S(1)}, f32[128,128]{1,0:T(8,128)S(1)}, u32[]{:S(2)}, u32[]{:S(2)}) collective-permute-start(f32[128,128]{1,0:T(8,128)S(1)} %add.48.p0), channel_id=1, source_target_pairs={{0,2},{1,3},{2,0},{3,1},{4,6},{5,7},{6,4},{7,5},{8,9},{9,8},{10,11... | collective-permute-start | bytes 196616 | tf_op jit(solution)/shard_map/ppermute | solution.py:58
  26.8 1.2 %collective-permute-done.4.p1 = f32[128,128]{1,0:T(8,128)S(1)} collective-permute-done((f32[128,128]{1,0:T(8,128)S(1)}, f32[128,128]{1,0:T(8,128)S(1)}, u32[]{:S(2)}, u32[]{:S(2)}) %collective-permute-start.4) | collective-permute-done | bytes 65568 | tf_op jit(solution)/shard_map/ppermute | solution.py:58
  28.0 1.3 %collective-permute-done.6.p3 = f32[128,128]{1,0:T(8,128)S(1)} collective-permute-done((f32[128,128]{1,0:T(8,128)S(1)}, f32[128,128]{1,0:T(8,128)S(1)}, u32[]{:S(2)}, u32[]{:S(2)}) %collective-permute-start.6) | collective-permute-done | bytes 65568 | tf_op jit(solution)/shard_map/ppermute | solution.py:58
  31.2 1.2 %collective-permute-start.19 = (f32[128,128]{1,0:T(8,128)S(1)}, f32[128,128]{1,0:T(8,128)S(1)}, u32[]{:S(2)}, u32[]{:S(2)}) collective-permute-start(f32[128,128]{1,0:T(8,128)S(1)} %add.55.gram), channel_id=1, source_target_pairs={{0,24},{1,25},{2,26},{3,27},{4,28},{5,29},{6,30},{7,31},{8,16},{9,... | collective-permute-start | bytes 196616 | tf_op jit(solution)/shard_map/ppermute | solution.py:74
  32.4 1.3 %collective-permute-start.17 = (f32[128,256]{1,0:T(8,128)S(1)}, f32[128,256]{1,0:T(8,128)S(1)}, u32[]{:S(2)}, u32[]{:S(2)}) collective-permute-start(f32[128,256]{1,0:T(8,128)S(1)} %add.53.rest), channel_id=1, source_target_pairs={{0,24},{1,25},{2,26},{3,27},{4,28},{5,29},{6,30},{7,31},{8,16},{9,... | collective-permute-start | bytes 393224 | tf_op jit(solution)/shard_map/ppermute | solution.py:74
  34.2 1.2 %collective-permute-done.19.came = f32[128,128]{1,0:T(8,128)S(1)} collective-permute-done((f32[128,128]{1,0:T(8,128)S(1)}, f32[128,128]{1,0:T(8,128)S(1)}, u32[]{:S(2)}, u32[]{:S(2)}) %collective-permute-start.19) | collective-permute-done | bytes 65568 | tf_op jit(solution)/shard_map/ppermute | solution.py:74
  35.4 2.9 %shard_map.71.inverse1 = f32[128,128]{1,0:T(8,128)S(1)} custom-call(f32[128,128]{1,0:T(8,128)S(1)} %add.55.gram, f32[128,128]{1,0:T(8,128)S(1)} %collective-permute-done.19.came), custom_call_target="tpu_custom_call" | custom-call | flops 4000000000 | tf_op jit(solution)/shard_map/pallas_call | solution.py:79
  38.4 3.5 %shard_map.72.inverse = f32[256,256]{1,0:T(8,128)S(1)} custom-call(f32[128,256]{1,0:T(8,128)S(1)} %add.53.rest, f32[128,256]{1,0:T(8,128)S(1)} %collective-permute-done.17.came, f32[128,128]{1,0:T(8,128)S(1)} %shard_map.71.inverse1), custom_call_target="tpu_custom_call" | custom-call | flops 4000000000 | tf_op jit(solution)/shard_map/pallas_call | solution.py:79
  42.3 1.5 %collective-permute-start.20 = (f32[1,256]{1,0:T(1,128)S(1)}, f32[1,256]{1,0:T(1,128)S(1)}, u32[]{:S(2)}, u32[]{:S(2)}) collective-permute-start(f32[1,256]{1,0:T(1,128)S(1)} %get-tuple-element.42), channel_id=1, source_target_pairs={{0,11},{1,10},{2,9},{3,8},{4,15},{5,14},{6,13},{7,12},{8,3},{9,2},... | collective-permute-start | bytes 3080 | tf_op jit(solution)/shard_map/ppermute | solution.py:74
  43.8 1.0 %collective-permute-start.21 = (f32[1,256]{1,0:T(1,128)S(1)}, f32[1,256]{1,0:T(1,128)S(1)}, u32[]{:S(2)}, u32[]{:S(2)}) collective-permute-start(f32[1,256]{1,0:T(1,128)S(1)} %get-tuple-element.42), channel_id=1, source_target_pairs={{0,9},{1,8},{2,11},{3,10},{4,13},{5,12},{6,15},{7,14},{8,1},{9,0},... | collective-permute-start | bytes 3080 | tf_op jit(solution)/shard_map/ppermute | solution.py:74
  44.8 1.1 %collective-permute-start.22 = (f32[1,256]{1,0:T(1,128)S(1)}, f32[1,256]{1,0:T(1,128)S(1)}, u32[]{:S(2)}, u32[]{:S(2)}) collective-permute-start(f32[1,256]{1,0:T(1,128)S(1)} %get-tuple-element.42), channel_id=1, source_target_pairs={{0,10},{1,11},{2,8},{3,9},{4,14},{5,15},{6,12},{7,13},{8,2},{9,3},... | collective-permute-start | bytes 3080 | tf_op jit(solution)/shard_map/ppermute | solution.py:74
  47.8 1.8 %collective-permute-start.23 = (f32[1,256]{1,0:T(1,128)S(1)}, f32[1,256]{1,0:T(1,128)S(1)}, u32[]{:S(2)}, u32[]{:S(2)}) collective-permute-start(f32[1,256]{1,0:T(1,128)S(1)} %add_add_fusion.2), channel_id=1, source_target_pairs={{0,12},{1,13},{2,14},{3,15},{4,8},{5,9},{6,10},{7,11},{8,4},{9,5},... | collective-permute-start | bytes 3080 | tf_op jit(solution)/shard_map/ppermute | solution.py:74
  49.5 1.1 %shard_map.76 = f32[112,512]{1,0:T(8,128)} custom-call(f32[112,512]{1,0:T(8,128)S(1)} %get-tuple-element.37.buf, f32[112,256]{1,0:T(8,128)S(1)} %get-tuple-element.41.right, f32[256,512]{1,0:T(8,128)S(1)} %get-tuple-element.43.ortho), custom_call_target="tpu_custom_call" | custom-call | flops 2000000000 | tf_op jit(solution)/shard_map/pallas_call | solution.py:79
  50.6 1.0 %collective-permute-done.23 = f32[1,256]{1,0:T(1,128)S(1)} collective-permute-done((f32[1,256]{1,0:T(1,128)S(1)}, f32[1,256]{1,0:T(1,128)S(1)}, u32[]{:S(2)}, u32[]{:S(2)}) %collective-permute-start.23) | collective-permute-done | bytes 1056 | tf_op jit(solution)/shard_map/ppermute | solution.py:74
  51.7 1.0 %shard_map.75 = (bf16[112,512]{1,0:T(8,128)(2,1)}, f32[112,256]{1,0:T(8,128)}) custom-call(bf16[112,512]{1,0:T(8,128)(2,1)S(1)} %copy-done, f32[112,256]{1,0:T(8,128)S(1)} %get-tuple-element.41.right, f32[1,256]{1,0:T(1,128)S(1)} %add.59.squares, bf16[256,512]{1,0:T(8,128)(2,1)S(1)} %get-tuple-element.45.high, bf16[256,512]{1,0:T(8,128)(2,1)S(1)} %get-tuple-element.46.mid), custom_call_target="tpu_custom_call" | custom-call | flops 1000000000 | tf_op jit(solution)/shard_map/pallas_call | solution.py:79
  (45 shorter events, 9.5 us)
Async XLA Ops:
  2.2 8.0 %collective-permute-start.7 = (f32[128,128]{1,0:T(8,128)S(1)}, f32[128,128]{1,0:T(8,128)S(1)}, u32[]{:S(2)}, u32[]{:S(2)}) collective-permute-start(f32[128,128]{1,0:T(8,128)S(1)} %get-tuple-element.31), channel_id=1, source_target_pairs={{0,3},{1,2},{2,1},{3,0},{4,7},{5,6},{6,5},{7,4},{8,11},{9,10},{10,... | collective-permute-start | bytes 196616 | tf_op jit(solution)/shard_map/ppermute | solution.py:58
  6.3 4.8 %collective-permute-start.8 = (f32[128,128]{1,0:T(8,128)S(1)}, f32[128,128]{1,0:T(8,128)S(1)}, u32[]{:S(2)}, u32[]{:S(2)}) collective-permute-start(f32[128,128]{1,0:T(8,128)S(1)} %get-tuple-element.32), channel_id=1, source_target_pairs={{0,1},{1,0},{2,3},{3,2},{4,5},{5,4},{6,7},{7,6},{8,10},{9,11},{10,... | collective-permute-start | bytes 196616 | tf_op jit(solution)/shard_map/ppermute | solution.py:58
  6.8 4.5 %collective-permute-start.9 = (f32[128,128]{1,0:T(8,128)S(1)}, f32[128,128]{1,0:T(8,128)S(1)}, u32[]{:S(2)}, u32[]{:S(2)}) collective-permute-start(f32[128,128]{1,0:T(8,128)S(1)} %get-tuple-element.33), channel_id=1, source_target_pairs={{0,2},{1,3},{2,0},{3,1},{4,6},{5,7},{6,4},{7,5},{8,9},{9,8},{10,11... | collective-permute-start | bytes 196616 | tf_op jit(solution)/shard_map/ppermute | solution.py:58
  6.9 7.1 %collective-permute-start = (f32[128,128]{1,0:T(8,128)S(1)}, f32[128,128]{1,0:T(8,128)S(1)}, u32[]{:S(2)}, u32[]{:S(2)}) collective-permute-start(f32[128,128]{1,0:T(8,128)S(1)} %get-tuple-element.27), channel_id=1, source_target_pairs={{0,3},{1,2},{2,1},{3,0},{4,7},{5,6},{6,5},{7,4},{8,11},{9,10},{10,... | collective-permute-start | bytes 196616 | tf_op jit(solution)/shard_map/ppermute | solution.py:58
  9.8 4.3 %collective-permute-start.1 = (f32[128,128]{1,0:T(8,128)S(1)}, f32[128,128]{1,0:T(8,128)S(1)}, u32[]{:S(2)}, u32[]{:S(2)}) collective-permute-start(f32[128,128]{1,0:T(8,128)S(1)} %get-tuple-element.28), channel_id=1, source_target_pairs={{0,1},{1,0},{2,3},{3,2},{4,5},{5,4},{6,7},{7,6},{8,10},{9,11},{10,... | collective-permute-start | bytes 196616 | tf_op jit(solution)/shard_map/ppermute | solution.py:58
  10.3 4.3 %collective-permute-start.2 = (f32[128,128]{1,0:T(8,128)S(1)}, f32[128,128]{1,0:T(8,128)S(1)}, u32[]{:S(2)}, u32[]{:S(2)}) collective-permute-start(f32[128,128]{1,0:T(8,128)S(1)} %get-tuple-element.29), channel_id=1, source_target_pairs={{0,2},{1,3},{2,0},{3,1},{4,6},{5,7},{6,4},{7,5},{8,9},{9,8},{10,11... | collective-permute-start | bytes 196616 | tf_op jit(solution)/shard_map/ppermute | solution.py:58
  11.3 7.8 %collective-permute-start.10 = (f32[128,128]{1,0:T(8,128)S(1)}, f32[128,128]{1,0:T(8,128)S(1)}, u32[]{:S(2)}, u32[]{:S(2)}) collective-permute-start(f32[128,128]{1,0:T(8,128)S(1)} %add_add_fusion), channel_id=1, source_target_pairs={{0,4},{1,5},{2,6},{3,7},{4,0},{5,1},{6,2},{7,3},{8,12},{9,13},{10,... | collective-permute-start | bytes 196616 | tf_op jit(solution)/shard_map/ppermute | solution.py:62
  14.6 8.2 %collective-permute-start.3 = (f32[128,128]{1,0:T(8,128)S(1)}, f32[128,128]{1,0:T(8,128)S(1)}, u32[]{:S(2)}, u32[]{:S(2)}) collective-permute-start(f32[128,128]{1,0:T(8,128)S(1)} %add_add_fusion.1), channel_id=1, source_target_pairs={{0,4},{1,5},{2,6},{3,7},{4,0},{5,1},{6,2},{7,3},{8,12},{9,13},{10,... | collective-permute-start | bytes 196616 | tf_op jit(solution)/shard_map/ppermute | solution.py:62
  19.2 5.9 %collective-permute-start.11 = (f32[128,128]{1,0:T(8,128)S(1)}, f32[128,128]{1,0:T(8,128)S(1)}, u32[]{:S(2)}, u32[]{:S(2)}) collective-permute-start(f32[128,128]{1,0:T(8,128)S(1)} %add.52.p0), channel_id=1, source_target_pairs={{0,3},{1,2},{2,1},{3,0},{4,7},{5,6},{6,5},{7,4},{8,11},{9,10},{10,... | collective-permute-start | bytes 196616 | tf_op jit(solution)/shard_map/ppermute | solution.py:58
  19.5 6.8 %collective-permute-start.12 = (f32[128,128]{1,0:T(8,128)S(1)}, f32[128,128]{1,0:T(8,128)S(1)}, u32[]{:S(2)}, u32[]{:S(2)}) collective-permute-start(f32[128,128]{1,0:T(8,128)S(1)} %add.52.p0), channel_id=1, source_target_pairs={{0,1},{1,0},{2,3},{3,2},{4,5},{5,4},{6,7},{7,6},{8,10},{9,11},{10,... | collective-permute-start | bytes 196616 | tf_op jit(solution)/shard_map/ppermute | solution.py:58
  20.5 5.8 %collective-permute-start.13 = (f32[128,128]{1,0:T(8,128)S(1)}, f32[128,128]{1,0:T(8,128)S(1)}, u32[]{:S(2)}, u32[]{:S(2)}) collective-permute-start(f32[128,128]{1,0:T(8,128)S(1)} %add.52.p0), channel_id=1, source_target_pairs={{0,2},{1,3},{2,0},{3,1},{4,6},{5,7},{6,4},{7,5},{8,9},{9,8},{10,11... | collective-permute-start | bytes 196616 | tf_op jit(solution)/shard_map/ppermute | solution.py:58
  22.7 5.3 %collective-permute-start.4 = (f32[128,128]{1,0:T(8,128)S(1)}, f32[128,128]{1,0:T(8,128)S(1)}, u32[]{:S(2)}, u32[]{:S(2)}) collective-permute-start(f32[128,128]{1,0:T(8,128)S(1)} %add.48.p0), channel_id=1, source_target_pairs={{0,3},{1,2},{2,1},{3,0},{4,7},{5,6},{6,5},{7,4},{8,11},{9,10},{10,... | collective-permute-start | bytes 196616 | tf_op jit(solution)/shard_map/ppermute | solution.py:58
  23.1 5.0 %collective-permute-start.5 = (f32[128,128]{1,0:T(8,128)S(1)}, f32[128,128]{1,0:T(8,128)S(1)}, u32[]{:S(2)}, u32[]{:S(2)}) collective-permute-start(f32[128,128]{1,0:T(8,128)S(1)} %add.48.p0), channel_id=1, source_target_pairs={{0,1},{1,0},{2,3},{3,2},{4,5},{5,4},{6,7},{7,6},{8,10},{9,11},{10,... | collective-permute-start | bytes 196616 | tf_op jit(solution)/shard_map/ppermute | solution.py:58
  25.1 4.3 %collective-permute-start.6 = (f32[128,128]{1,0:T(8,128)S(1)}, f32[128,128]{1,0:T(8,128)S(1)}, u32[]{:S(2)}, u32[]{:S(2)}) collective-permute-start(f32[128,128]{1,0:T(8,128)S(1)} %add.48.p0), channel_id=1, source_target_pairs={{0,2},{1,3},{2,0},{3,1},{4,6},{5,7},{6,4},{7,5},{8,9},{9,8},{10,11... | collective-permute-start | bytes 196616 | tf_op jit(solution)/shard_map/ppermute | solution.py:58
  26.7 4.5 %collective-permute-start.18 = (f32[128,128]{1,0:T(8,128)S(1)}, f32[128,128]{1,0:T(8,128)S(1)}, u32[]{:S(2)}, u32[]{:S(2)}) collective-permute-start(f32[128,128]{1,0:T(8,128)S(1)} %get-tuple-element.40), channel_id=1, source_target_pairs={{0,8},{8,0},{16,24},{24,16},{1,9},{9,1},{17,25},{25,17},{2,10},{10... | collective-permute-start | bytes 196616 | tf_op jit(solution)/shard_map/ppermute | solution.py:66
  29.9 2.5 %collective-permute-start.14 = (f32[128,256]{1,0:T(8,128)S(1)}, f32[128,256]{1,0:T(8,128)S(1)}, u32[]{:S(2)}, u32[]{:S(2)}) collective-permute-start(f32[128,256]{1,0:T(8,128)S(1)} %get-tuple-element.35), channel_id=1, source_target_pairs={{0,8},{8,0},{16,24},{24,16},{1,9},{9,1},{17,25},{25,17},{2,10},{10... | collective-permute-start | bytes 393224 | tf_op jit(solution)/shard_map/ppermute | solution.py:66
  30.6 1.8 %collective-permute-start.15 = (f32[112,256]{1,0:T(8,128)S(1)}, f32[112,256]{1,0:T(8,128)S(1)}, u32[]{:S(2)}, u32[]{:S(2)}) collective-permute-start(f32[112,256]{1,0:T(8,128)S(1)} %shard_map.70), channel_id=1, source_target_pairs={{0,8},{8,0},{16,24},{24,16},{1,9},{9,1},{17,25},{25,17},{2,10},{10... | collective-permute-start | bytes 344072 | tf_op jit(solution)/shard_map/ppermute | solution.py:66
  31.2 4.2 %collective-permute-start.19 = (f32[128,128]{1,0:T(8,128)S(1)}, f32[128,128]{1,0:T(8,128)S(1)}, u32[]{:S(2)}, u32[]{:S(2)}) collective-permute-start(f32[128,128]{1,0:T(8,128)S(1)} %add.55.gram), channel_id=1, source_target_pairs={{0,24},{1,25},{2,26},{3,27},{4,28},{5,29},{6,30},{7,31},{8,16},{9,... | collective-permute-start | bytes 196616 | tf_op jit(solution)/shard_map/ppermute | solution.py:74
  32.4 5.9 %collective-permute-start.17 = (f32[128,256]{1,0:T(8,128)S(1)}, f32[128,256]{1,0:T(8,128)S(1)}, u32[]{:S(2)}, u32[]{:S(2)}) collective-permute-start(f32[128,256]{1,0:T(8,128)S(1)} %add.53.rest), channel_id=1, source_target_pairs={{0,24},{1,25},{2,26},{3,27},{4,28},{5,29},{6,30},{7,31},{8,16},{9,... | collective-permute-start | bytes 393224 | tf_op jit(solution)/shard_map/ppermute | solution.py:74
  33.7 8.2 %collective-permute-start.16 = (f32[112,256]{1,0:T(8,128)S(1)}, f32[112,256]{1,0:T(8,128)S(1)}, u32[]{:S(2)}, u32[]{:S(2)}) collective-permute-start(f32[112,256]{1,0:T(8,128)S(1)} %add.54.cross), channel_id=1, source_target_pairs={{0,24},{1,25},{2,26},{3,27},{4,28},{5,29},{6,30},{7,31},{8,16},{9,... | collective-permute-start | bytes 344072 | tf_op jit(solution)/shard_map/ppermute | solution.py:74
  42.3 4.2 %collective-permute-start.20 = (f32[1,256]{1,0:T(1,128)S(1)}, f32[1,256]{1,0:T(1,128)S(1)}, u32[]{:S(2)}, u32[]{:S(2)}) collective-permute-start(f32[1,256]{1,0:T(1,128)S(1)} %get-tuple-element.42), channel_id=1, source_target_pairs={{0,11},{1,10},{2,9},{3,8},{4,15},{5,14},{6,13},{7,12},{8,3},{9,2},... | collective-permute-start | bytes 3080 | tf_op jit(solution)/shard_map/ppermute | solution.py:74
  43.8 3.0 %collective-permute-start.21 = (f32[1,256]{1,0:T(1,128)S(1)}, f32[1,256]{1,0:T(1,128)S(1)}, u32[]{:S(2)}, u32[]{:S(2)}) collective-permute-start(f32[1,256]{1,0:T(1,128)S(1)} %get-tuple-element.42), channel_id=1, source_target_pairs={{0,9},{1,8},{2,11},{3,10},{4,13},{5,12},{6,15},{7,14},{8,1},{9,0},... | collective-permute-start | bytes 3080 | tf_op jit(solution)/shard_map/ppermute | solution.py:74
  44.8 3.0 %collective-permute-start.22 = (f32[1,256]{1,0:T(1,128)S(1)}, f32[1,256]{1,0:T(1,128)S(1)}, u32[]{:S(2)}, u32[]{:S(2)}) collective-permute-start(f32[1,256]{1,0:T(1,128)S(1)} %get-tuple-element.42), channel_id=1, source_target_pairs={{0,10},{1,11},{2,8},{3,9},{4,14},{5,15},{6,12},{7,13},{8,2},{9,3},... | collective-permute-start | bytes 3080 | tf_op jit(solution)/shard_map/ppermute | solution.py:74
  47.8 3.9 %collective-permute-start.23 = (f32[1,256]{1,0:T(1,128)S(1)}, f32[1,256]{1,0:T(1,128)S(1)}, u32[]{:S(2)}, u32[]{:S(2)}) collective-permute-start(f32[1,256]{1,0:T(1,128)S(1)} %add_add_fusion.2), channel_id=1, source_target_pairs={{0,12},{1,13},{2,14},{3,15},{4,8},{5,9},{6,10},{7,11},{8,4},{9,5},... | collective-permute-start | bytes 3080 | tf_op jit(solution)/shard_map/ppermute | solution.py:74
  (1 other events, 2.1 us)

commit v5 on v4

--- a/solution.py
+++ b/solution.py
@@ -41,21 +41,16 @@
     return size.bit_length() - 1
 
 
-def partner(core, j):
-    return ((0, 3, 1, 2), (0, 3, 2, 1))[core][j]
+def partner(j):
+    return (0, 3, 1, 2)[j]
 
 
 def block_of(j):
-    mine, core = lax.axis_index("tensor") % 4, lax.axis_index("fsdp") % 2
-    return jnp.where(core == 0, mine ^ partner(0, j), mine ^ partner(1, j))
-
-
-def to_partner(x, j, fsdp, tensor):
-    pairs = []
-    for f in range(fsdp):
-        for t in range(tensor):
-            pairs.append((f * tensor + t, f * tensor + (t ^ partner(f % 2, j))))
-    return lax.ppermute(x, ("fsdp", "tensor"), pairs)
+    return (lax.axis_index("tensor") % 4) ^ partner(j)
+
+
+def to_partner(x, j, tensor):
+    return lax.ppermute(x, "tensor", [(t, t ^ partner(j)) for t in range(tensor)])
 
 
 def flip_tensor(x, bit, tensor):
@@ -262,11 +257,11 @@
     )(*[pltpu.with_memory_space_constraint(x, pltpu.HBM) for x in (momentum, grad, q_prev)])
     totals = []
     for mine in (parts[:4], parts[4:]):
-        came = [to_partner(mine[j], j, fsdp, tensor) for j in (1, 2, 3)]
+        came = [to_partner(mine[j], j, tensor) for j in (1, 2, 3)]
         totals.append(mine[0] + came[0] + came[1] + came[2])
     for bit in range(2, bits_of(tensor)):
         totals = [x + flip_tensor(x, bit, tensor) for x in totals]
-    pieces = [[x] + [to_partner(x, j, fsdp, tensor) for j in (1, 2, 3)] for x in totals]
+    pieces = [[x] + [to_partner(x, j, tensor) for j in (1, 2, 3)] for x in totals]
     upper, first = call(first_gram_kernel, [((half, rows), f32), ((half, half), f32)], pieces[0])
     lower, second = call(second_gram_kernel, [((half, rows), f32), ((half, rank), f32)], [*pieces[1], upper])
     (third,) = call(cross_kernel, [((cols, rank), f32)], [upper, lower, buf])

time: 53 us -> 52.4 us (0.989)
  waiting for transfers between devices: 9.16 us -> 8.22 us
    ppermute x12, waiting for transfers between devices: 4.37 us -> 3.28 us  [to_partner(): lax.ppermute(x, 'tensor', [(t, t ^ partner(j)) for t in range(tensor)])]
    ppermute x12, starting transfers between devices: 14.9 us -> 15.5 us  [to_partner(): lax.ppermute(x, 'tensor', [(t, t ^ partner(j)) for t in range(tensor)])]
where the time goes in v5:
time: 52.4 us; the launch traced here: 52.1 us
  starting transfers between devices  30.3 us (58%)
  Pallas kernels  12.7 us (24%)
  waiting for transfers between devices  8.22 us (16%)
  between operations  0.79 us (2%)
    ppermute x12, starting transfers between devices, to_partner(): lax.ppermute(x, 'tensor', [(t, t ^ partner(j)) for t in range(tensor)])  15.5 us
    pallas_call x9, Pallas kernels, call(): pl.pallas_call(body, out_shape=shapes, in_specs=[pl.BlockSpec(memory_spac...  11.1 us
    ppermute x7, starting transfers between devices, flip_across(): return lax.ppermute(x, ('fsdp', 'tensor'), pairs)  8.46 us
    ppermute x2, starting transfers between devices, flip_tensor(): return lax.ppermute(x, 'tensor', [(t, t ^ 1 << bit) for t in range(tensor)])  5.61 us
    ppermute x7, waiting for transfers between devices, flip_across(): return lax.ppermute(x, ('fsdp', 'tensor'), pairs)  3.88 us
    ppermute x12, waiting for transfers between devices, to_partner(): lax.ppermute(x, 'tensor', [(t, t ^ partner(j)) for t in range(tensor)])  3.28 us
    pallas_call x1, Pallas kernels, per_device(): pl.pallas_call(power_kernel, out_shape=[jax.ShapeDtypeStruct(*x) for x in...  1.58 us
    ppermute x2, waiting for transfers between devices, flip_tensor(): return lax.ppermute(x, 'tensor', [(t, t ^ 1 << bit) for t in range(tensor)])  1.05 us
  transfers between devices with their start and end apart: 24, of which 11 were waited for; matrix products, arithmetic and copies ran while one was open for 0% of the time, Pallas kernels for 19%

profile of v5, /device:TPU:0, one launch (start us, length us, event | category | flops | bytes accessed | tf_op | source)
XLA Modules:
  0.0 52.1 jit_solution(11003708792547301062)
XLA Ops:
  0.6 1.6 %shard_map.67 = (f32[112,512]{1,0:T(8,128)S(1)}, f32[128,128]{1,0:T(8,128)S(1)}, f32[128,128]{1,0:T(8,128)S(1)}, f32[128,128]{1,0:T(8,128)S(1)}, f32[128,128]{1,...) custom-call(f32[112,512]{1,0:T(8,128)} %mom_in.1, ...), custom_call_target="tpu_custom_call" | custom-call | tf_op jit(solution)/shard_map/pallas_call | solution.py:244
  2.2 4.0 %collective-permute-start.7 = (f32[128,128]{1,0:T(8,128)S(1)}, f32[128,128]{1,0:T(8,128)S(1)}, u32[]{:S(2)}, u32[]{:S(2)}) collective-permute-start(f32[128,128]{1,0:T(8,128)S(1)} %get-tuple-element.31), channel_id=1, source_target_pairs={{0,3},{1,2},{2,1},{3,0},{4,7},{5,6},{6,5},{7,4},{8,11},{9,10},{10,... | collective-permute-start | bytes 196616 | tf_op jit(solution)/shard_map/ppermute | solution.py:53
  6.9 2.8 %collective-permute-start = (f32[128,128]{1,0:T(8,128)S(1)}, f32[128,128]{1,0:T(8,128)S(1)}, u32[]{:S(2)}, u32[]{:S(2)}) collective-permute-start(f32[128,128]{1,0:T(8,128)S(1)} %get-tuple-element.27), channel_id=1, source_target_pairs={{0,3},{1,2},{2,1},{3,0},{4,7},{5,6},{6,5},{7,4},{8,11},{9,10},{10,... | collective-permute-start | bytes 196616 | tf_op jit(solution)/shard_map/ppermute | solution.py:53
  11.4 2.6 %collective-permute-start.10 = (f32[128,128]{1,0:T(8,128)S(1)}, f32[128,128]{1,0:T(8,128)S(1)}, u32[]{:S(2)}, u32[]{:S(2)}) collective-permute-start(f32[128,128]{1,0:T(8,128)S(1)} %add_add_fusion), channel_id=1, source_target_pairs={{0,4},{1,5},{2,6},{3,7},{4,0},{5,1},{6,2},{7,3},{8,12},{9,13},{10,... | collective-permute-start | bytes 196616 | tf_op jit(solution)/shard_map/ppermute | solution.py:57
  14.6 3.0 %collective-permute-start.3 = (f32[128,128]{1,0:T(8,128)S(1)}, f32[128,128]{1,0:T(8,128)S(1)}, u32[]{:S(2)}, u32[]{:S(2)}) collective-permute-start(f32[128,128]{1,0:T(8,128)S(1)} %add_add_fusion.1), channel_id=1, source_target_pairs={{0,4},{1,5},{2,6},{3,7},{4,0},{5,1},{6,2},{7,3},{8,12},{9,13},{10,... | collective-permute-start | bytes 196616 | tf_op jit(solution)/shard_map/ppermute | solution.py:57
  17.5 1.0 %collective-permute-done.10 = f32[128,128]{1,0:T(8,128)S(1)} collective-permute-done((f32[128,128]{1,0:T(8,128)S(1)}, f32[128,128]{1,0:T(8,128)S(1)}, u32[]{:S(2)}, u32[]{:S(2)}) %collective-permute-start.10) | collective-permute-done | bytes 65568 | tf_op jit(solution)/shard_map/ppermute | solution.py:57
  18.6 1.1 %collective-permute-start.11 = (f32[128,128]{1,0:T(8,128)S(1)}, f32[128,128]{1,0:T(8,128)S(1)}, u32[]{:S(2)}, u32[]{:S(2)}) collective-permute-start(f32[128,128]{1,0:T(8,128)S(1)} %add.52.p0), channel_id=1, source_target_pairs={{0,3},{1,2},{2,1},{3,0},{4,7},{5,6},{6,5},{7,4},{8,11},{9,10},{10,... | collective-permute-start | bytes 196616 | tf_op jit(solution)/shard_map/ppermute | solution.py:53
  20.1 2.1 %collective-permute-start.13 = (f32[128,128]{1,0:T(8,128)S(1)}, f32[128,128]{1,0:T(8,128)S(1)}, u32[]{:S(2)}, u32[]{:S(2)}) collective-permute-start(f32[128,128]{1,0:T(8,128)S(1)} %add.52.p0), channel_id=1, source_target_pairs={{0,2},{1,3},{2,0},{3,1},{4,6},{5,7},{6,4},{7,5},{8,10},{9,11},{10,... | collective-permute-start | bytes 196616 | tf_op jit(solution)/shard_map/ppermute | solution.py:53
  22.2 1.1 %collective-permute-start.4 = (f32[128,128]{1,0:T(8,128)S(1)}, f32[128,128]{1,0:T(8,128)S(1)}, u32[]{:S(2)}, u32[]{:S(2)}) collective-permute-start(f32[128,128]{1,0:T(8,128)S(1)} %add.48.p0), channel_id=1, source_target_pairs={{0,3},{1,2},{2,1},{3,0},{4,7},{5,6},{6,5},{7,4},{8,11},{9,10},{10,... | collective-permute-start | bytes 196616 | tf_op jit(solution)/shard_map/ppermute | solution.py:53
  24.0 1.7 %collective-permute-start.6 = (f32[128,128]{1,0:T(8,128)S(1)}, f32[128,128]{1,0:T(8,128)S(1)}, u32[]{:S(2)}, u32[]{:S(2)}) collective-permute-start(f32[128,128]{1,0:T(8,128)S(1)} %add.48.p0), channel_id=1, source_target_pairs={{0,2},{1,3},{2,0},{3,1},{4,6},{5,7},{6,4},{7,5},{8,10},{9,11},{10,... | collective-permute-start | bytes 196616 | tf_op jit(solution)/shard_map/ppermute | solution.py:53
  26.2 1.2 %collective-permute-done.4.p1 = f32[128,128]{1,0:T(8,128)S(1)} collective-permute-done((f32[128,128]{1,0:T(8,128)S(1)}, f32[128,128]{1,0:T(8,128)S(1)}, u32[]{:S(2)}, u32[]{:S(2)}) %collective-permute-start.4) | collective-permute-done | bytes 65568 | tf_op jit(solution)/shard_map/ppermute | solution.py:53
  30.1 1.1 %collective-permute-start.19 = (f32[128,128]{1,0:T(8,128)S(1)}, f32[128,128]{1,0:T(8,128)S(1)}, u32[]{:S(2)}, u32[]{:S(2)}) collective-permute-start(f32[128,128]{1,0:T(8,128)S(1)} %add.55.gram), channel_id=1, source_target_pairs={{0,24},{1,25},{2,26},{3,27},{4,28},{5,29},{6,30},{7,31},{8,16},{9,... | collective-permute-start | bytes 196616 | tf_op jit(solution)/shard_map/ppermute | solution.py:69
  31.3 1.3 %collective-permute-start.17 = (f32[128,256]{1,0:T(8,128)S(1)}, f32[128,256]{1,0:T(8,128)S(1)}, u32[]{:S(2)}, u32[]{:S(2)}) collective-permute-start(f32[128,256]{1,0:T(8,128)S(1)} %add.53.rest), channel_id=1, source_target_pairs={{0,24},{1,25},{2,26},{3,27},{4,28},{5,29},{6,30},{7,31},{8,16},{9,... | collective-permute-start | bytes 393224 | tf_op jit(solution)/shard_map/ppermute | solution.py:69
  33.1 1.2 %collective-permute-done.19.came = f32[128,128]{1,0:T(8,128)S(1)} collective-permute-done((f32[128,128]{1,0:T(8,128)S(1)}, f32[128,128]{1,0:T(8,128)S(1)}, u32[]{:S(2)}, u32[]{:S(2)}) %collective-permute-start.19) | collective-permute-done | bytes 65568 | tf_op jit(solution)/shard_map/ppermute | solution.py:69
  34.3 2.9 %shard_map.71.inverse1 = f32[128,128]{1,0:T(8,128)S(1)} custom-call(f32[128,128]{1,0:T(8,128)S(1)} %add.55.gram, f32[128,128]{1,0:T(8,128)S(1)} %collective-permute-done.19.came), custom_call_target="tpu_custom_call" | custom-call | flops 4000000000 | tf_op jit(solution)/shard_map/pallas_call | solution.py:74
  37.3 3.5 %shard_map.72.inverse = f32[256,256]{1,0:T(8,128)S(1)} custom-call(f32[128,256]{1,0:T(8,128)S(1)} %add.53.rest, f32[128,256]{1,0:T(8,128)S(1)} %collective-permute-done.17.came, f32[128,128]{1,0:T(8,128)S(1)} %shard_map.71.inverse1), custom_call_target="tpu_custom_call" | custom-call | flops 4000000000 | tf_op jit(solution)/shard_map/pallas_call | solution.py:74
  41.2 2.3 %collective-permute-start.20 = (f32[1,256]{1,0:T(1,128)S(1)}, f32[1,256]{1,0:T(1,128)S(1)}, u32[]{:S(2)}, u32[]{:S(2)}) collective-permute-start(f32[1,256]{1,0:T(1,128)S(1)} %get-tuple-element.42), channel_id=1, source_target_pairs={{0,11},{1,10},{2,9},{3,8},{4,15},{5,14},{6,13},{7,12},{8,3},{9,2},... | collective-permute-start | bytes 3080 | tf_op jit(solution)/shard_map/ppermute | solution.py:69
  43.5 0.7 %collective-permute-start.21 = (f32[1,256]{1,0:T(1,128)S(1)}, f32[1,256]{1,0:T(1,128)S(1)}, u32[]{:S(2)}, u32[]{:S(2)}) collective-permute-start(f32[1,256]{1,0:T(1,128)S(1)} %get-tuple-element.42), channel_id=1, source_target_pairs={{0,9},{1,8},{2,11},{3,10},{4,13},{5,12},{6,15},{7,14},{8,1},{9,0},... | collective-permute-start | bytes 3080 | tf_op jit(solution)/shard_map/ppermute | solution.py:69
  45.3 1.2 %collective-permute-done.21 = f32[1,256]{1,0:T(1,128)S(1)} collective-permute-done((f32[1,256]{1,0:T(1,128)S(1)}, f32[1,256]{1,0:T(1,128)S(1)}, u32[]{:S(2)}, u32[]{:S(2)}) %collective-permute-start.21) | collective-permute-done | bytes 1056 | tf_op jit(solution)/shard_map/ppermute | solution.py:69
  46.5 0.7 %collective-permute-done.22 = f32[1,256]{1,0:T(1,128)S(1)} collective-permute-done((f32[1,256]{1,0:T(1,128)S(1)}, f32[1,256]{1,0:T(1,128)S(1)}, u32[]{:S(2)}, u32[]{:S(2)}) %collective-permute-start.22) | collective-permute-done | bytes 1056 | tf_op jit(solution)/shard_map/ppermute | solution.py:69
  47.2 2.0 %collective-permute-start.23 = (f32[1,256]{1,0:T(1,128)S(1)}, f32[1,256]{1,0:T(1,128)S(1)}, u32[]{:S(2)}, u32[]{:S(2)}) collective-permute-start(f32[1,256]{1,0:T(1,128)S(1)} %add_add_fusion.2), channel_id=1, source_target_pairs={{0,12},{1,13},{2,14},{3,15},{4,8},{5,9},{6,10},{7,11},{8,4},{9,5},... | collective-permute-start | bytes 3080 | tf_op jit(solution)/shard_map/ppermute | solution.py:69
  49.2 1.1 %shard_map.76 = f32[112,512]{1,0:T(8,128)} custom-call(f32[112,512]{1,0:T(8,128)S(1)} %get-tuple-element.37.buf, f32[112,256]{1,0:T(8,128)S(1)} %get-tuple-element.41.right, f32[256,512]{1,0:T(8,128)S(1)} %get-tuple-element.43.ortho), custom_call_target="tpu_custom_call" | custom-call | flops 2000000000 | tf_op jit(solution)/shard_map/pallas_call | solution.py:74
  50.3 0.8 %collective-permute-done.23 = f32[1,256]{1,0:T(1,128)S(1)} collective-permute-done((f32[1,256]{1,0:T(1,128)S(1)}, f32[1,256]{1,0:T(1,128)S(1)}, u32[]{:S(2)}, u32[]{:S(2)}) %collective-permute-start.23) | collective-permute-done | bytes 1056 | tf_op jit(solution)/shard_map/ppermute | solution.py:69
  51.1 1.0 %shard_map.75 = (bf16[112,512]{1,0:T(8,128)(2,1)}, f32[112,256]{1,0:T(8,128)}) custom-call(bf16[112,512]{1,0:T(8,128)(2,1)S(1)} %copy-done, f32[112,256]{1,0:T(8,128)S(1)} %get-tuple-element.41.right, f32[1,256]{1,0:T(1,128)S(1)} %add.59.squares, bf16[256,512]{1,0:T(8,128)(2,1)S(1)} %get-tuple-element.45.high, bf16[256,512]{1,0:T(8,128)(2,1)S(1)} %get-tuple-element.46.mid), custom_call_target="tpu_custom_call" | custom-call | flops 1000000000 | tf_op jit(solution)/shard_map/pallas_call | solution.py:74
  (45 shorter events, 9.2 us)
Async XLA Ops:
  2.2 8.0 %collective-permute-start.7 = (f32[128,128]{1,0:T(8,128)S(1)}, f32[128,128]{1,0:T(8,128)S(1)}, u32[]{:S(2)}, u32[]{:S(2)}) collective-permute-start(f32[128,128]{1,0:T(8,128)S(1)} %get-tuple-element.31), channel_id=1, source_target_pairs={{0,3},{1,2},{2,1},{3,0},{4,7},{5,6},{6,5},{7,4},{8,11},{9,10},{10,... | collective-permute-start | bytes 196616 | tf_op jit(solution)/shard_map/ppermute | solution.py:53
  6.3 5.1 %collective-permute-start.8 = (f32[128,128]{1,0:T(8,128)S(1)}, f32[128,128]{1,0:T(8,128)S(1)}, u32[]{:S(2)}, u32[]{:S(2)}) collective-permute-start(f32[128,128]{1,0:T(8,128)S(1)} %get-tuple-element.32), channel_id=1, source_target_pairs={{0,1},{1,0},{2,3},{3,2},{4,5},{5,4},{6,7},{7,6},{8,9},{9,8},{10,11... | collective-permute-start | bytes 196616 | tf_op jit(solution)/shard_map/ppermute | solution.py:53
  6.8 4.6 %collective-permute-start.9 = (f32[128,128]{1,0:T(8,128)S(1)}, f32[128,128]{1,0:T(8,128)S(1)}, u32[]{:S(2)}, u32[]{:S(2)}) collective-permute-start(f32[128,128]{1,0:T(8,128)S(1)} %get-tuple-element.33), channel_id=1, source_target_pairs={{0,2},{1,3},{2,0},{3,1},{4,6},{5,7},{6,4},{7,5},{8,10},{9,11},{10,... | collective-permute-start | bytes 196616 | tf_op jit(solution)/shard_map/ppermute | solution.py:53
  6.9 7.1 %collective-permute-start = (f32[128,128]{1,0:T(8,128)S(1)}, f32[128,128]{1,0:T(8,128)S(1)}, u32[]{:S(2)}, u32[]{:S(2)}) collective-permute-start(f32[128,128]{1,0:T(8,128)S(1)} %get-tuple-element.27), channel_id=1, source_target_pairs={{0,3},{1,2},{2,1},{3,0},{4,7},{5,6},{6,5},{7,4},{8,11},{9,10},{10,... | collective-permute-start | bytes 196616 | tf_op jit(solution)/shard_map/ppermute | solution.py:53
  9.8 4.3 %collective-permute-start.1 = (f32[128,128]{1,0:T(8,128)S(1)}, f32[128,128]{1,0:T(8,128)S(1)}, u32[]{:S(2)}, u32[]{:S(2)}) collective-permute-start(f32[128,128]{1,0:T(8,128)S(1)} %get-tuple-element.28), channel_id=1, source_target_pairs={{0,1},{1,0},{2,3},{3,2},{4,5},{5,4},{6,7},{7,6},{8,9},{9,8},{10,11... | collective-permute-start | bytes 196616 | tf_op jit(solution)/shard_map/ppermute | solution.py:53
  10.3 4.3 %collective-permute-start.2 = (f32[128,128]{1,0:T(8,128)S(1)}, f32[128,128]{1,0:T(8,128)S(1)}, u32[]{:S(2)}, u32[]{:S(2)}) collective-permute-start(f32[128,128]{1,0:T(8,128)S(1)} %get-tuple-element.29), channel_id=1, source_target_pairs={{0,2},{1,3},{2,0},{3,1},{4,6},{5,7},{6,4},{7,5},{8,10},{9,11},{10,... | collective-permute-start | bytes 196616 | tf_op jit(solution)/shard_map/ppermute | solution.py:53
  11.4 7.2 %collective-permute-start.10 = (f32[128,128]{1,0:T(8,128)S(1)}, f32[128,128]{1,0:T(8,128)S(1)}, u32[]{:S(2)}, u32[]{:S(2)}) collective-permute-start(f32[128,128]{1,0:T(8,128)S(1)} %add_add_fusion), channel_id=1, source_target_pairs={{0,4},{1,5},{2,6},{3,7},{4,0},{5,1},{6,2},{7,3},{8,12},{9,13},{10,... | collective-permute-start | bytes 196616 | tf_op jit(solution)/shard_map/ppermute | solution.py:57
  14.6 7.6 %collective-permute-start.3 = (f32[128,128]{1,0:T(8,128)S(1)}, f32[128,128]{1,0:T(8,128)S(1)}, u32[]{:S(2)}, u32[]{:S(2)}) collective-permute-start(f32[128,128]{1,0:T(8,128)S(1)} %add_add_fusion.1), channel_id=1, source_target_pairs={{0,4},{1,5},{2,6},{3,7},{4,0},{5,1},{6,2},{7,3},{8,12},{9,13},{10,... | collective-permute-start | bytes 196616 | tf_op jit(solution)/shard_map/ppermute | solution.py:57
  18.6 5.4 %collective-permute-start.11 = (f32[128,128]{1,0:T(8,128)S(1)}, f32[128,128]{1,0:T(8,128)S(1)}, u32[]{:S(2)}, u32[]{:S(2)}) collective-permute-start(f32[128,128]{1,0:T(8,128)S(1)} %add.52.p0), channel_id=1, source_target_pairs={{0,3},{1,2},{2,1},{3,0},{4,7},{5,6},{6,5},{7,4},{8,11},{9,10},{10,... | collective-permute-start | bytes 196616 | tf_op jit(solution)/shard_map/ppermute | solution.py:53
  19.7 6.1 %collective-permute-start.12 = (f32[128,128]{1,0:T(8,128)S(1)}, f32[128,128]{1,0:T(8,128)S(1)}, u32[]{:S(2)}, u32[]{:S(2)}) collective-permute-start(f32[128,128]{1,0:T(8,128)S(1)} %add.52.p0), channel_id=1, source_target_pairs={{0,1},{1,0},{2,3},{3,2},{4,5},{5,4},{6,7},{7,6},{8,9},{9,8},{10,11... | collective-permute-start | bytes 196616 | tf_op jit(solution)/shard_map/ppermute | solution.py:53
  20.1 5.7 %collective-permute-start.13 = (f32[128,128]{1,0:T(8,128)S(1)}, f32[128,128]{1,0:T(8,128)S(1)}, u32[]{:S(2)}, u32[]{:S(2)}) collective-permute-start(f32[128,128]{1,0:T(8,128)S(1)} %add.52.p0), channel_id=1, source_target_pairs={{0,2},{1,3},{2,0},{3,1},{4,6},{5,7},{6,4},{7,5},{8,10},{9,11},{10,... | collective-permute-start | bytes 196616 | tf_op jit(solution)/shard_map/ppermute | solution.py:53
  22.2 5.3 %collective-permute-start.4 = (f32[128,128]{1,0:T(8,128)S(1)}, f32[128,128]{1,0:T(8,128)S(1)}, u32[]{:S(2)}, u32[]{:S(2)}) collective-permute-start(f32[128,128]{1,0:T(8,128)S(1)} %add.48.p0), channel_id=1, source_target_pairs={{0,3},{1,2},{2,1},{3,0},{4,7},{5,6},{6,5},{7,4},{8,11},{9,10},{10,... | collective-permute-start | bytes 196616 | tf_op jit(solution)/shard_map/ppermute | solution.py:53
  23.2 4.9 %collective-permute-start.5 = (f32[128,128]{1,0:T(8,128)S(1)}, f32[128,128]{1,0:T(8,128)S(1)}, u32[]{:S(2)}, u32[]{:S(2)}) collective-permute-start(f32[128,128]{1,0:T(8,128)S(1)} %add.48.p0), channel_id=1, source_target_pairs={{0,1},{1,0},{2,3},{3,2},{4,5},{5,4},{6,7},{7,6},{8,9},{9,8},{10,11... | collective-permute-start | bytes 196616 | tf_op jit(solution)/shard_map/ppermute | solution.py:53
  24.0 4.3 %collective-permute-start.6 = (f32[128,128]{1,0:T(8,128)S(1)}, f32[128,128]{1,0:T(8,128)S(1)}, u32[]{:S(2)}, u32[]{:S(2)}) collective-permute-start(f32[128,128]{1,0:T(8,128)S(1)} %add.48.p0), channel_id=1, source_target_pairs={{0,2},{1,3},{2,0},{3,1},{4,6},{5,7},{6,4},{7,5},{8,10},{9,11},{10,... | collective-permute-start | bytes 196616 | tf_op jit(solution)/shard_map/ppermute | solution.py:53
  26.1 3.9 %collective-permute-start.18 = (f32[128,128]{1,0:T(8,128)S(1)}, f32[128,128]{1,0:T(8,128)S(1)}, u32[]{:S(2)}, u32[]{:S(2)}) collective-permute-start(f32[128,128]{1,0:T(8,128)S(1)} %get-tuple-element.40), channel_id=1, source_target_pairs={{0,8},{8,0},{16,24},{24,16},{1,9},{9,1},{17,25},{25,17},{2,10},{10... | collective-permute-start | bytes 196616 | tf_op jit(solution)/shard_map/ppermute | solution.py:61
  28.8 2.4 %collective-permute-start.14 = (f32[128,256]{1,0:T(8,128)S(1)}, f32[128,256]{1,0:T(8,128)S(1)}, u32[]{:S(2)}, u32[]{:S(2)}) collective-permute-start(f32[128,256]{1,0:T(8,128)S(1)} %get-tuple-element.35), channel_id=1, source_target_pairs={{0,8},{8,0},{16,24},{24,16},{1,9},{9,1},{17,25},{25,17},{2,10},{10... | collective-permute-start | bytes 393224 | tf_op jit(solution)/shard_map/ppermute | solution.py:61
  29.5 1.7 %collective-permute-start.15 = (f32[112,256]{1,0:T(8,128)S(1)}, f32[112,256]{1,0:T(8,128)S(1)}, u32[]{:S(2)}, u32[]{:S(2)}) collective-permute-start(f32[112,256]{1,0:T(8,128)S(1)} %shard_map.70), channel_id=1, source_target_pairs={{0,8},{8,0},{16,24},{24,16},{1,9},{9,1},{17,25},{25,17},{2,10},{10... | collective-permute-start | bytes 344072 | tf_op jit(solution)/shard_map/ppermute | solution.py:61
  30.1 4.2 %collective-permute-start.19 = (f32[128,128]{1,0:T(8,128)S(1)}, f32[128,128]{1,0:T(8,128)S(1)}, u32[]{:S(2)}, u32[]{:S(2)}) collective-permute-start(f32[128,128]{1,0:T(8,128)S(1)} %add.55.gram), channel_id=1, source_target_pairs={{0,24},{1,25},{2,26},{3,27},{4,28},{5,29},{6,30},{7,31},{8,16},{9,... | collective-permute-start | bytes 196616 | tf_op jit(solution)/shard_map/ppermute | solution.py:69
  31.3 6.0 %collective-permute-start.17 = (f32[128,256]{1,0:T(8,128)S(1)}, f32[128,256]{1,0:T(8,128)S(1)}, u32[]{:S(2)}, u32[]{:S(2)}) collective-permute-start(f32[128,256]{1,0:T(8,128)S(1)} %add.53.rest), channel_id=1, source_target_pairs={{0,24},{1,25},{2,26},{3,27},{4,28},{5,29},{6,30},{7,31},{8,16},{9,... | collective-permute-start | bytes 393224 | tf_op jit(solution)/shard_map/ppermute | solution.py:69
  32.6 8.2 %collective-permute-start.16 = (f32[112,256]{1,0:T(8,128)S(1)}, f32[112,256]{1,0:T(8,128)S(1)}, u32[]{:S(2)}, u32[]{:S(2)}) collective-permute-start(f32[112,256]{1,0:T(8,128)S(1)} %add.54.cross), channel_id=1, source_target_pairs={{0,24},{1,25},{2,26},{3,27},{4,28},{5,29},{6,30},{7,31},{8,16},{9,... | collective-permute-start | bytes 344072 | tf_op jit(solution)/shard_map/ppermute | solution.py:69
  41.2 4.1 %collective-permute-start.20 = (f32[1,256]{1,0:T(1,128)S(1)}, f32[1,256]{1,0:T(1,128)S(1)}, u32[]{:S(2)}, u32[]{:S(2)}) collective-permute-start(f32[1,256]{1,0:T(1,128)S(1)} %get-tuple-element.42), channel_id=1, source_target_pairs={{0,11},{1,10},{2,9},{3,8},{4,15},{5,14},{6,13},{7,12},{8,3},{9,2},... | collective-permute-start | bytes 3080 | tf_op jit(solution)/shard_map/ppermute | solution.py:69
  43.5 3.0 %collective-permute-start.21 = (f32[1,256]{1,0:T(1,128)S(1)}, f32[1,256]{1,0:T(1,128)S(1)}, u32[]{:S(2)}, u32[]{:S(2)}) collective-permute-start(f32[1,256]{1,0:T(1,128)S(1)} %get-tuple-element.42), channel_id=1, source_target_pairs={{0,9},{1,8},{2,11},{3,10},{4,13},{5,12},{6,15},{7,14},{8,1},{9,0},... | collective-permute-start | bytes 3080 | tf_op jit(solution)/shard_map/ppermute | solution.py:69
  44.2 3.0 %collective-permute-start.22 = (f32[1,256]{1,0:T(1,128)S(1)}, f32[1,256]{1,0:T(1,128)S(1)}, u32[]{:S(2)}, u32[]{:S(2)}) collective-permute-start(f32[1,256]{1,0:T(1,128)S(1)} %get-tuple-element.42), channel_id=1, source_target_pairs={{0,10},{1,11},{2,8},{3,9},{4,14},{5,15},{6,12},{7,13},{8,2},{9,3},... | collective-permute-start | bytes 3080 | tf_op jit(solution)/shard_map/ppermute | solution.py:69
  47.2 3.9 %collective-permute-start.23 = (f32[1,256]{1,0:T(1,128)S(1)}, f32[1,256]{1,0:T(1,128)S(1)}, u32[]{:S(2)}, u32[]{:S(2)}) collective-permute-start(f32[1,256]{1,0:T(1,128)S(1)} %add_add_fusion.2), channel_id=1, source_target_pairs={{0,12},{1,13},{2,14},{3,15},{4,8},{5,9},{6,10},{7,11},{8,4},{9,5},... | collective-permute-start | bytes 3080 | tf_op jit(solution)/shard_map/ppermute | solution.py:69
  (1 other events, 1.9 us)

commit v6 on v5

--- a/solution.py
+++ b/solution.py
@@ -123,9 +123,13 @@
     second[:, half:] = dot6(lower[...], lower[...], NT)
 
 
-def cross_kernel(upper, lower, buf, third):
+def first_cross_kernel(upper, buf, cross):
+    cross[...] = dot6(buf[...], upper[...], NT)
+
+
+def cross_kernel(lower, buf, cross, third):
     half = lower.shape[0]
-    third[:, :half] = dot6(buf[...], upper[...], NT)
+    third[:, :half] = cross[...]
     third[:, half:] = dot6(buf[...], lower[...], NT)
 
 
@@ -263,8 +267,10 @@
         totals = [x + flip_tensor(x, bit, tensor) for x in totals]
     pieces = [[x] + [to_partner(x, j, tensor) for j in (1, 2, 3)] for x in totals]
     upper, first = call(first_gram_kernel, [((half, rows), f32), ((half, half), f32)], pieces[0])
+    (cross,) = call(first_cross_kernel, [((cols, half), f32)], [upper, buf])
+    cross, upper = lax.optimization_barrier((cross, upper))
     lower, second = call(second_gram_kernel, [((half, rows), f32), ((half, rank), f32)], [*pieces[1], upper])
-    (third,) = call(cross_kernel, [((cols, rank), f32)], [upper, lower, buf])
+    (third,) = call(cross_kernel, [((cols, rank), f32)], [lower, buf, cross])
     first = first + flip_fsdp(first, 0, fsdp)
     came = [flip_fsdp(x, 0, fsdp) for x in (second, third)]
     second, third = lax.optimization_barrier((second + came[0], third + came[1]))

time: 52.4 us -> 52.2 us (level)
    pallas_call x9 -> x10, Pallas kernels: 11.1 us -> 11.2 us  [call(): pl.pallas_call(body, out_shape=shapes, in_specs=[pl.BlockSpec(memory_spac...]
where the time goes in v6:
time: 52.2 us; the launch traced here: 51.8 us
  starting transfers between devices  30.3 us (58%)
  Pallas kernels  12.8 us (25%)
  waiting for transfers between devices  7.84 us (15%)
  between operations  0.79 us (2%)
    ppermute x12, starting transfers between devices, to_partner(): lax.ppermute(x, 'tensor', [(t, t ^ partner(j)) for t in range(tensor)])  15.5 us
    pallas_call x10, Pallas kernels, call(): pl.pallas_call(body, out_shape=shapes, in_specs=[pl.BlockSpec(memory_spac...  11.2 us
    ppermute x7, starting transfers between devices, flip_across(): return lax.ppermute(x, ('fsdp', 'tensor'), pairs)  8.46 us
    ppermute x2, starting transfers between devices, flip_tensor(): return lax.ppermute(x, 'tensor', [(t, t ^ 1 << bit) for t in range(tensor)])  5.61 us
    ppermute x7, waiting for transfers between devices, flip_across(): return lax.ppermute(x, ('fsdp', 'tensor'), pairs)  3.88 us
    ppermute x12, waiting for transfers between devices, to_partner(): lax.ppermute(x, 'tensor', [(t, t ^ partner(j)) for t in range(tensor)])  2.9 us
    pallas_call x1, Pallas kernels, per_device(): pl.pallas_call(power_kernel, out_shape=[jax.ShapeDtypeStruct(*x) for x in...  1.58 us
    ppermute x2, waiting for transfers between devices, flip_tensor(): return lax.ppermute(x, 'tensor', [(t, t ^ 1 << bit) for t in range(tensor)])  1.05 us
  transfers between devices with their start and end apart: 24, of which 11 were waited for; matrix products, arithmetic and copies ran while one was open for 0% of the time, Pallas kernels for 19%

profile of v6, /device:TPU:0, one launch (start us, length us, event | category | flops | bytes accessed | tf_op | source)
XLA Modules:
  0.0 51.8 jit_solution(9445331854311928289)
XLA Ops:
  0.6 1.6 %shard_map.67 = (f32[112,512]{1,0:T(8,128)S(1)}, f32[128,128]{1,0:T(8,128)S(1)}, f32[128,128]{1,0:T(8,128)S(1)}, f32[128,128]{1,0:T(8,128)S(1)}, f32[128,128]{1,...) custom-call(f32[112,512]{1,0:T(8,128)} %mom_in.1, ...), custom_call_target="tpu_custom_call" | custom-call | tf_op jit(solution)/shard_map/pallas_call | solution.py:248
  2.2 4.0 %collective-permute-start.7 = (f32[128,128]{1,0:T(8,128)S(1)}, f32[128,128]{1,0:T(8,128)S(1)}, u32[]{:S(2)}, u32[]{:S(2)}) collective-permute-start(f32[128,128]{1,0:T(8,128)S(1)} %get-tuple-element.33), channel_id=1, source_target_pairs={{0,3},{1,2},{2,1},{3,0},{4,7},{5,6},{6,5},{7,4},{8,11},{9,10},{10,... | collective-permute-start | bytes 196616 | tf_op jit(solution)/shard_map/ppermute | solution.py:53
  6.9 2.8 %collective-permute-start = (f32[128,128]{1,0:T(8,128)S(1)}, f32[128,128]{1,0:T(8,128)S(1)}, u32[]{:S(2)}, u32[]{:S(2)}) collective-permute-start(f32[128,128]{1,0:T(8,128)S(1)} %get-tuple-element.29), channel_id=1, source_target_pairs={{0,3},{1,2},{2,1},{3,0},{4,7},{5,6},{6,5},{7,4},{8,11},{9,10},{10,... | collective-permute-start | bytes 196616 | tf_op jit(solution)/shard_map/ppermute | solution.py:53
  11.4 2.6 %collective-permute-start.10 = (f32[128,128]{1,0:T(8,128)S(1)}, f32[128,128]{1,0:T(8,128)S(1)}, u32[]{:S(2)}, u32[]{:S(2)}) collective-permute-start(f32[128,128]{1,0:T(8,128)S(1)} %add_add_fusion), channel_id=1, source_target_pairs={{0,4},{1,5},{2,6},{3,7},{4,0},{5,1},{6,2},{7,3},{8,12},{9,13},{10,... | collective-permute-start | bytes 196616 | tf_op jit(solution)/shard_map/ppermute | solution.py:57
  14.6 3.0 %collective-permute-start.3 = (f32[128,128]{1,0:T(8,128)S(1)}, f32[128,128]{1,0:T(8,128)S(1)}, u32[]{:S(2)}, u32[]{:S(2)}) collective-permute-start(f32[128,128]{1,0:T(8,128)S(1)} %add_add_fusion.1), channel_id=1, source_target_pairs={{0,4},{1,5},{2,6},{3,7},{4,0},{5,1},{6,2},{7,3},{8,12},{9,13},{10,... | collective-permute-start | bytes 196616 | tf_op jit(solution)/shard_map/ppermute | solution.py:57
  17.5 1.0 %collective-permute-done.10 = f32[128,128]{1,0:T(8,128)S(1)} collective-permute-done((f32[128,128]{1,0:T(8,128)S(1)}, f32[128,128]{1,0:T(8,128)S(1)}, u32[]{:S(2)}, u32[]{:S(2)}) %collective-permute-start.10) | collective-permute-done | bytes 65568 | tf_op jit(solution)/shard_map/ppermute | solution.py:57
  18.6 1.1 %collective-permute-start.11 = (f32[128,128]{1,0:T(8,128)S(1)}, f32[128,128]{1,0:T(8,128)S(1)}, u32[]{:S(2)}, u32[]{:S(2)}) collective-permute-start(f32[128,128]{1,0:T(8,128)S(1)} %add.52.p0), channel_id=1, source_target_pairs={{0,3},{1,2},{2,1},{3,0},{4,7},{5,6},{6,5},{7,4},{8,11},{9,10},{10,... | collective-permute-start | bytes 196616 | tf_op jit(solution)/shard_map/ppermute | solution.py:53
  20.1 2.1 %collective-permute-start.13 = (f32[128,128]{1,0:T(8,128)S(1)}, f32[128,128]{1,0:T(8,128)S(1)}, u32[]{:S(2)}, u32[]{:S(2)}) collective-permute-start(f32[128,128]{1,0:T(8,128)S(1)} %add.52.p0), channel_id=1, source_target_pairs={{0,2},{1,3},{2,0},{3,1},{4,6},{5,7},{6,4},{7,5},{8,10},{9,11},{10,... | collective-permute-start | bytes 196616 | tf_op jit(solution)/shard_map/ppermute | solution.py:53
  22.2 1.1 %collective-permute-start.4 = (f32[128,128]{1,0:T(8,128)S(1)}, f32[128,128]{1,0:T(8,128)S(1)}, u32[]{:S(2)}, u32[]{:S(2)}) collective-permute-start(f32[128,128]{1,0:T(8,128)S(1)} %add.48.p0), channel_id=1, source_target_pairs={{0,3},{1,2},{2,1},{3,0},{4,7},{5,6},{6,5},{7,4},{8,11},{9,10},{10,... | collective-permute-start | bytes 196616 | tf_op jit(solution)/shard_map/ppermute | solution.py:53
  24.0 1.7 %collective-permute-start.6 = (f32[128,128]{1,0:T(8,128)S(1)}, f32[128,128]{1,0:T(8,128)S(1)}, u32[]{:S(2)}, u32[]{:S(2)}) collective-permute-start(f32[128,128]{1,0:T(8,128)S(1)} %add.48.p0), channel_id=1, source_target_pairs={{0,2},{1,3},{2,0},{3,1},{4,6},{5,7},{6,4},{7,5},{8,10},{9,11},{10,... | collective-permute-start | bytes 196616 | tf_op jit(solution)/shard_map/ppermute | solution.py:53
  26.6 0.9 %collective-permute-done.4.p1 = f32[128,128]{1,0:T(8,128)S(1)} collective-permute-done((f32[128,128]{1,0:T(8,128)S(1)}, f32[128,128]{1,0:T(8,128)S(1)}, u32[]{:S(2)}, u32[]{:S(2)}) %collective-permute-start.4) | collective-permute-done | bytes 65568 | tf_op jit(solution)/shard_map/ppermute | solution.py:53
  29.9 1.1 %collective-permute-start.19 = (f32[128,128]{1,0:T(8,128)S(1)}, f32[128,128]{1,0:T(8,128)S(1)}, u32[]{:S(2)}, u32[]{:S(2)}) collective-permute-start(f32[128,128]{1,0:T(8,128)S(1)} %add.55.gram), channel_id=1, source_target_pairs={{0,24},{1,25},{2,26},{3,27},{4,28},{5,29},{6,30},{7,31},{8,16},{9,... | collective-permute-start | bytes 196616 | tf_op jit(solution)/shard_map/ppermute | solution.py:69
  31.1 1.3 %collective-permute-start.17 = (f32[128,256]{1,0:T(8,128)S(1)}, f32[128,256]{1,0:T(8,128)S(1)}, u32[]{:S(2)}, u32[]{:S(2)}) collective-permute-start(f32[128,256]{1,0:T(8,128)S(1)} %add.53.rest), channel_id=1, source_target_pairs={{0,24},{1,25},{2,26},{3,27},{4,28},{5,29},{6,30},{7,31},{8,16},{9,... | collective-permute-start | bytes 393224 | tf_op jit(solution)/shard_map/ppermute | solution.py:69
  32.9 1.2 %collective-permute-done.19.came = f32[128,128]{1,0:T(8,128)S(1)} collective-permute-done((f32[128,128]{1,0:T(8,128)S(1)}, f32[128,128]{1,0:T(8,128)S(1)}, u32[]{:S(2)}, u32[]{:S(2)}) %collective-permute-start.19) | collective-permute-done | bytes 65568 | tf_op jit(solution)/shard_map/ppermute | solution.py:69
  34.1 2.9 %shard_map.72.inverse1 = f32[128,128]{1,0:T(8,128)S(1)} custom-call(f32[128,128]{1,0:T(8,128)S(1)} %add.55.gram, f32[128,128]{1,0:T(8,128)S(1)} %collective-permute-done.19.came), custom_call_target="tpu_custom_call" | custom-call | flops 4000000000 | tf_op jit(solution)/shard_map/pallas_call | solution.py:74
  37.1 3.5 %shard_map.73.inverse = f32[256,256]{1,0:T(8,128)S(1)} custom-call(f32[128,256]{1,0:T(8,128)S(1)} %add.53.rest, f32[128,256]{1,0:T(8,128)S(1)} %collective-permute-done.17.came, f32[128,128]{1,0:T(8,128)S(1)} %shard_map.72.inverse1), custom_call_target="tpu_custom_call" | custom-call | flops 4000000000 | tf_op jit(solution)/shard_map/pallas_call | solution.py:74
  41.0 2.3 %collective-permute-start.20 = (f32[1,256]{1,0:T(1,128)S(1)}, f32[1,256]{1,0:T(1,128)S(1)}, u32[]{:S(2)}, u32[]{:S(2)}) collective-permute-start(f32[1,256]{1,0:T(1,128)S(1)} %get-tuple-element.46), channel_id=1, source_target_pairs={{0,11},{1,10},{2,9},{3,8},{4,15},{5,14},{6,13},{7,12},{8,3},{9,2},... | collective-permute-start | bytes 3080 | tf_op jit(solution)/shard_map/ppermute | solution.py:69
  43.3 0.7 %collective-permute-start.21 = (f32[1,256]{1,0:T(1,128)S(1)}, f32[1,256]{1,0:T(1,128)S(1)}, u32[]{:S(2)}, u32[]{:S(2)}) collective-permute-start(f32[1,256]{1,0:T(1,128)S(1)} %get-tuple-element.46), channel_id=1, source_target_pairs={{0,9},{1,8},{2,11},{3,10},{4,13},{5,12},{6,15},{7,14},{8,1},{9,0},... | collective-permute-start | bytes 3080 | tf_op jit(solution)/shard_map/ppermute | solution.py:69
  45.1 1.2 %collective-permute-done.21 = f32[1,256]{1,0:T(1,128)S(1)} collective-permute-done((f32[1,256]{1,0:T(1,128)S(1)}, f32[1,256]{1,0:T(1,128)S(1)}, u32[]{:S(2)}, u32[]{:S(2)}) %collective-permute-start.21) | collective-permute-done | bytes 1056 | tf_op jit(solution)/shard_map/ppermute | solution.py:69
  46.3 0.7 %collective-permute-done.22 = f32[1,256]{1,0:T(1,128)S(1)} collective-permute-done((f32[1,256]{1,0:T(1,128)S(1)}, f32[1,256]{1,0:T(1,128)S(1)}, u32[]{:S(2)}, u32[]{:S(2)}) %collective-permute-start.22) | collective-permute-done | bytes 1056 | tf_op jit(solution)/shard_map/ppermute | solution.py:69
  47.0 2.0 %collective-permute-start.23 = (f32[1,256]{1,0:T(1,128)S(1)}, f32[1,256]{1,0:T(1,128)S(1)}, u32[]{:S(2)}, u32[]{:S(2)}) collective-permute-start(f32[1,256]{1,0:T(1,128)S(1)} %add_add_fusion.2), channel_id=1, source_target_pairs={{0,12},{1,13},{2,14},{3,15},{4,8},{5,9},{6,10},{7,11},{8,4},{9,5},... | collective-permute-start | bytes 3080 | tf_op jit(solution)/shard_map/ppermute | solution.py:69
  49.0 1.1 %shard_map.77 = f32[112,512]{1,0:T(8,128)} custom-call(f32[112,512]{1,0:T(8,128)S(1)} %get-tuple-element.37.buf, f32[112,256]{1,0:T(8,128)S(1)} %get-tuple-element.45.right, f32[256,512]{1,0:T(8,128)S(1)} %get-tuple-element.47.ortho), custom_call_target="tpu_custom_call" | custom-call | flops 2000000000 | tf_op jit(solution)/shard_map/pallas_call | solution.py:74
  50.1 0.8 %collective-permute-done.23 = f32[1,256]{1,0:T(1,128)S(1)} collective-permute-done((f32[1,256]{1,0:T(1,128)S(1)}, f32[1,256]{1,0:T(1,128)S(1)}, u32[]{:S(2)}, u32[]{:S(2)}) %collective-permute-start.23) | collective-permute-done | bytes 1056 | tf_op jit(solution)/shard_map/ppermute | solution.py:69
  50.9 1.0 %shard_map.76 = (bf16[112,512]{1,0:T(8,128)(2,1)}, f32[112,256]{1,0:T(8,128)}) custom-call(bf16[112,512]{1,0:T(8,128)(2,1)S(1)} %copy-done, f32[112,256]{1,0:T(8,128)S(1)} %get-tuple-element.45.right, f32[1,256]{1,0:T(1,128)S(1)} %add.59.squares, bf16[256,512]{1,0:T(8,128)(2,1)S(1)} %get-tuple-element.49.high, bf16[256,512]{1,0:T(8,128)(2,1)S(1)} %get-tuple-element.50.mid), custom_call_target="tpu_custom_call" | custom-call | flops 1000000000 | tf_op jit(solution)/shard_map/pallas_call | solution.py:74
  (46 shorter events, 9.3 us)
Async XLA Ops:
  2.2 8.0 %collective-permute-start.7 = (f32[128,128]{1,0:T(8,128)S(1)}, f32[128,128]{1,0:T(8,128)S(1)}, u32[]{:S(2)}, u32[]{:S(2)}) collective-permute-start(f32[128,128]{1,0:T(8,128)S(1)} %get-tuple-element.33), channel_id=1, source_target_pairs={{0,3},{1,2},{2,1},{3,0},{4,7},{5,6},{6,5},{7,4},{8,11},{9,10},{10,... | collective-permute-start | bytes 196616 | tf_op jit(solution)/shard_map/ppermute | solution.py:53
  6.3 5.1 %collective-permute-start.8 = (f32[128,128]{1,0:T(8,128)S(1)}, f32[128,128]{1,0:T(8,128)S(1)}, u32[]{:S(2)}, u32[]{:S(2)}) collective-permute-start(f32[128,128]{1,0:T(8,128)S(1)} %get-tuple-element.34), channel_id=1, source_target_pairs={{0,1},{1,0},{2,3},{3,2},{4,5},{5,4},{6,7},{7,6},{8,9},{9,8},{10,11... | collective-permute-start | bytes 196616 | tf_op jit(solution)/shard_map/ppermute | solution.py:53
  6.8 4.6 %collective-permute-start.9 = (f32[128,128]{1,0:T(8,128)S(1)}, f32[128,128]{1,0:T(8,128)S(1)}, u32[]{:S(2)}, u32[]{:S(2)}) collective-permute-start(f32[128,128]{1,0:T(8,128)S(1)} %get-tuple-element.35), channel_id=1, source_target_pairs={{0,2},{1,3},{2,0},{3,1},{4,6},{5,7},{6,4},{7,5},{8,10},{9,11},{10,... | collective-permute-start | bytes 196616 | tf_op jit(solution)/shard_map/ppermute | solution.py:53
  6.9 7.1 %collective-permute-start = (f32[128,128]{1,0:T(8,128)S(1)}, f32[128,128]{1,0:T(8,128)S(1)}, u32[]{:S(2)}, u32[]{:S(2)}) collective-permute-start(f32[128,128]{1,0:T(8,128)S(1)} %get-tuple-element.29), channel_id=1, source_target_pairs={{0,3},{1,2},{2,1},{3,0},{4,7},{5,6},{6,5},{7,4},{8,11},{9,10},{10,... | collective-permute-start | bytes 196616 | tf_op jit(solution)/shard_map/ppermute | solution.py:53
  9.8 4.3 %collective-permute-start.1 = (f32[128,128]{1,0:T(8,128)S(1)}, f32[128,128]{1,0:T(8,128)S(1)}, u32[]{:S(2)}, u32[]{:S(2)}) collective-permute-start(f32[128,128]{1,0:T(8,128)S(1)} %get-tuple-element.30), channel_id=1, source_target_pairs={{0,1},{1,0},{2,3},{3,2},{4,5},{5,4},{6,7},{7,6},{8,9},{9,8},{10,11... | collective-permute-start | bytes 196616 | tf_op jit(solution)/shard_map/ppermute | solution.py:53
  10.3 4.3 %collective-permute-start.2 = (f32[128,128]{1,0:T(8,128)S(1)}, f32[128,128]{1,0:T(8,128)S(1)}, u32[]{:S(2)}, u32[]{:S(2)}) collective-permute-start(f32[128,128]{1,0:T(8,128)S(1)} %get-tuple-element.31), channel_id=1, source_target_pairs={{0,2},{1,3},{2,0},{3,1},{4,6},{5,7},{6,4},{7,5},{8,10},{9,11},{10,... | collective-permute-start | bytes 196616 | tf_op jit(solution)/shard_map/ppermute | solution.py:53
  11.4 7.2 %collective-permute-start.10 = (f32[128,128]{1,0:T(8,128)S(1)}, f32[128,128]{1,0:T(8,128)S(1)}, u32[]{:S(2)}, u32[]{:S(2)}) collective-permute-start(f32[128,128]{1,0:T(8,128)S(1)} %add_add_fusion), channel_id=1, source_target_pairs={{0,4},{1,5},{2,6},{3,7},{4,0},{5,1},{6,2},{7,3},{8,12},{9,13},{10,... | collective-permute-start | bytes 196616 | tf_op jit(solution)/shard_map/ppermute | solution.py:57
  14.6 7.6 %collective-permute-start.3 = (f32[128,128]{1,0:T(8,128)S(1)}, f32[128,128]{1,0:T(8,128)S(1)}, u32[]{:S(2)}, u32[]{:S(2)}) collective-permute-start(f32[128,128]{1,0:T(8,128)S(1)} %add_add_fusion.1), channel_id=1, source_target_pairs={{0,4},{1,5},{2,6},{3,7},{4,0},{5,1},{6,2},{7,3},{8,12},{9,13},{10,... | collective-permute-start | bytes 196616 | tf_op jit(solution)/shard_map/ppermute | solution.py:57
  18.6 5.4 %collective-permute-start.11 = (f32[128,128]{1,0:T(8,128)S(1)}, f32[128,128]{1,0:T(8,128)S(1)}, u32[]{:S(2)}, u32[]{:S(2)}) collective-permute-start(f32[128,128]{1,0:T(8,128)S(1)} %add.52.p0), channel_id=1, source_target_pairs={{0,3},{1,2},{2,1},{3,0},{4,7},{5,6},{6,5},{7,4},{8,11},{9,10},{10,... | collective-permute-start | bytes 196616 | tf_op jit(solution)/shard_map/ppermute | solution.py:53
  19.7 6.1 %collective-permute-start.12 = (f32[128,128]{1,0:T(8,128)S(1)}, f32[128,128]{1,0:T(8,128)S(1)}, u32[]{:S(2)}, u32[]{:S(2)}) collective-permute-start(f32[128,128]{1,0:T(8,128)S(1)} %add.52.p0), channel_id=1, source_target_pairs={{0,1},{1,0},{2,3},{3,2},{4,5},{5,4},{6,7},{7,6},{8,9},{9,8},{10,11... | collective-permute-start | bytes 196616 | tf_op jit(solution)/shard_map/ppermute | solution.py:53
  20.1 5.7 %collective-permute-start.13 = (f32[128,128]{1,0:T(8,128)S(1)}, f32[128,128]{1,0:T(8,128)S(1)}, u32[]{:S(2)}, u32[]{:S(2)}) collective-permute-start(f32[128,128]{1,0:T(8,128)S(1)} %add.52.p0), channel_id=1, source_target_pairs={{0,2},{1,3},{2,0},{3,1},{4,6},{5,7},{6,4},{7,5},{8,10},{9,11},{10,... | collective-permute-start | bytes 196616 | tf_op jit(solution)/shard_map/ppermute | solution.py:53
  22.2 5.3 %collective-permute-start.4 = (f32[128,128]{1,0:T(8,128)S(1)}, f32[128,128]{1,0:T(8,128)S(1)}, u32[]{:S(2)}, u32[]{:S(2)}) collective-permute-start(f32[128,128]{1,0:T(8,128)S(1)} %add.48.p0), channel_id=1, source_target_pairs={{0,3},{1,2},{2,1},{3,0},{4,7},{5,6},{6,5},{7,4},{8,11},{9,10},{10,... | collective-permute-start | bytes 196616 | tf_op jit(solution)/shard_map/ppermute | solution.py:53
  23.2 4.9 %collective-permute-start.5 = (f32[128,128]{1,0:T(8,128)S(1)}, f32[128,128]{1,0:T(8,128)S(1)}, u32[]{:S(2)}, u32[]{:S(2)}) collective-permute-start(f32[128,128]{1,0:T(8,128)S(1)} %add.48.p0), channel_id=1, source_target_pairs={{0,1},{1,0},{2,3},{3,2},{4,5},{5,4},{6,7},{7,6},{8,9},{9,8},{10,11... | collective-permute-start | bytes 196616 | tf_op jit(solution)/shard_map/ppermute | solution.py:53
  24.0 4.3 %collective-permute-start.6 = (f32[128,128]{1,0:T(8,128)S(1)}, f32[128,128]{1,0:T(8,128)S(1)}, u32[]{:S(2)}, u32[]{:S(2)}) collective-permute-start(f32[128,128]{1,0:T(8,128)S(1)} %add.48.p0), channel_id=1, source_target_pairs={{0,2},{1,3},{2,0},{3,1},{4,6},{5,7},{6,4},{7,5},{8,10},{9,11},{10,... | collective-permute-start | bytes 196616 | tf_op jit(solution)/shard_map/ppermute | solution.py:53
  26.1 3.7 %collective-permute-start.18 = (f32[128,128]{1,0:T(8,128)S(1)}, f32[128,128]{1,0:T(8,128)S(1)}, u32[]{:S(2)}, u32[]{:S(2)}) collective-permute-start(f32[128,128]{1,0:T(8,128)S(1)} %get-tuple-element.44), channel_id=1, source_target_pairs={{0,8},{8,0},{16,24},{24,16},{1,9},{9,1},{17,25},{25,17},{2,10},{10... | collective-permute-start | bytes 196616 | tf_op jit(solution)/shard_map/ppermute | solution.py:61
  28.8 2.2 %collective-permute-start.14 = (f32[128,256]{1,0:T(8,128)S(1)}, f32[128,256]{1,0:T(8,128)S(1)}, u32[]{:S(2)}, u32[]{:S(2)}) collective-permute-start(f32[128,256]{1,0:T(8,128)S(1)} %get-tuple-element.39), channel_id=1, source_target_pairs={{0,8},{8,0},{16,24},{24,16},{1,9},{9,1},{17,25},{25,17},{2,10},{10... | collective-permute-start | bytes 393224 | tf_op jit(solution)/shard_map/ppermute | solution.py:61
  29.3 1.7 %collective-permute-start.15 = (f32[112,256]{1,0:T(8,128)S(1)}, f32[112,256]{1,0:T(8,128)S(1)}, u32[]{:S(2)}, u32[]{:S(2)}) collective-permute-start(f32[112,256]{1,0:T(8,128)S(1)} %shard_map.71), channel_id=1, source_target_pairs={{0,8},{8,0},{16,24},{24,16},{1,9},{9,1},{17,25},{25,17},{2,10},{10... | collective-permute-start | bytes 344072 | tf_op jit(solution)/shard_map/ppermute | solution.py:61
  29.9 4.2 %collective-permute-start.19 = (f32[128,128]{1,0:T(8,128)S(1)}, f32[128,128]{1,0:T(8,128)S(1)}, u32[]{:S(2)}, u32[]{:S(2)}) collective-permute-start(f32[128,128]{1,0:T(8,128)S(1)} %add.55.gram), channel_id=1, source_target_pairs={{0,24},{1,25},{2,26},{3,27},{4,28},{5,29},{6,30},{7,31},{8,16},{9,... | collective-permute-start | bytes 196616 | tf_op jit(solution)/shard_map/ppermute | solution.py:69
  31.1 6.0 %collective-permute-start.17 = (f32[128,256]{1,0:T(8,128)S(1)}, f32[128,256]{1,0:T(8,128)S(1)}, u32[]{:S(2)}, u32[]{:S(2)}) collective-permute-start(f32[128,256]{1,0:T(8,128)S(1)} %add.53.rest), channel_id=1, source_target_pairs={{0,24},{1,25},{2,26},{3,27},{4,28},{5,29},{6,30},{7,31},{8,16},{9,... | collective-permute-start | bytes 393224 | tf_op jit(solution)/shard_map/ppermute | solution.py:69
  32.4 8.2 %collective-permute-start.16 = (f32[112,256]{1,0:T(8,128)S(1)}, f32[112,256]{1,0:T(8,128)S(1)}, u32[]{:S(2)}, u32[]{:S(2)}) collective-permute-start(f32[112,256]{1,0:T(8,128)S(1)} %add.54.cross), channel_id=1, source_target_pairs={{0,24},{1,25},{2,26},{3,27},{4,28},{5,29},{6,30},{7,31},{8,16},{9,... | collective-permute-start | bytes 344072 | tf_op jit(solution)/shard_map/ppermute | solution.py:69
  41.0 4.1 %collective-permute-start.20 = (f32[1,256]{1,0:T(1,128)S(1)}, f32[1,256]{1,0:T(1,128)S(1)}, u32[]{:S(2)}, u32[]{:S(2)}) collective-permute-start(f32[1,256]{1,0:T(1,128)S(1)} %get-tuple-element.46), channel_id=1, source_target_pairs={{0,11},{1,10},{2,9},{3,8},{4,15},{5,14},{6,13},{7,12},{8,3},{9,2},... | collective-permute-start | bytes 3080 | tf_op jit(solution)/shard_map/ppermute | solution.py:69
  43.3 3.0 %collective-permute-start.21 = (f32[1,256]{1,0:T(1,128)S(1)}, f32[1,256]{1,0:T(1,128)S(1)}, u32[]{:S(2)}, u32[]{:S(2)}) collective-permute-start(f32[1,256]{1,0:T(1,128)S(1)} %get-tuple-element.46), channel_id=1, source_target_pairs={{0,9},{1,8},{2,11},{3,10},{4,13},{5,12},{6,15},{7,14},{8,1},{9,0},... | collective-permute-start | bytes 3080 | tf_op jit(solution)/shard_map/ppermute | solution.py:69
  44.0 3.0 %collective-permute-start.22 = (f32[1,256]{1,0:T(1,128)S(1)}, f32[1,256]{1,0:T(1,128)S(1)}, u32[]{:S(2)}, u32[]{:S(2)}) collective-permute-start(f32[1,256]{1,0:T(1,128)S(1)} %get-tuple-element.46), channel_id=1, source_target_pairs={{0,10},{1,11},{2,8},{3,9},{4,14},{5,15},{6,12},{7,13},{8,2},{9,3},... | collective-permute-start | bytes 3080 | tf_op jit(solution)/shard_map/ppermute | solution.py:69
  47.0 3.9 %collective-permute-start.23 = (f32[1,256]{1,0:T(1,128)S(1)}, f32[1,256]{1,0:T(1,128)S(1)}, u32[]{:S(2)}, u32[]{:S(2)}) collective-permute-start(f32[1,256]{1,0:T(1,128)S(1)} %add_add_fusion.2), channel_id=1, source_target_pairs={{0,12},{1,13},{2,14},{3,15},{4,8},{5,9},{6,10},{7,11},{8,4},{9,5},... | collective-permute-start | bytes 3080 | tf_op jit(solution)/shard_map/ppermute | solution.py:69
  (1 other events, 1.9 us)

commit v7 on v6

--- a/solution.py
+++ b/solution.py
@@ -227,16 +227,26 @@
     out[...] = buf[...] - (1.0 - momentum_decay) * dot6(right[...], ortho[...], NN)
 
 
-def weight_kernel(scale, weight, right, squares, high, mid, out, q_new):
+def weight_kernel(scale, weight, right, squares, high, mid, out_hbm, q_hbm, out, q_new, sems):
     q = right[...] / (jnp.sqrt(squares[...]) + norm_eps)
     q_new[...] = q
+    copies = [pltpu.make_async_copy(q_new, q_hbm, sems.at[2])]
+    copies[0].start()
     qh, qm, _ = split3(q)
 
     def one(x, y):
-        return lax.dot_general(x, y[...], NN, preferred_element_type=f32)
-
-    update = one(qh, high) + (one(qh, mid) + one(qm, high) + one(qm, mid))
-    out[...] = (weight[...].astype(f32) - scale * update).astype(bf16)
+        return lax.dot_general(x, y, NN, preferred_element_type=f32)
+
+    half = out.shape[1] // 2
+    for i in range(2):
+        here = pl.ds(i * half, half)
+        h, m = high[:, here], mid[:, here]
+        update = one(qh, h) + (one(qh, m) + one(qm, h) + one(qm, m))
+        out[:, here] = (weight[:, here].astype(f32) - scale * update).astype(bf16)
+        copies.append(pltpu.make_async_copy(out.at[:, here], out_hbm.at[:, here], sems.at[i]))
+        copies[-1].start()
+    for copy in copies:
+        copy.wait()
 
 
 def per_device(fsdp, tensor, weight, momentum, grad, q_prev):
@@ -291,11 +301,18 @@
     squares, ortho = lax.optimization_barrier((squares, ortho))
     for bit in range(2, bits_of(tensor)):
         squares = squares + flip_across(squares, 0, 1 << bit, fsdp, tensor)
-    new_weight, q_new = call(
+    new_weight, q_new = pl.pallas_call(
         functools.partial(weight_kernel, scale),
-        [((cols, rows), bf16), ((cols, rank), f32)],
-        [weight, right, squares, high, mid],
-    )
+        out_shape=[jax.ShapeDtypeStruct((cols, rows), bf16), jax.ShapeDtypeStruct((cols, rank), f32)],
+        in_specs=[pl.BlockSpec(memory_space=pltpu.VMEM)] * 5,
+        out_specs=[pl.BlockSpec(memory_space=pltpu.HBM)] * 2,
+        scratch_shapes=[
+            pltpu.VMEM((cols, rows), bf16),
+            pltpu.VMEM((cols, rank), f32),
+            pltpu.SemaphoreType.DMA((3,)),
+        ],
+        compiler_params=pltpu.CompilerParams(vmem_limit_bytes=vmem_bytes),
+    )(weight, right, squares, high, mid)
     return (new_weight, new_momentum, q_new)
 
 

time: 52.2 us -> 52.2 us (level)
    pallas_call x0 -> x1, Pallas kernels: none -> 0.98 us  [per_device(): pl.pallas_call(functools.partial(weight_kernel, scale), out_shape=[jax.Sh...]
    pallas_call x10 -> x9, Pallas kernels: 11.2 us -> 10.3 us  [call(): pl.pallas_call(body, out_shape=shapes, in_specs=[pl.BlockSpec(memory_spac...]
where the time goes in v7:
time: 52.2 us; the launch traced here: 51.9 us
  starting transfers between devices  30.3 us (58%)
  Pallas kernels  12.8 us (25%)
  waiting for transfers between devices  7.84 us (15%)
  between operations  0.79 us (2%)
    ppermute x12, starting transfers between devices, to_partner(): lax.ppermute(x, 'tensor', [(t, t ^ partner(j)) for t in range(tensor)])  15.5 us
    pallas_call x9, Pallas kernels, call(): pl.pallas_call(body, out_shape=shapes, in_specs=[pl.BlockSpec(memory_spac...  10.3 us
    ppermute x7, starting transfers between devices, flip_across(): return lax.ppermute(x, ('fsdp', 'tensor'), pairs)  8.46 us
    ppermute x2, starting transfers between devices, flip_tensor(): return lax.ppermute(x, 'tensor', [(t, t ^ 1 << bit) for t in range(tensor)])  5.61 us
    ppermute x7, waiting for transfers between devices, flip_across(): return lax.ppermute(x, ('fsdp', 'tensor'), pairs)  3.88 us
    ppermute x12, waiting for transfers between devices, to_partner(): lax.ppermute(x, 'tensor', [(t, t ^ partner(j)) for t in range(tensor)])  2.9 us
    pallas_call x1, Pallas kernels, per_device(): pl.pallas_call(power_kernel, out_shape=[jax.ShapeDtypeStruct(*x) for x in...  1.58 us
    ppermute x2, waiting for transfers between devices, flip_tensor(): return lax.ppermute(x, 'tensor', [(t, t ^ 1 << bit) for t in range(tensor)])  1.05 us
  transfers between devices with their start and end apart: 24, of which 11 were waited for; matrix products, arithmetic and copies ran while one was open for 0% of the time, Pallas kernels for 19%

profile of v7, /device:TPU:0, one launch (start us, length us, event | category | flops | bytes accessed | tf_op | source)
XLA Modules:
  0.0 51.9 jit_solution(17234742796907594907)
XLA Ops:
  0.6 1.6 %shard_map.67 = (f32[112,512]{1,0:T(8,128)S(1)}, f32[128,128]{1,0:T(8,128)S(1)}, f32[128,128]{1,0:T(8,128)S(1)}, f32[128,128]{1,0:T(8,128)S(1)}, f32[128,128]{1,...) custom-call(f32[112,512]{1,0:T(8,128)} %mom_in.1, ...), custom_call_target="tpu_custom_call" | custom-call | tf_op jit(solution)/shard_map/pallas_call | solution.py:258
  2.2 4.0 %collective-permute-start.7 = (f32[128,128]{1,0:T(8,128)S(1)}, f32[128,128]{1,0:T(8,128)S(1)}, u32[]{:S(2)}, u32[]{:S(2)}) collective-permute-start(f32[128,128]{1,0:T(8,128)S(1)} %get-tuple-element.33), channel_id=1, source_target_pairs={{0,3},{1,2},{2,1},{3,0},{4,7},{5,6},{6,5},{7,4},{8,11},{9,10},{10,... | collective-permute-start | bytes 196616 | tf_op jit(solution)/shard_map/ppermute | solution.py:53
  6.9 2.8 %collective-permute-start = (f32[128,128]{1,0:T(8,128)S(1)}, f32[128,128]{1,0:T(8,128)S(1)}, u32[]{:S(2)}, u32[]{:S(2)}) collective-permute-start(f32[128,128]{1,0:T(8,128)S(1)} %get-tuple-element.29), channel_id=1, source_target_pairs={{0,3},{1,2},{2,1},{3,0},{4,7},{5,6},{6,5},{7,4},{8,11},{9,10},{10,... | collective-permute-start | bytes 196616 | tf_op jit(solution)/shard_map/ppermute | solution.py:53
  11.4 2.6 %collective-permute-start.10 = (f32[128,128]{1,0:T(8,128)S(1)}, f32[128,128]{1,0:T(8,128)S(1)}, u32[]{:S(2)}, u32[]{:S(2)}) collective-permute-start(f32[128,128]{1,0:T(8,128)S(1)} %add_add_fusion), channel_id=1, source_target_pairs={{0,4},{1,5},{2,6},{3,7},{4,0},{5,1},{6,2},{7,3},{8,12},{9,13},{10,... | collective-permute-start | bytes 196616 | tf_op jit(solution)/shard_map/ppermute | solution.py:57
  14.6 3.0 %collective-permute-start.3 = (f32[128,128]{1,0:T(8,128)S(1)}, f32[128,128]{1,0:T(8,128)S(1)}, u32[]{:S(2)}, u32[]{:S(2)}) collective-permute-start(f32[128,128]{1,0:T(8,128)S(1)} %add_add_fusion.1), channel_id=1, source_target_pairs={{0,4},{1,5},{2,6},{3,7},{4,0},{5,1},{6,2},{7,3},{8,12},{9,13},{10,... | collective-permute-start | bytes 196616 | tf_op jit(solution)/shard_map/ppermute | solution.py:57
  17.5 1.0 %collective-permute-done.10 = f32[128,128]{1,0:T(8,128)S(1)} collective-permute-done((f32[128,128]{1,0:T(8,128)S(1)}, f32[128,128]{1,0:T(8,128)S(1)}, u32[]{:S(2)}, u32[]{:S(2)}) %collective-permute-start.10) | collective-permute-done | bytes 65568 | tf_op jit(solution)/shard_map/ppermute | solution.py:57
  18.6 1.1 %collective-permute-start.11 = (f32[128,128]{1,0:T(8,128)S(1)}, f32[128,128]{1,0:T(8,128)S(1)}, u32[]{:S(2)}, u32[]{:S(2)}) collective-permute-start(f32[128,128]{1,0:T(8,128)S(1)} %add.52.p0), channel_id=1, source_target_pairs={{0,3},{1,2},{2,1},{3,0},{4,7},{5,6},{6,5},{7,4},{8,11},{9,10},{10,... | collective-permute-start | bytes 196616 | tf_op jit(solution)/shard_map/ppermute | solution.py:53
  20.1 2.1 %collective-permute-start.13 = (f32[128,128]{1,0:T(8,128)S(1)}, f32[128,128]{1,0:T(8,128)S(1)}, u32[]{:S(2)}, u32[]{:S(2)}) collective-permute-start(f32[128,128]{1,0:T(8,128)S(1)} %add.52.p0), channel_id=1, source_target_pairs={{0,2},{1,3},{2,0},{3,1},{4,6},{5,7},{6,4},{7,5},{8,10},{9,11},{10,... | collective-permute-start | bytes 196616 | tf_op jit(solution)/shard_map/ppermute | solution.py:53
  22.2 1.1 %collective-permute-start.4 = (f32[128,128]{1,0:T(8,128)S(1)}, f32[128,128]{1,0:T(8,128)S(1)}, u32[]{:S(2)}, u32[]{:S(2)}) collective-permute-start(f32[128,128]{1,0:T(8,128)S(1)} %add.48.p0), channel_id=1, source_target_pairs={{0,3},{1,2},{2,1},{3,0},{4,7},{5,6},{6,5},{7,4},{8,11},{9,10},{10,... | collective-permute-start | bytes 196616 | tf_op jit(solution)/shard_map/ppermute | solution.py:53
  24.0 1.7 %collective-permute-start.6 = (f32[128,128]{1,0:T(8,128)S(1)}, f32[128,128]{1,0:T(8,128)S(1)}, u32[]{:S(2)}, u32[]{:S(2)}) collective-permute-start(f32[128,128]{1,0:T(8,128)S(1)} %add.48.p0), channel_id=1, source_target_pairs={{0,2},{1,3},{2,0},{3,1},{4,6},{5,7},{6,4},{7,5},{8,10},{9,11},{10,... | collective-permute-start | bytes 196616 | tf_op jit(solution)/shard_map/ppermute | solution.py:53
  26.6 0.9 %collective-permute-done.4.p1 = f32[128,128]{1,0:T(8,128)S(1)} collective-permute-done((f32[128,128]{1,0:T(8,128)S(1)}, f32[128,128]{1,0:T(8,128)S(1)}, u32[]{:S(2)}, u32[]{:S(2)}) %collective-permute-start.4) | collective-permute-done | bytes 65568 | tf_op jit(solution)/shard_map/ppermute | solution.py:53
  29.9 1.1 %collective-permute-start.19 = (f32[128,128]{1,0:T(8,128)S(1)}, f32[128,128]{1,0:T(8,128)S(1)}, u32[]{:S(2)}, u32[]{:S(2)}) collective-permute-start(f32[128,128]{1,0:T(8,128)S(1)} %add.55.gram), channel_id=1, source_target_pairs={{0,24},{1,25},{2,26},{3,27},{4,28},{5,29},{6,30},{7,31},{8,16},{9,... | collective-permute-start | bytes 196616 | tf_op jit(solution)/shard_map/ppermute | solution.py:69
  31.1 1.3 %collective-permute-start.17 = (f32[128,256]{1,0:T(8,128)S(1)}, f32[128,256]{1,0:T(8,128)S(1)}, u32[]{:S(2)}, u32[]{:S(2)}) collective-permute-start(f32[128,256]{1,0:T(8,128)S(1)} %add.53.rest), channel_id=1, source_target_pairs={{0,24},{1,25},{2,26},{3,27},{4,28},{5,29},{6,30},{7,31},{8,16},{9,... | collective-permute-start | bytes 393224 | tf_op jit(solution)/shard_map/ppermute | solution.py:69
  32.9 1.2 %collective-permute-done.19.came = f32[128,128]{1,0:T(8,128)S(1)} collective-permute-done((f32[128,128]{1,0:T(8,128)S(1)}, f32[128,128]{1,0:T(8,128)S(1)}, u32[]{:S(2)}, u32[]{:S(2)}) %collective-permute-start.19) | collective-permute-done | bytes 65568 | tf_op jit(solution)/shard_map/ppermute | solution.py:69
  34.1 2.9 %shard_map.72.inverse1 = f32[128,128]{1,0:T(8,128)S(1)} custom-call(f32[128,128]{1,0:T(8,128)S(1)} %add.55.gram, f32[128,128]{1,0:T(8,128)S(1)} %collective-permute-done.19.came), custom_call_target="tpu_custom_call" | custom-call | flops 4000000000 | tf_op jit(solution)/shard_map/pallas_call | solution.py:74
  37.1 3.5 %shard_map.73.inverse = f32[256,256]{1,0:T(8,128)S(1)} custom-call(f32[128,256]{1,0:T(8,128)S(1)} %add.53.rest, f32[128,256]{1,0:T(8,128)S(1)} %collective-permute-done.17.came, f32[128,128]{1,0:T(8,128)S(1)} %shard_map.72.inverse1), custom_call_target="tpu_custom_call" | custom-call | flops 4000000000 | tf_op jit(solution)/shard_map/pallas_call | solution.py:74
  41.0 2.3 %collective-permute-start.20 = (f32[1,256]{1,0:T(1,128)S(1)}, f32[1,256]{1,0:T(1,128)S(1)}, u32[]{:S(2)}, u32[]{:S(2)}) collective-permute-start(f32[1,256]{1,0:T(1,128)S(1)} %get-tuple-element.46), channel_id=1, source_target_pairs={{0,11},{1,10},{2,9},{3,8},{4,15},{5,14},{6,13},{7,12},{8,3},{9,2},... | collective-permute-start | bytes 3080 | tf_op jit(solution)/shard_map/ppermute | solution.py:69
  43.3 0.7 %collective-permute-start.21 = (f32[1,256]{1,0:T(1,128)S(1)}, f32[1,256]{1,0:T(1,128)S(1)}, u32[]{:S(2)}, u32[]{:S(2)}) collective-permute-start(f32[1,256]{1,0:T(1,128)S(1)} %get-tuple-element.46), channel_id=1, source_target_pairs={{0,9},{1,8},{2,11},{3,10},{4,13},{5,12},{6,15},{7,14},{8,1},{9,0},... | collective-permute-start | bytes 3080 | tf_op jit(solution)/shard_map/ppermute | solution.py:69
  45.1 1.2 %collective-permute-done.21 = f32[1,256]{1,0:T(1,128)S(1)} collective-permute-done((f32[1,256]{1,0:T(1,128)S(1)}, f32[1,256]{1,0:T(1,128)S(1)}, u32[]{:S(2)}, u32[]{:S(2)}) %collective-permute-start.21) | collective-permute-done | bytes 1056 | tf_op jit(solution)/shard_map/ppermute | solution.py:69
  46.3 0.7 %collective-permute-done.22 = f32[1,256]{1,0:T(1,128)S(1)} collective-permute-done((f32[1,256]{1,0:T(1,128)S(1)}, f32[1,256]{1,0:T(1,128)S(1)}, u32[]{:S(2)}, u32[]{:S(2)}) %collective-permute-start.22) | collective-permute-done | bytes 1056 | tf_op jit(solution)/shard_map/ppermute | solution.py:69
  47.0 2.0 %collective-permute-start.23 = (f32[1,256]{1,0:T(1,128)S(1)}, f32[1,256]{1,0:T(1,128)S(1)}, u32[]{:S(2)}, u32[]{:S(2)}) collective-permute-start(f32[1,256]{1,0:T(1,128)S(1)} %add_add_fusion.2), channel_id=1, source_target_pairs={{0,12},{1,13},{2,14},{3,15},{4,8},{5,9},{6,10},{7,11},{8,4},{9,5},... | collective-permute-start | bytes 3080 | tf_op jit(solution)/shard_map/ppermute | solution.py:69
  49.0 1.1 %shard_map.77 = f32[112,512]{1,0:T(8,128)} custom-call(f32[112,512]{1,0:T(8,128)S(1)} %get-tuple-element.37.buf, f32[112,256]{1,0:T(8,128)S(1)} %get-tuple-element.45.right, f32[256,512]{1,0:T(8,128)S(1)} %get-tuple-element.47.ortho), custom_call_target="tpu_custom_call" | custom-call | flops 2000000000 | tf_op jit(solution)/shard_map/pallas_call | solution.py:74
  50.1 0.8 %collective-permute-done.23 = f32[1,256]{1,0:T(1,128)S(1)} collective-permute-done((f32[1,256]{1,0:T(1,128)S(1)}, f32[1,256]{1,0:T(1,128)S(1)}, u32[]{:S(2)}, u32[]{:S(2)}) %collective-permute-start.23) | collective-permute-done | bytes 1056 | tf_op jit(solution)/shard_map/ppermute | solution.py:69
  50.9 1.0 %shard_map.76 = (bf16[112,512]{1,0:T(8,128)(2,1)}, f32[112,256]{1,0:T(8,128)}) custom-call(bf16[112,512]{1,0:T(8,128)(2,1)S(1)} %copy-done, f32[112,256]{1,0:T(8,128)S(1)} %get-tuple-element.45.right, f32[1,256]{1,0:T(1,128)S(1)} %add.59.squares, bf16[256,512]{1,0:T(8,128)(2,1)S(1)} %get-tuple-element.49.high, bf16[256,512]{1,0:T(8,128)(2,1)S(1)} %get-tuple-element.50.mid), custom_call_target="tpu_custom_call" | custom-call | tf_op jit(solution)/shard_map/pallas_call | solution.py:304
  (46 shorter events, 9.3 us)
Async XLA Ops:
  2.2 8.0 %collective-permute-start.7 = (f32[128,128]{1,0:T(8,128)S(1)}, f32[128,128]{1,0:T(8,128)S(1)}, u32[]{:S(2)}, u32[]{:S(2)}) collective-permute-start(f32[128,128]{1,0:T(8,128)S(1)} %get-tuple-element.33), channel_id=1, source_target_pairs={{0,3},{1,2},{2,1},{3,0},{4,7},{5,6},{6,5},{7,4},{8,11},{9,10},{10,... | collective-permute-start | bytes 196616 | tf_op jit(solution)/shard_map/ppermute | solution.py:53
  6.3 5.1 %collective-permute-start.8 = (f32[128,128]{1,0:T(8,128)S(1)}, f32[128,128]{1,0:T(8,128)S(1)}, u32[]{:S(2)}, u32[]{:S(2)}) collective-permute-start(f32[128,128]{1,0:T(8,128)S(1)} %get-tuple-element.34), channel_id=1, source_target_pairs={{0,1},{1,0},{2,3},{3,2},{4,5},{5,4},{6,7},{7,6},{8,9},{9,8},{10,11... | collective-permute-start | bytes 196616 | tf_op jit(solution)/shard_map/ppermute | solution.py:53
  6.8 4.6 %collective-permute-start.9 = (f32[128,128]{1,0:T(8,128)S(1)}, f32[128,128]{1,0:T(8,128)S(1)}, u32[]{:S(2)}, u32[]{:S(2)}) collective-permute-start(f32[128,128]{1,0:T(8,128)S(1)} %get-tuple-element.35), channel_id=1, source_target_pairs={{0,2},{1,3},{2,0},{3,1},{4,6},{5,7},{6,4},{7,5},{8,10},{9,11},{10,... | collective-permute-start | bytes 196616 | tf_op jit(solution)/shard_map/ppermute | solution.py:53
  6.9 7.1 %collective-permute-start = (f32[128,128]{1,0:T(8,128)S(1)}, f32[128,128]{1,0:T(8,128)S(1)}, u32[]{:S(2)}, u32[]{:S(2)}) collective-permute-start(f32[128,128]{1,0:T(8,128)S(1)} %get-tuple-element.29), channel_id=1, source_target_pairs={{0,3},{1,2},{2,1},{3,0},{4,7},{5,6},{6,5},{7,4},{8,11},{9,10},{10,... | collective-permute-start | bytes 196616 | tf_op jit(solution)/shard_map/ppermute | solution.py:53
  9.8 4.3 %collective-permute-start.1 = (f32[128,128]{1,0:T(8,128)S(1)}, f32[128,128]{1,0:T(8,128)S(1)}, u32[]{:S(2)}, u32[]{:S(2)}) collective-permute-start(f32[128,128]{1,0:T(8,128)S(1)} %get-tuple-element.30), channel_id=1, source_target_pairs={{0,1},{1,0},{2,3},{3,2},{4,5},{5,4},{6,7},{7,6},{8,9},{9,8},{10,11... | collective-permute-start | bytes 196616 | tf_op jit(solution)/shard_map/ppermute | solution.py:53
  10.3 4.3 %collective-permute-start.2 = (f32[128,128]{1,0:T(8,128)S(1)}, f32[128,128]{1,0:T(8,128)S(1)}, u32[]{:S(2)}, u32[]{:S(2)}) collective-permute-start(f32[128,128]{1,0:T(8,128)S(1)} %get-tuple-element.31), channel_id=1, source_target_pairs={{0,2},{1,3},{2,0},{3,1},{4,6},{5,7},{6,4},{7,5},{8,10},{9,11},{10,... | collective-permute-start | bytes 196616 | tf_op jit(solution)/shard_map/ppermute | solution.py:53
  11.4 7.2 %collective-permute-start.10 = (f32[128,128]{1,0:T(8,128)S(1)}, f32[128,128]{1,0:T(8,128)S(1)}, u32[]{:S(2)}, u32[]{:S(2)}) collective-permute-start(f32[128,128]{1,0:T(8,128)S(1)} %add_add_fusion), channel_id=1, source_target_pairs={{0,4},{1,5},{2,6},{3,7},{4,0},{5,1},{6,2},{7,3},{8,12},{9,13},{10,... | collective-permute-start | bytes 196616 | tf_op jit(solution)/shard_map/ppermute | solution.py:57
  14.6 7.6 %collective-permute-start.3 = (f32[128,128]{1,0:T(8,128)S(1)}, f32[128,128]{1,0:T(8,128)S(1)}, u32[]{:S(2)}, u32[]{:S(2)}) collective-permute-start(f32[128,128]{1,0:T(8,128)S(1)} %add_add_fusion.1), channel_id=1, source_target_pairs={{0,4},{1,5},{2,6},{3,7},{4,0},{5,1},{6,2},{7,3},{8,12},{9,13},{10,... | collective-permute-start | bytes 196616 | tf_op jit(solution)/shard_map/ppermute | solution.py:57
  18.6 5.4 %collective-permute-start.11 = (f32[128,128]{1,0:T(8,128)S(1)}, f32[128,128]{1,0:T(8,128)S(1)}, u32[]{:S(2)}, u32[]{:S(2)}) collective-permute-start(f32[128,128]{1,0:T(8,128)S(1)} %add.52.p0), channel_id=1, source_target_pairs={{0,3},{1,2},{2,1},{3,0},{4,7},{5,6},{6,5},{7,4},{8,11},{9,10},{10,... | collective-permute-start | bytes 196616 | tf_op jit(solution)/shard_map/ppermute | solution.py:53
  19.7 6.1 %collective-permute-start.12 = (f32[128,128]{1,0:T(8,128)S(1)}, f32[128,128]{1,0:T(8,128)S(1)}, u32[]{:S(2)}, u32[]{:S(2)}) collective-permute-start(f32[128,128]{1,0:T(8,128)S(1)} %add.52.p0), channel_id=1, source_target_pairs={{0,1},{1,0},{2,3},{3,2},{4,5},{5,4},{6,7},{7,6},{8,9},{9,8},{10,11... | collective-permute-start | bytes 196616 | tf_op jit(solution)/shard_map/ppermute | solution.py:53
  20.1 5.7 %collective-permute-start.13 = (f32[128,128]{1,0:T(8,128)S(1)}, f32[128,128]{1,0:T(8,128)S(1)}, u32[]{:S(2)}, u32[]{:S(2)}) collective-permute-start(f32[128,128]{1,0:T(8,128)S(1)} %add.52.p0), channel_id=1, source_target_pairs={{0,2},{1,3},{2,0},{3,1},{4,6},{5,7},{6,4},{7,5},{8,10},{9,11},{10,... | collective-permute-start | bytes 196616 | tf_op jit(solution)/shard_map/ppermute | solution.py:53
  22.2 5.3 %collective-permute-start.4 = (f32[128,128]{1,0:T(8,128)S(1)}, f32[128,128]{1,0:T(8,128)S(1)}, u32[]{:S(2)}, u32[]{:S(2)}) collective-permute-start(f32[128,128]{1,0:T(8,128)S(1)} %add.48.p0), channel_id=1, source_target_pairs={{0,3},{1,2},{2,1},{3,0},{4,7},{5,6},{6,5},{7,4},{8,11},{9,10},{10,... | collective-permute-start | bytes 196616 | tf_op jit(solution)/shard_map/ppermute | solution.py:53
  23.2 4.9 %collective-permute-start.5 = (f32[128,128]{1,0:T(8,128)S(1)}, f32[128,128]{1,0:T(8,128)S(1)}, u32[]{:S(2)}, u32[]{:S(2)}) collective-permute-start(f32[128,128]{1,0:T(8,128)S(1)} %add.48.p0), channel_id=1, source_target_pairs={{0,1},{1,0},{2,3},{3,2},{4,5},{5,4},{6,7},{7,6},{8,9},{9,8},{10,11... | collective-permute-start | bytes 196616 | tf_op jit(solution)/shard_map/ppermute | solution.py:53
  24.0 4.3 %collective-permute-start.6 = (f32[128,128]{1,0:T(8,128)S(1)}, f32[128,128]{1,0:T(8,128)S(1)}, u32[]{:S(2)}, u32[]{:S(2)}) collective-permute-start(f32[128,128]{1,0:T(8,128)S(1)} %add.48.p0), channel_id=1, source_target_pairs={{0,2},{1,3},{2,0},{3,1},{4,6},{5,7},{6,4},{7,5},{8,10},{9,11},{10,... | collective-permute-start | bytes 196616 | tf_op jit(solution)/shard_map/ppermute | solution.py:53
  26.1 3.7 %collective-permute-start.18 = (f32[128,128]{1,0:T(8,128)S(1)}, f32[128,128]{1,0:T(8,128)S(1)}, u32[]{:S(2)}, u32[]{:S(2)}) collective-permute-start(f32[128,128]{1,0:T(8,128)S(1)} %get-tuple-element.44), channel_id=1, source_target_pairs={{0,8},{8,0},{16,24},{24,16},{1,9},{9,1},{17,25},{25,17},{2,10},{10... | collective-permute-start | bytes 196616 | tf_op jit(solution)/shard_map/ppermute | solution.py:61
  28.8 2.2 %collective-permute-start.14 = (f32[128,256]{1,0:T(8,128)S(1)}, f32[128,256]{1,0:T(8,128)S(1)}, u32[]{:S(2)}, u32[]{:S(2)}) collective-permute-start(f32[128,256]{1,0:T(8,128)S(1)} %get-tuple-element.39), channel_id=1, source_target_pairs={{0,8},{8,0},{16,24},{24,16},{1,9},{9,1},{17,25},{25,17},{2,10},{10... | collective-permute-start | bytes 393224 | tf_op jit(solution)/shard_map/ppermute | solution.py:61
  29.3 1.7 %collective-permute-start.15 = (f32[112,256]{1,0:T(8,128)S(1)}, f32[112,256]{1,0:T(8,128)S(1)}, u32[]{:S(2)}, u32[]{:S(2)}) collective-permute-start(f32[112,256]{1,0:T(8,128)S(1)} %shard_map.71), channel_id=1, source_target_pairs={{0,8},{8,0},{16,24},{24,16},{1,9},{9,1},{17,25},{25,17},{2,10},{10... | collective-permute-start | bytes 344072 | tf_op jit(solution)/shard_map/ppermute | solution.py:61
  29.9 4.2 %collective-permute-start.19 = (f32[128,128]{1,0:T(8,128)S(1)}, f32[128,128]{1,0:T(8,128)S(1)}, u32[]{:S(2)}, u32[]{:S(2)}) collective-permute-start(f32[128,128]{1,0:T(8,128)S(1)} %add.55.gram), channel_id=1, source_target_pairs={{0,24},{1,25},{2,26},{3,27},{4,28},{5,29},{6,30},{7,31},{8,16},{9,... | collective-permute-start | bytes 196616 | tf_op jit(solution)/shard_map/ppermute | solution.py:69
  31.1 6.0 %collective-permute-start.17 = (f32[128,256]{1,0:T(8,128)S(1)}, f32[128,256]{1,0:T(8,128)S(1)}, u32[]{:S(2)}, u32[]{:S(2)}) collective-permute-start(f32[128,256]{1,0:T(8,128)S(1)} %add.53.rest), channel_id=1, source_target_pairs={{0,24},{1,25},{2,26},{3,27},{4,28},{5,29},{6,30},{7,31},{8,16},{9,... | collective-permute-start | bytes 393224 | tf_op jit(solution)/shard_map/ppermute | solution.py:69
  32.4 8.2 %collective-permute-start.16 = (f32[112,256]{1,0:T(8,128)S(1)}, f32[112,256]{1,0:T(8,128)S(1)}, u32[]{:S(2)}, u32[]{:S(2)}) collective-permute-start(f32[112,256]{1,0:T(8,128)S(1)} %add.54.cross), channel_id=1, source_target_pairs={{0,24},{1,25},{2,26},{3,27},{4,28},{5,29},{6,30},{7,31},{8,16},{9,... | collective-permute-start | bytes 344072 | tf_op jit(solution)/shard_map/ppermute | solution.py:69
  41.0 4.1 %collective-permute-start.20 = (f32[1,256]{1,0:T(1,128)S(1)}, f32[1,256]{1,0:T(1,128)S(1)}, u32[]{:S(2)}, u32[]{:S(2)}) collective-permute-start(f32[1,256]{1,0:T(1,128)S(1)} %get-tuple-element.46), channel_id=1, source_target_pairs={{0,11},{1,10},{2,9},{3,8},{4,15},{5,14},{6,13},{7,12},{8,3},{9,2},... | collective-permute-start | bytes 3080 | tf_op jit(solution)/shard_map/ppermute | solution.py:69
  43.3 3.0 %collective-permute-start.21 = (f32[1,256]{1,0:T(1,128)S(1)}, f32[1,256]{1,0:T(1,128)S(1)}, u32[]{:S(2)}, u32[]{:S(2)}) collective-permute-start(f32[1,256]{1,0:T(1,128)S(1)} %get-tuple-element.46), channel_id=1, source_target_pairs={{0,9},{1,8},{2,11},{3,10},{4,13},{5,12},{6,15},{7,14},{8,1},{9,0},... | collective-permute-start | bytes 3080 | tf_op jit(solution)/shard_map/ppermute | solution.py:69
  44.0 3.0 %collective-permute-start.22 = (f32[1,256]{1,0:T(1,128)S(1)}, f32[1,256]{1,0:T(1,128)S(1)}, u32[]{:S(2)}, u32[]{:S(2)}) collective-permute-start(f32[1,256]{1,0:T(1,128)S(1)} %get-tuple-element.46), channel_id=1, source_target_pairs={{0,10},{1,11},{2,8},{3,9},{4,14},{5,15},{6,12},{7,13},{8,2},{9,3},... | collective-permute-start | bytes 3080 | tf_op jit(solution)/shard_map/ppermute | solution.py:69
  47.0 3.9 %collective-permute-start.23 = (f32[1,256]{1,0:T(1,128)S(1)}, f32[1,256]{1,0:T(1,128)S(1)}, u32[]{:S(2)}, u32[]{:S(2)}) collective-permute-start(f32[1,256]{1,0:T(1,128)S(1)} %add_add_fusion.2), channel_id=1, source_target_pairs={{0,12},{1,13},{2,14},{3,15},{4,8},{5,9},{6,10},{7,11},{8,4},{9,5},... | collective-permute-start | bytes 3080 | tf_op jit(solution)/shard_map/ppermute | solution.py:69
  (1 other events, 1.9 us)

commit v8 on v7

--- a/solution.py
+++ b/solution.py
@@ -286,7 +286,8 @@
     second, third = lax.optimization_barrier((second + came[0], third + came[1]))
     for bit in range(1, bits_of(fsdp) - 1):
         first, second, third = [x + flip_across(x, 1 << bit, 0, fsdp, tensor) for x in (first, second, third)]
-    came = [flip_across(x, fsdp // 2, 0, fsdp, tensor) for x in (first, second, third)]
+    came = [flip_across(x, fsdp // 2, 0, fsdp, tensor) for x in (first, second)]
+    came.append(flip_fsdp(third, bits_of(fsdp) - 1, fsdp))
     (inverse1,) = call(first_kernel, [((half, half), f32)], [first, came[0]], micros=4)
     (inverse,) = call(second_kernel, [((rank, rank), f32)], [second, came[1], inverse1], [(half, half)], micros=4)
     right, squares = call(right_kernel, [((cols, rank), f32), ((1, rank), f32)], [third, came[2], inverse])

time: 52.2 us -> 52.1 us (level)
    ppermute x3 -> x4, starting transfers between devices: 0.7 us -> 1.6 us  [flip_fsdp(): return lax.ppermute(x, 'fsdp', [(f, f ^ 1 << bit) for f in range(fsdp)])]
    ppermute x7 -> x6, starting transfers between devices: 8.46 us -> 7.64 us  [flip_across(): return lax.ppermute(x, ('fsdp', 'tensor'), pairs)]
    ppermute x7 -> x6, waiting for transfers between devices: 3.88 us -> 3.79 us  [flip_across(): return lax.ppermute(x, ('fsdp', 'tensor'), pairs)]
where the time goes in v8:
time: 52.1 us; the launch traced here: 51.9 us
  starting transfers between devices  30.4 us (58%)
  Pallas kernels  12.8 us (25%)
  waiting for transfers between devices  7.76 us (15%)
  between operations  0.79 us (2%)
    ppermute x12, starting transfers between devices, to_partner(): lax.ppermute(x, 'tensor', [(t, t ^ partner(j)) for t in range(tensor)])  15.5 us
    pallas_call x9, Pallas kernels, call(): pl.pallas_call(body, out_shape=shapes, in_specs=[pl.BlockSpec(memory_spac...  10.3 us
    ppermute x6, starting transfers between devices, flip_across(): return lax.ppermute(x, ('fsdp', 'tensor'), pairs)  7.64 us
    ppermute x2, starting transfers between devices, flip_tensor(): return lax.ppermute(x, 'tensor', [(t, t ^ 1 << bit) for t in range(tensor)])  5.61 us
    ppermute x6, waiting for transfers between devices, flip_across(): return lax.ppermute(x, ('fsdp', 'tensor'), pairs)  3.79 us
    ppermute x12, waiting for transfers between devices, to_partner(): lax.ppermute(x, 'tensor', [(t, t ^ partner(j)) for t in range(tensor)])  2.9 us
    ppermute x4, starting transfers between devices, flip_fsdp(): return lax.ppermute(x, 'fsdp', [(f, f ^ 1 << bit) for f in range(fsdp)])  1.6 us
    pallas_call x1, Pallas kernels, per_device(): pl.pallas_call(power_kernel, out_shape=[jax.ShapeDtypeStruct(*x) for x in...  1.58 us
  transfers between devices with their start and end apart: 24, of which 11 were waited for; matrix products, arithmetic and copies ran while one was open for 0% of the time, Pallas kernels for 19%

profile of v8, /device:TPU:0, one launch (start us, length us, event | category | flops | bytes accessed | tf_op | source)
XLA Modules:
  0.0 51.9 jit_solution(3505476276137067334)
XLA Ops:
  0.6 1.6 %shard_map.67 = (f32[112,512]{1,0:T(8,128)S(1)}, f32[128,128]{1,0:T(8,128)S(1)}, f32[128,128]{1,0:T(8,128)S(1)}, f32[128,128]{1,0:T(8,128)S(1)}, f32[128,128]{1,...) custom-call(f32[112,512]{1,0:T(8,128)} %mom_in.1, ...), custom_call_target="tpu_custom_call" | custom-call | tf_op jit(solution)/shard_map/pallas_call | solution.py:258
  2.2 4.0 %collective-permute-start.7 = (f32[128,128]{1,0:T(8,128)S(1)}, f32[128,128]{1,0:T(8,128)S(1)}, u32[]{:S(2)}, u32[]{:S(2)}) collective-permute-start(f32[128,128]{1,0:T(8,128)S(1)} %get-tuple-element.33), channel_id=1, source_target_pairs={{0,3},{1,2},{2,1},{3,0},{4,7},{5,6},{6,5},{7,4},{8,11},{9,10},{10,... | collective-permute-start | bytes 196616 | tf_op jit(solution)/shard_map/ppermute | solution.py:53
  6.9 2.8 %collective-permute-start = (f32[128,128]{1,0:T(8,128)S(1)}, f32[128,128]{1,0:T(8,128)S(1)}, u32[]{:S(2)}, u32[]{:S(2)}) collective-permute-start(f32[128,128]{1,0:T(8,128)S(1)} %get-tuple-element.29), channel_id=1, source_target_pairs={{0,3},{1,2},{2,1},{3,0},{4,7},{5,6},{6,5},{7,4},{8,11},{9,10},{10,... | collective-permute-start | bytes 196616 | tf_op jit(solution)/shard_map/ppermute | solution.py:53
  11.4 2.6 %collective-permute-start.10 = (f32[128,128]{1,0:T(8,128)S(1)}, f32[128,128]{1,0:T(8,128)S(1)}, u32[]{:S(2)}, u32[]{:S(2)}) collective-permute-start(f32[128,128]{1,0:T(8,128)S(1)} %add_add_fusion), channel_id=1, source_target_pairs={{0,4},{1,5},{2,6},{3,7},{4,0},{5,1},{6,2},{7,3},{8,12},{9,13},{10,... | collective-permute-start | bytes 196616 | tf_op jit(solution)/shard_map/ppermute | solution.py:57
  14.6 3.0 %collective-permute-start.3 = (f32[128,128]{1,0:T(8,128)S(1)}, f32[128,128]{1,0:T(8,128)S(1)}, u32[]{:S(2)}, u32[]{:S(2)}) collective-permute-start(f32[128,128]{1,0:T(8,128)S(1)} %add_add_fusion.1), channel_id=1, source_target_pairs={{0,4},{1,5},{2,6},{3,7},{4,0},{5,1},{6,2},{7,3},{8,12},{9,13},{10,... | collective-permute-start | bytes 196616 | tf_op jit(solution)/shard_map/ppermute | solution.py:57
  17.5 1.0 %collective-permute-done.10 = f32[128,128]{1,0:T(8,128)S(1)} collective-permute-done((f32[128,128]{1,0:T(8,128)S(1)}, f32[128,128]{1,0:T(8,128)S(1)}, u32[]{:S(2)}, u32[]{:S(2)}) %collective-permute-start.10) | collective-permute-done | bytes 65568 | tf_op jit(solution)/shard_map/ppermute | solution.py:57
  18.6 1.1 %collective-permute-start.11 = (f32[128,128]{1,0:T(8,128)S(1)}, f32[128,128]{1,0:T(8,128)S(1)}, u32[]{:S(2)}, u32[]{:S(2)}) collective-permute-start(f32[128,128]{1,0:T(8,128)S(1)} %add.52.p0), channel_id=1, source_target_pairs={{0,3},{1,2},{2,1},{3,0},{4,7},{5,6},{6,5},{7,4},{8,11},{9,10},{10,... | collective-permute-start | bytes 196616 | tf_op jit(solution)/shard_map/ppermute | solution.py:53
  20.1 2.1 %collective-permute-start.13 = (f32[128,128]{1,0:T(8,128)S(1)}, f32[128,128]{1,0:T(8,128)S(1)}, u32[]{:S(2)}, u32[]{:S(2)}) collective-permute-start(f32[128,128]{1,0:T(8,128)S(1)} %add.52.p0), channel_id=1, source_target_pairs={{0,2},{1,3},{2,0},{3,1},{4,6},{5,7},{6,4},{7,5},{8,10},{9,11},{10,... | collective-permute-start | bytes 196616 | tf_op jit(solution)/shard_map/ppermute | solution.py:53
  22.2 1.1 %collective-permute-start.4 = (f32[128,128]{1,0:T(8,128)S(1)}, f32[128,128]{1,0:T(8,128)S(1)}, u32[]{:S(2)}, u32[]{:S(2)}) collective-permute-start(f32[128,128]{1,0:T(8,128)S(1)} %add.48.p0), channel_id=1, source_target_pairs={{0,3},{1,2},{2,1},{3,0},{4,7},{5,6},{6,5},{7,4},{8,11},{9,10},{10,... | collective-permute-start | bytes 196616 | tf_op jit(solution)/shard_map/ppermute | solution.py:53
  24.0 1.7 %collective-permute-start.6 = (f32[128,128]{1,0:T(8,128)S(1)}, f32[128,128]{1,0:T(8,128)S(1)}, u32[]{:S(2)}, u32[]{:S(2)}) collective-permute-start(f32[128,128]{1,0:T(8,128)S(1)} %add.48.p0), channel_id=1, source_target_pairs={{0,2},{1,3},{2,0},{3,1},{4,6},{5,7},{6,4},{7,5},{8,10},{9,11},{10,... | collective-permute-start | bytes 196616 | tf_op jit(solution)/shard_map/ppermute | solution.py:53
  29.9 1.1 %collective-permute-start.19 = (f32[128,128]{1,0:T(8,128)S(1)}, f32[128,128]{1,0:T(8,128)S(1)}, u32[]{:S(2)}, u32[]{:S(2)}) collective-permute-start(f32[128,128]{1,0:T(8,128)S(1)} %add.55.gram), channel_id=1, source_target_pairs={{0,24},{1,25},{2,26},{3,27},{4,28},{5,29},{6,30},{7,31},{8,16},{9,... | collective-permute-start | bytes 196616 | tf_op jit(solution)/shard_map/ppermute | solution.py:69
  31.1 1.3 %collective-permute-start.17 = (f32[128,256]{1,0:T(8,128)S(1)}, f32[128,256]{1,0:T(8,128)S(1)}, u32[]{:S(2)}, u32[]{:S(2)}) collective-permute-start(f32[128,256]{1,0:T(8,128)S(1)} %add.53.rest), channel_id=1, source_target_pairs={{0,24},{1,25},{2,26},{3,27},{4,28},{5,29},{6,30},{7,31},{8,16},{9,... | collective-permute-start | bytes 393224 | tf_op jit(solution)/shard_map/ppermute | solution.py:69
  32.4 0.9 %collective-permute-start.16 = (f32[112,256]{1,0:T(8,128)S(1)}, f32[112,256]{1,0:T(8,128)S(1)}, u32[]{:S(2)}, u32[]{:S(2)}) collective-permute-start(f32[112,256]{1,0:T(8,128)S(1)} %add.54.cross), channel_id=1, source_target_pairs={{0,16},{8,24},{16,0},{24,8},{1,17},{9,25},{17,1},{25,9},{2,18},{10... | collective-permute-start | bytes 344072 | tf_op jit(solution)/shard_map/ppermute | solution.py:61
  33.3 0.9 %collective-permute-done.19.came = f32[128,128]{1,0:T(8,128)S(1)} collective-permute-done((f32[128,128]{1,0:T(8,128)S(1)}, f32[128,128]{1,0:T(8,128)S(1)}, u32[]{:S(2)}, u32[]{:S(2)}) %collective-permute-start.19) | collective-permute-done | bytes 65568 | tf_op jit(solution)/shard_map/ppermute | solution.py:69
  34.1 2.9 %shard_map.72.inverse1 = f32[128,128]{1,0:T(8,128)S(1)} custom-call(f32[128,128]{1,0:T(8,128)S(1)} %add.55.gram, f32[128,128]{1,0:T(8,128)S(1)} %collective-permute-done.19.came), custom_call_target="tpu_custom_call" | custom-call | flops 4000000000 | tf_op jit(solution)/shard_map/pallas_call | solution.py:74
  37.1 3.5 %shard_map.73.inverse = f32[256,256]{1,0:T(8,128)S(1)} custom-call(f32[128,256]{1,0:T(8,128)S(1)} %add.53.rest, f32[128,256]{1,0:T(8,128)S(1)} %collective-permute-done.17.came, f32[128,128]{1,0:T(8,128)S(1)} %shard_map.72.inverse1), custom_call_target="tpu_custom_call" | custom-call | flops 4000000000 | tf_op jit(solution)/shard_map/pallas_call | solution.py:74
  41.0 2.1 %collective-permute-start.20 = (f32[1,256]{1,0:T(1,128)S(1)}, f32[1,256]{1,0:T(1,128)S(1)}, u32[]{:S(2)}, u32[]{:S(2)}) collective-permute-start(f32[1,256]{1,0:T(1,128)S(1)} %get-tuple-element.46), channel_id=1, source_target_pairs={{0,11},{1,10},{2,9},{3,8},{4,15},{5,14},{6,13},{7,12},{8,3},{9,2},... | collective-permute-start | bytes 3080 | tf_op jit(solution)/shard_map/ppermute | solution.py:69
  43.1 0.9 %collective-permute-start.21 = (f32[1,256]{1,0:T(1,128)S(1)}, f32[1,256]{1,0:T(1,128)S(1)}, u32[]{:S(2)}, u32[]{:S(2)}) collective-permute-start(f32[1,256]{1,0:T(1,128)S(1)} %get-tuple-element.46), channel_id=1, source_target_pairs={{0,9},{1,8},{2,11},{3,10},{4,13},{5,12},{6,15},{7,14},{8,1},{9,0},... | collective-permute-start | bytes 3080 | tf_op jit(solution)/shard_map/ppermute | solution.py:69
  45.0 1.1 %collective-permute-done.21 = f32[1,256]{1,0:T(1,128)S(1)} collective-permute-done((f32[1,256]{1,0:T(1,128)S(1)}, f32[1,256]{1,0:T(1,128)S(1)}, u32[]{:S(2)}, u32[]{:S(2)}) %collective-permute-start.21) | collective-permute-done | bytes 1056 | tf_op jit(solution)/shard_map/ppermute | solution.py:69
  46.1 0.9 %collective-permute-done.22 = f32[1,256]{1,0:T(1,128)S(1)} collective-permute-done((f32[1,256]{1,0:T(1,128)S(1)}, f32[1,256]{1,0:T(1,128)S(1)}, u32[]{:S(2)}, u32[]{:S(2)}) %collective-permute-start.22) | collective-permute-done | bytes 1056 | tf_op jit(solution)/shard_map/ppermute | solution.py:69
  47.0 1.8 %collective-permute-start.23 = (f32[1,256]{1,0:T(1,128)S(1)}, f32[1,256]{1,0:T(1,128)S(1)}, u32[]{:S(2)}, u32[]{:S(2)}) collective-permute-start(f32[1,256]{1,0:T(1,128)S(1)} %add_add_fusion.2), channel_id=1, source_target_pairs={{0,12},{1,13},{2,14},{3,15},{4,8},{5,9},{6,10},{7,11},{8,4},{9,5},... | collective-permute-start | bytes 3080 | tf_op jit(solution)/shard_map/ppermute | solution.py:69
  48.8 1.1 %shard_map.77 = f32[112,512]{1,0:T(8,128)} custom-call(f32[112,512]{1,0:T(8,128)S(1)} %get-tuple-element.37.buf, f32[112,256]{1,0:T(8,128)S(1)} %get-tuple-element.45.right, f32[256,512]{1,0:T(8,128)S(1)} %get-tuple-element.47.ortho), custom_call_target="tpu_custom_call" | custom-call | flops 2000000000 | tf_op jit(solution)/shard_map/pallas_call | solution.py:74
  49.9 1.0 %collective-permute-done.23 = f32[1,256]{1,0:T(1,128)S(1)} collective-permute-done((f32[1,256]{1,0:T(1,128)S(1)}, f32[1,256]{1,0:T(1,128)S(1)}, u32[]{:S(2)}, u32[]{:S(2)}) %collective-permute-start.23) | collective-permute-done | bytes 1056 | tf_op jit(solution)/shard_map/ppermute | solution.py:69
  50.9 1.0 %shard_map.76 = (bf16[112,512]{1,0:T(8,128)(2,1)}, f32[112,256]{1,0:T(8,128)}) custom-call(bf16[112,512]{1,0:T(8,128)(2,1)S(1)} %copy-done, f32[112,256]{1,0:T(8,128)S(1)} %get-tuple-element.45.right, f32[1,256]{1,0:T(1,128)S(1)} %add.59.squares, bf16[256,512]{1,0:T(8,128)(2,1)S(1)} %get-tuple-element.49.high, bf16[256,512]{1,0:T(8,128)(2,1)S(1)} %get-tuple-element.50.mid), custom_call_target="tpu_custom_call" | custom-call | tf_op jit(solution)/shard_map/pallas_call | solution.py:305
  (46 shorter events, 9.6 us)
Async XLA Ops:
  2.2 8.0 %collective-permute-start.7 = (f32[128,128]{1,0:T(8,128)S(1)}, f32[128,128]{1,0:T(8,128)S(1)}, u32[]{:S(2)}, u32[]{:S(2)}) collective-permute-start(f32[128,128]{1,0:T(8,128)S(1)} %get-tuple-element.33), channel_id=1, source_target_pairs={{0,3},{1,2},{2,1},{3,0},{4,7},{5,6},{6,5},{7,4},{8,11},{9,10},{10,... | collective-permute-start | bytes 196616 | tf_op jit(solution)/shard_map/ppermute | solution.py:53
  6.3 5.1 %collective-permute-start.8 = (f32[128,128]{1,0:T(8,128)S(1)}, f32[128,128]{1,0:T(8,128)S(1)}, u32[]{:S(2)}, u32[]{:S(2)}) collective-permute-start(f32[128,128]{1,0:T(8,128)S(1)} %get-tuple-element.34), channel_id=1, source_target_pairs={{0,1},{1,0},{2,3},{3,2},{4,5},{5,4},{6,7},{7,6},{8,9},{9,8},{10,11... | collective-permute-start | bytes 196616 | tf_op jit(solution)/shard_map/ppermute | solution.py:53
  6.8 4.6 %collective-permute-start.9 = (f32[128,128]{1,0:T(8,128)S(1)}, f32[128,128]{1,0:T(8,128)S(1)}, u32[]{:S(2)}, u32[]{:S(2)}) collective-permute-start(f32[128,128]{1,0:T(8,128)S(1)} %get-tuple-element.35), channel_id=1, source_target_pairs={{0,2},{1,3},{2,0},{3,1},{4,6},{5,7},{6,4},{7,5},{8,10},{9,11},{10,... | collective-permute-start | bytes 196616 | tf_op jit(solution)/shard_map/ppermute | solution.py:53
  6.9 7.1 %collective-permute-start = (f32[128,128]{1,0:T(8,128)S(1)}, f32[128,128]{1,0:T(8,128)S(1)}, u32[]{:S(2)}, u32[]{:S(2)}) collective-permute-start(f32[128,128]{1,0:T(8,128)S(1)} %get-tuple-element.29), channel_id=1, source_target_pairs={{0,3},{1,2},{2,1},{3,0},{4,7},{5,6},{6,5},{7,4},{8,11},{9,10},{10,... | collective-permute-start | bytes 196616 | tf_op jit(solution)/shard_map/ppermute | solution.py:53
  9.8 4.3 %collective-permute-start.1 = (f32[128,128]{1,0:T(8,128)S(1)}, f32[128,128]{1,0:T(8,128)S(1)}, u32[]{:S(2)}, u32[]{:S(2)}) collective-permute-start(f32[128,128]{1,0:T(8,128)S(1)} %get-tuple-element.30), channel_id=1, source_target_pairs={{0,1},{1,0},{2,3},{3,2},{4,5},{5,4},{6,7},{7,6},{8,9},{9,8},{10,11... | collective-permute-start | bytes 196616 | tf_op jit(solution)/shard_map/ppermute | solution.py:53
  10.3 4.3 %collective-permute-start.2 = (f32[128,128]{1,0:T(8,128)S(1)}, f32[128,128]{1,0:T(8,128)S(1)}, u32[]{:S(2)}, u32[]{:S(2)}) collective-permute-start(f32[128,128]{1,0:T(8,128)S(1)} %get-tuple-element.31), channel_id=1, source_target_pairs={{0,2},{1,3},{2,0},{3,1},{4,6},{5,7},{6,4},{7,5},{8,10},{9,11},{10,... | collective-permute-start | bytes 196616 | tf_op jit(solution)/shard_map/ppermute | solution.py:53
  11.4 7.2 %collective-permute-start.10 = (f32[128,128]{1,0:T(8,128)S(1)}, f32[128,128]{1,0:T(8,128)S(1)}, u32[]{:S(2)}, u32[]{:S(2)}) collective-permute-start(f32[128,128]{1,0:T(8,128)S(1)} %add_add_fusion), channel_id=1, source_target_pairs={{0,4},{1,5},{2,6},{3,7},{4,0},{5,1},{6,2},{7,3},{8,12},{9,13},{10,... | collective-permute-start | bytes 196616 | tf_op jit(solution)/shard_map/ppermute | solution.py:57
  14.6 7.6 %collective-permute-start.3 = (f32[128,128]{1,0:T(8,128)S(1)}, f32[128,128]{1,0:T(8,128)S(1)}, u32[]{:S(2)}, u32[]{:S(2)}) collective-permute-start(f32[128,128]{1,0:T(8,128)S(1)} %add_add_fusion.1), channel_id=1, source_target_pairs={{0,4},{1,5},{2,6},{3,7},{4,0},{5,1},{6,2},{7,3},{8,12},{9,13},{10,... | collective-permute-start | bytes 196616 | tf_op jit(solution)/shard_map/ppermute | solution.py:57
  18.6 5.4 %collective-permute-start.11 = (f32[128,128]{1,0:T(8,128)S(1)}, f32[128,128]{1,0:T(8,128)S(1)}, u32[]{:S(2)}, u32[]{:S(2)}) collective-permute-start(f32[128,128]{1,0:T(8,128)S(1)} %add.52.p0), channel_id=1, source_target_pairs={{0,3},{1,2},{2,1},{3,0},{4,7},{5,6},{6,5},{7,4},{8,11},{9,10},{10,... | collective-permute-start | bytes 196616 | tf_op jit(solution)/shard_map/ppermute | solution.py:53
  19.7 6.1 %collective-permute-start.12 = (f32[128,128]{1,0:T(8,128)S(1)}, f32[128,128]{1,0:T(8,128)S(1)}, u32[]{:S(2)}, u32[]{:S(2)}) collective-permute-start(f32[128,128]{1,0:T(8,128)S(1)} %add.52.p0), channel_id=1, source_target_pairs={{0,1},{1,0},{2,3},{3,2},{4,5},{5,4},{6,7},{7,6},{8,9},{9,8},{10,11... | collective-permute-start | bytes 196616 | tf_op jit(solution)/shard_map/ppermute | solution.py:53
  20.1 5.7 %collective-permute-start.13 = (f32[128,128]{1,0:T(8,128)S(1)}, f32[128,128]{1,0:T(8,128)S(1)}, u32[]{:S(2)}, u32[]{:S(2)}) collective-permute-start(f32[128,128]{1,0:T(8,128)S(1)} %add.52.p0), channel_id=1, source_target_pairs={{0,2},{1,3},{2,0},{3,1},{4,6},{5,7},{6,4},{7,5},{8,10},{9,11},{10,... | collective-permute-start | bytes 196616 | tf_op jit(solution)/shard_map/ppermute | solution.py:53
  22.2 5.3 %collective-permute-start.4 = (f32[128,128]{1,0:T(8,128)S(1)}, f32[128,128]{1,0:T(8,128)S(1)}, u32[]{:S(2)}, u32[]{:S(2)}) collective-permute-start(f32[128,128]{1,0:T(8,128)S(1)} %add.48.p0), channel_id=1, source_target_pairs={{0,3},{1,2},{2,1},{3,0},{4,7},{5,6},{6,5},{7,4},{8,11},{9,10},{10,... | collective-permute-start | bytes 196616 | tf_op jit(solution)/shard_map/ppermute | solution.py:53
  23.2 4.9 %collective-permute-start.5 = (f32[128,128]{1,0:T(8,128)S(1)}, f32[128,128]{1,0:T(8,128)S(1)}, u32[]{:S(2)}, u32[]{:S(2)}) collective-permute-start(f32[128,128]{1,0:T(8,128)S(1)} %add.48.p0), channel_id=1, source_target_pairs={{0,1},{1,0},{2,3},{3,2},{4,5},{5,4},{6,7},{7,6},{8,9},{9,8},{10,11... | collective-permute-start | bytes 196616 | tf_op jit(solution)/shard_map/ppermute | solution.py:53
  24.0 4.3 %collective-permute-start.6 = (f32[128,128]{1,0:T(8,128)S(1)}, f32[128,128]{1,0:T(8,128)S(1)}, u32[]{:S(2)}, u32[]{:S(2)}) collective-permute-start(f32[128,128]{1,0:T(8,128)S(1)} %add.48.p0), channel_id=1, source_target_pairs={{0,2},{1,3},{2,0},{3,1},{4,6},{5,7},{6,4},{7,5},{8,10},{9,11},{10,... | collective-permute-start | bytes 196616 | tf_op jit(solution)/shard_map/ppermute | solution.py:53
  26.1 3.7 %collective-permute-start.18 = (f32[128,128]{1,0:T(8,128)S(1)}, f32[128,128]{1,0:T(8,128)S(1)}, u32[]{:S(2)}, u32[]{:S(2)}) collective-permute-start(f32[128,128]{1,0:T(8,128)S(1)} %get-tuple-element.44), channel_id=1, source_target_pairs={{0,8},{8,0},{16,24},{24,16},{1,9},{9,1},{17,25},{25,17},{2,10},{10... | collective-permute-start | bytes 196616 | tf_op jit(solution)/shard_map/ppermute | solution.py:61
  28.8 2.2 %collective-permute-start.14 = (f32[128,256]{1,0:T(8,128)S(1)}, f32[128,256]{1,0:T(8,128)S(1)}, u32[]{:S(2)}, u32[]{:S(2)}) collective-permute-start(f32[128,256]{1,0:T(8,128)S(1)} %get-tuple-element.39), channel_id=1, source_target_pairs={{0,8},{8,0},{16,24},{24,16},{1,9},{9,1},{17,25},{25,17},{2,10},{10... | collective-permute-start | bytes 393224 | tf_op jit(solution)/shard_map/ppermute | solution.py:61
  29.3 1.7 %collective-permute-start.15 = (f32[112,256]{1,0:T(8,128)S(1)}, f32[112,256]{1,0:T(8,128)S(1)}, u32[]{:S(2)}, u32[]{:S(2)}) collective-permute-start(f32[112,256]{1,0:T(8,128)S(1)} %shard_map.71), channel_id=1, source_target_pairs={{0,8},{8,0},{16,24},{24,16},{1,9},{9,1},{17,25},{25,17},{2,10},{10... | collective-permute-start | bytes 344072 | tf_op jit(solution)/shard_map/ppermute | solution.py:61
  29.9 4.2 %collective-permute-start.19 = (f32[128,128]{1,0:T(8,128)S(1)}, f32[128,128]{1,0:T(8,128)S(1)}, u32[]{:S(2)}, u32[]{:S(2)}) collective-permute-start(f32[128,128]{1,0:T(8,128)S(1)} %add.55.gram), channel_id=1, source_target_pairs={{0,24},{1,25},{2,26},{3,27},{4,28},{5,29},{6,30},{7,31},{8,16},{9,... | collective-permute-start | bytes 196616 | tf_op jit(solution)/shard_map/ppermute | solution.py:69
  31.1 6.0 %collective-permute-start.17 = (f32[128,256]{1,0:T(8,128)S(1)}, f32[128,256]{1,0:T(8,128)S(1)}, u32[]{:S(2)}, u32[]{:S(2)}) collective-permute-start(f32[128,256]{1,0:T(8,128)S(1)} %add.53.rest), channel_id=1, source_target_pairs={{0,24},{1,25},{2,26},{3,27},{4,28},{5,29},{6,30},{7,31},{8,16},{9,... | collective-permute-start | bytes 393224 | tf_op jit(solution)/shard_map/ppermute | solution.py:69
  32.4 8.2 %collective-permute-start.16 = (f32[112,256]{1,0:T(8,128)S(1)}, f32[112,256]{1,0:T(8,128)S(1)}, u32[]{:S(2)}, u32[]{:S(2)}) collective-permute-start(f32[112,256]{1,0:T(8,128)S(1)} %add.54.cross), channel_id=1, source_target_pairs={{0,16},{8,24},{16,0},{24,8},{1,17},{9,25},{17,1},{25,9},{2,18},{10... | collective-permute-start | bytes 344072 | tf_op jit(solution)/shard_map/ppermute | solution.py:61
  41.0 4.0 %collective-permute-start.20 = (f32[1,256]{1,0:T(1,128)S(1)}, f32[1,256]{1,0:T(1,128)S(1)}, u32[]{:S(2)}, u32[]{:S(2)}) collective-permute-start(f32[1,256]{1,0:T(1,128)S(1)} %get-tuple-element.46), channel_id=1, source_target_pairs={{0,11},{1,10},{2,9},{3,8},{4,15},{5,14},{6,13},{7,12},{8,3},{9,2},... | collective-permute-start | bytes 3080 | tf_op jit(solution)/shard_map/ppermute | solution.py:69
  43.1 3.0 %collective-permute-start.21 = (f32[1,256]{1,0:T(1,128)S(1)}, f32[1,256]{1,0:T(1,128)S(1)}, u32[]{:S(2)}, u32[]{:S(2)}) collective-permute-start(f32[1,256]{1,0:T(1,128)S(1)} %get-tuple-element.46), channel_id=1, source_target_pairs={{0,9},{1,8},{2,11},{3,10},{4,13},{5,12},{6,15},{7,14},{8,1},{9,0},... | collective-permute-start | bytes 3080 | tf_op jit(solution)/shard_map/ppermute | solution.py:69
  44.0 3.0 %collective-permute-start.22 = (f32[1,256]{1,0:T(1,128)S(1)}, f32[1,256]{1,0:T(1,128)S(1)}, u32[]{:S(2)}, u32[]{:S(2)}) collective-permute-start(f32[1,256]{1,0:T(1,128)S(1)} %get-tuple-element.46), channel_id=1, source_target_pairs={{0,10},{1,11},{2,8},{3,9},{4,14},{5,15},{6,12},{7,13},{8,2},{9,3},... | collective-permute-start | bytes 3080 | tf_op jit(solution)/shard_map/ppermute | solution.py:69
  47.0 3.9 %collective-permute-start.23 = (f32[1,256]{1,0:T(1,128)S(1)}, f32[1,256]{1,0:T(1,128)S(1)}, u32[]{:S(2)}, u32[]{:S(2)}) collective-permute-start(f32[1,256]{1,0:T(1,128)S(1)} %add_add_fusion.2), channel_id=1, source_target_pairs={{0,12},{1,13},{2,14},{3,15},{4,8},{5,9},{6,10},{7,11},{8,4},{9,5},... | collective-permute-start | bytes 3080 | tf_op jit(solution)/shard_map/ppermute | solution.py:69
  (1 other events, 2.1 us)
